TPU v7x, 128 devices: a whole 4x4x4 slice. The times are simulated.
128 devices in a mesh: pos: 16 (over y, x_hi, core), off: 8 (over z, x_lo).
Axes of the slice: x: 4 (x_hi: 2, x_lo: 2; x = x_hi * 2 + x_lo), y: 4, z: 4, core: 2. Of those that a mesh axis runs over, the one named last changes fastest.
Arguments:
- band_map: bfloat16 [48, 2304, 2048], P(None, 'pos', 'off'), may hold values from -6 to 6
- dilations: int32 [2], replicated, may hold values from 1 to 32, as said below
- row_limit: int32 [2304], replicated, may hold values from 512 to 1023
- weight_one: bfloat16 [9, 48, 48], replicated, may hold values from -0.3125 to 0.3125
- bias_one: float32 [48], replicated, may hold values from -3 to 3
- weight_two: bfloat16 [9, 48, 48], replicated, may hold values from -0.3125 to 0.3125
- bias_two: float32 [48], replicated, may hold values from -3 to 3
Outputs:
- mixed: bfloat16 [48, 2304, 2048], P(None, 'pos', 'off')
Inputs may be any that keep to these rules, and one draw needn't show every extreme that they name: One of the two dilations equals 32.
All inputs are finite; a program needn't handle non-finite values.
Results may differ from a plain program's by a relative error of at most 0.0052.
Values may be sent and summed in bfloat16 or wider, within the bound.
No kernel may reach another device: no remote copies, remote signals or barrier semaphores. Data moves between devices by JAX's collectives and lax.ppermute only.
A program may use at most 384 MiB of HBM per device.

v0:
```python
import jax
import jax.numpy as jnp
from jax import lax
from jax.sharding import PartitionSpec as P

BAND = 1024
DMAX = 32


def with_halo(cells, sides, width):
    for axis, dim in sides:
        count = lax.axis_size(axis)
        ends = count - 1
        head = lax.slice_in_dim(cells, 0, width, axis=dim)
        tail = lax.slice_in_dim(cells, cells.shape[dim] - width, cells.shape[dim], axis=dim)
        cells = jnp.concatenate(
            [
                lax.ppermute(tail, axis, [(i, (i + 1) % count) for i in range(ends)]),
                cells,
                lax.ppermute(head, axis, [((i + 1) % count, i) for i in range(ends)]),
            ],
            axis=dim,
        )
    return cells


def valid_mask(row_ids, col_ids, limits, total_rows):
    offset_cols = col_ids - BAND
    parity_cols = col_ids % 2
    first_bin = row_ids[:, None] + ((parity_cols - offset_cols) // 2)[None, :]
    second_bin = row_ids[:, None] + ((parity_cols + offset_cols) // 2)[None, :]
    inside = (
        (first_bin >= 0) & (first_bin < total_rows) & (second_bin >= 0) & (second_bin < total_rows)
    )
    return inside & (jnp.abs(offset_cols)[None, :] <= limits[:, None])


def dilated_conv(padded, weight, dilation, row_count, col_count, margin):
    channels = padded.shape[0]
    odd_cols = (jnp.arange(col_count) % 2 == 1)[None, None, :]
    accum_sum = jnp.zeros((weight.shape[1], row_count, col_count), jnp.float32)
    tap_index = 0
    for row_sign in (-1, 0, 1):
        for col_sign in (-1, 0, 1):
            row_step = dilation * (row_sign + col_sign)
            col_step = dilation * (col_sign - row_sign)
            col_first = margin + col_step
            low_start = margin + row_step // 2
            high_start = margin + (row_step + 1) // 2
            low_slice = lax.dynamic_slice(
                padded, (jnp.int32(0), low_start, col_first), (channels, row_count, col_count)
            )
            high_slice = lax.dynamic_slice(
                padded, (jnp.int32(0), high_start, col_first), (channels, row_count, col_count)
            )
            picked = jnp.where(odd_cols, high_slice, low_slice)
            accum_sum = accum_sum + jnp.einsum(
                "oc,crk->ork", weight[tap_index], picked, preferred_element_type=jnp.float32
            )
            tap_index += 1
    return accum_sum


def local(band_map, dilations, row_limit, weight_one, bias_one, weight_two, bias_two):
    channels, row_count, col_count = band_map.shape
    margin = 2 * DMAX
    total_rows = lax.axis_size("pos") * row_count
    row_start = lax.axis_index("pos") * row_count
    col_start = lax.axis_index("off") * col_count

    def cells(extra):
        row_ids = row_start - extra + jnp.arange(row_count + 2 * extra, dtype=jnp.int32)
        col_ids = col_start - extra + jnp.arange(col_count + 2 * extra, dtype=jnp.int32)
        limits = jnp.take(row_limit, jnp.clip(row_ids, 0, total_rows - 1))
        return valid_mask(row_ids, col_ids, limits, total_rows)[None]

    own_cells = cells(0)
    masked = jnp.where(own_cells, band_map, jnp.zeros((), jnp.bfloat16))
    padded = with_halo(masked, (("pos", 1), ("off", 2)), margin)
    first = (
        dilated_conv(padded, weight_one, dilations[0], row_count, col_count, margin)
        + bias_one[:, None, None]
    )
    hidden = jnp.where(own_cells, jnp.maximum(first, 0.0), 0.0).astype(jnp.bfloat16)
    padded_hidden = with_halo(hidden, (("pos", 1), ("off", 2)), margin)
    second = (
        dilated_conv(padded_hidden, weight_two, dilations[1], row_count, col_count, margin)
        + bias_two[:, None, None]
    )
    summed = jnp.where(own_cells, second + masked.astype(jnp.float32), 0.0).astype(jnp.bfloat16)
    block_rows = lax.all_to_all(summed, "off", split_axis=1, concat_axis=2, tiled=True)
    zero_col = jnp.zeros(block_rows.shape[:2] + (1,), jnp.bfloat16)
    flipped = jnp.concatenate([zero_col, block_rows[:, :, :0:-1]], axis=2)
    averaged = (0.5 * (block_rows.astype(jnp.float32) + flipped.astype(jnp.float32))).astype(
        jnp.bfloat16
    )
    merged = lax.all_to_all(averaged, "off", split_axis=2, concat_axis=1, tiled=True)
    return jnp.where(own_cells, merged, jnp.zeros((), jnp.bfloat16))


def solution(mesh):
    in_specs = (P(None, "pos", "off"), P(), P(), P(), P(), P(), P())
    out_specs = P(None, "pos", "off")
    return jax.shard_map(local, mesh=mesh, in_specs=in_specs, out_specs=out_specs, check_vma=False)
```

profile of v0, /device:TPU:8, one launch (start us, length us, event | category | flops | bytes accessed | tf_op | source)
XLA Modules:
  0.0 672.2 jit_solution(2942363400045503774)
XLA Ops:
  0.7 1.4 gather_fusion
  2.3 3.2 copy_select_fusion
  5.8 1.9 collective-permute-start
  7.7 6.0 collective-permute-start.1
  13.8 28.7 %collective-permute-done = bf16[48,64,256]{2,0,1:T(8,128)(2,1)S(1)} collective-permute-done((bf16[48,64,256]{2,0,1:T(8,128)(2,1)S(1)}, bf16[48,64,256]{2,0,1:T(8,128)(2,1)S(1)}, u32[]{:S(2)}, u32[]{:S(2)}) %collective-permute-start) | collective-permute-done | bytes 1572896 | tf_op jit(solution)/shard_map/ppermute | solution.py:18
  42.5 2.4 collective-permute-done.1
  44.9 1.2 copy-done.8
  46.9 4.3 fusion.146
  51.2 5.9 copy.15
  57.1 4.4 collective-permute-start.2
  61.5 5.8 copy.16
  67.3 1.3 collective-permute-start.3
  76.3 4.6 fusion.93
  81.0 29.8 %collective-permute-done.2 = bf16[48,272,64]{1,2,0:T(8,128)(2,1)} collective-permute-done((bf16[48,272,64]{1,2,0:T(8,128)(2,1)}, bf16[48,272,64]{1,2,0:T(8,128)(2,1)}, u32[]{:S(2)}, u32[]{:S(2)}) %collective-permute-start.2) | collective-permute-done | bytes 1671200 | tf_op jit(solution)/shard_map/ppermute | solution.py:18
  110.8 6.0 copy.17
  116.8 47.7 %collective-permute-done.3 = bf16[48,272,64]{1,2,0:T(8,128)(2,1)} collective-permute-done((bf16[48,272,64]{1,2,0:T(8,128)(2,1)}, bf16[48,272,64]{1,2,0:T(8,128)(2,1)}, u32[]{:S(2)}, u32[]{:S(2)}) %collective-permute-start.3) | collective-permute-done | bytes 1671200 | tf_op jit(solution)/shard_map/ppermute | solution.py:20
  164.5 5.9 copy.18
  170.4 10.4 %pad_maximum_fusion = bf16[48,272,384]{2,0,1:T(8,128)(2,1)S(1)} fusion(bf16[48,272,64]{2,0,1:T(8,128)(2,1)} %copy.18, bf16[48,64,256]{2,0,1:T(8,128)(2,1)} %copy-done.8, bf16[48,144,256]{2,0,1:T(8,128)(2,1)S(1)} %copy_select_fusion, bf16[48,64,256]{2,0,1:T(8,128)(2,1)} %copy-done.7, bf16[48,272,64]{2,0,1:T(8,128)(2,1)} %copy.17), kind=kLoop, calls=%fused_computation.1 | loop fusion | flops 50135040 | bytes 20054016 | tf_op jit(solution)/shard_map/concatenate | solution.py:16
  180.8 5.8 fusion.44
  186.5 5.2 fusion.50
  191.7 5.3 fusion.40
  197.1 5.2 fusion.34
  202.3 4.2 fusion.38
  206.5 4.6 fusion.48
  211.1 5.3 fusion.54
  216.3 30.0 %fusion.70 = bf16[48,144,256]{2,0,1:T(8,128)(2,1)} fusion(f32[48]{0:T(128)S(1)} %copy-done.15, f32[144,256,48]{1,2,0:T(8,128)} %fusion.34, f32[144,256,48]{1,2,0:T(8,128)} %fusion.38, f32[144,256,48]{1,2,0:T(8,128)} %fusion.40, f32[144,256,48]{1,2,0:T(8,128)} %fusion.93, f32[144,256,48]{1,2,0:T(8,128)} %fusion.44, f32[144,256,48]{1,2,0:T(8,128)} %fusion.48, ...), kind=kOutput, calls=%fused_computation.81 | convolution fusion | flops 192872448 | bytes 67290120 | tf_op jit(solution)/shard_map/oc,crk->ork/dot_general | solution.py:57
  246.4 2.2 fusion.147
  248.6 2.5 collective-permute-start.4
  251.1 5.4 collective-permute-start.5
  256.6 31.9 %collective-permute-done.4 = bf16[48,64,256]{2,0,1:T(8,128)(2,1)S(1)} collective-permute-done((bf16[48,64,256]{2,0,1:T(8,128)(2,1)S(1)}, bf16[48,64,256]{2,0,1:T(8,128)(2,1)S(1)}, u32[]{:S(2)}, u32[]{:S(2)}) %collective-permute-start.4) | collective-permute-done | bytes 1572896 | tf_op jit(solution)/shard_map/ppermute | solution.py:18
  288.4 1.2 copy-done.5
  291.6 4.2 fusion.145
  295.8 5.9 copy.19
  301.7 2.7 collective-permute-start.6
  304.4 5.8 copy.20
  310.2 1.3 collective-permute-start.7
  317.4 5.9 fusion.83
  323.3 31.1 %collective-permute-done.6 = bf16[48,272,64]{1,2,0:T(8,128)(2,1)} collective-permute-done((bf16[48,272,64]{1,2,0:T(8,128)(2,1)}, bf16[48,272,64]{1,2,0:T(8,128)(2,1)}, u32[]{:S(2)}, u32[]{:S(2)}) %collective-permute-start.6) | collective-permute-done | bytes 1671200 | tf_op jit(solution)/shard_map/ppermute | solution.py:18
  354.4 6.0 copy.21
  360.4 48.7 %collective-permute-done.7 = bf16[48,272,64]{1,2,0:T(8,128)(2,1)} collective-permute-done((bf16[48,272,64]{1,2,0:T(8,128)(2,1)}, bf16[48,272,64]{1,2,0:T(8,128)(2,1)}, u32[]{:S(2)}, u32[]{:S(2)}) %collective-permute-start.7) | collective-permute-done | bytes 1671200 | tf_op jit(solution)/shard_map/ppermute | solution.py:20
  409.1 6.0 copy.22
  415.2 10.8 %pad_maximum_fusion.1 = bf16[48,272,384]{2,0,1:T(8,128)(2,1)S(1)} fusion(bf16[48,272,64]{2,0,1:T(8,128)(2,1)} %copy.22, bf16[48,64,256]{2,0,1:T(8,128)(2,1)} %copy-done.6, bf16[48,144,256]{2,0,1:T(8,128)(2,1)} %fusion.70, bf16[48,64,256]{2,0,1:T(8,128)(2,1)} %copy-done.5, bf16[48,272,64]{2,0,1:T(8,128)(2,1)} %copy.21), kind=kLoop, calls=%fused_computation.2 | loop fusion | flops 50135040 | bytes 20054016 | tf_op jit(solution)/shard_map/concatenate | solution.py:16
  426.0 5.7 fusion.16
  431.7 5.2 fusion.22
  436.9 5.3 fusion.12
  442.2 5.2 fusion.6
  447.4 4.2 fusion.10
  451.6 4.3 fusion.20
  455.9 5.2 fusion.26
  461.2 24.8 %fusion.1 = bf16[48,144,256]{2,0,1:T(8,128)(2,1)} fusion(f32[144,256,48]{1,2,0:T(8,128)} %fusion.6, f32[144,256,48]{1,2,0:T(8,128)} %fusion.10, f32[144,256,48]{1,2,0:T(8,128)} %fusion.12, bf16[48,144,256]{2,0,1:T(8,128)(2,1)S(1)} %copy_select_fusion, f32[144,256,48]{1,2,0:T(8,128)} %fusion.83, f32[144,256,48]{1,2,0:T(8,128)} %fusion.16, ...), kind=kOutput, calls=%fused_computation.5 | convolution fusion | flops 194641920 | bytes 70828488 | tf_op jit(solution)/shard_map/oc,crk->ork/dot_general | solution.py:57
  486.0 45.9 %all_to_all.36 = bf16[48,144,256]{2,0,1:T(8,128)(2,1)S(1)} all-to-all(bf16[48,144,256]{2,0,1:T(8,128)(2,1)} %fusion.1), channel_id=1, replica_groups=mesh['pos'=16,'off'=8] {'off'}, dimensions={1} | all-to-all | bytes 7077888 | tf_op jit(solution)/shard_map/all_to_all | solution.py:91
  531.9 3.8 copy.32
  535.6 5.1 all_to_all.29
  540.8 3.6 slice.130
  544.4 10.8 %reverse = bf16[48,18,2048]{2,0,1:T(8,128)(2,1)} reverse(bf16[48,18,2048]{2,0,1:T(8,128)(2,1)} %bitcast.106), dimensions={2} | reverse | bytes 7077888
  555.2 3.7 slice.203
  558.9 4.7 multiply_convert_fusion
  563.7 13.4 %copy.24 = bf16[48,18,2048]{0,1,2:T(8,128)(2,1)} copy(bf16[48,18,2048]{2,0,1:T(8,128)(2,1)} %multiply_convert_fusion) | data formatting | bytes 7077888 | tf_op jit(solution)/shard_map/convert_element_type | solution.py:94
  577.0 14.9 %reshape.214 = bf16[8,2,110592]{2,1,0:T(2,128)(2,1)S(1)} reshape(bf16[2048,18,48]{2,1,0:T(8,128)(2,1)} %bitcast.102) | data formatting | bytes 7077888
  591.9 45.0 %all_to_all.37 = bf16[8,2,110592]{2,1,0:T(2,128)(2,1)} all-to-all(bf16[8,2,110592]{2,1,0:T(2,128)(2,1)S(1)} %reshape.214), channel_id=1, replica_groups=mesh['pos'=16,'off'=8] {'off'}, dimensions={0} | all-to-all | bytes 7077888 | tf_op jit(solution)/shard_map/all_to_all | solution.py:97
  636.9 17.0 %reshape.215 = bf16[2048,18,48]{2,1,0:T(8,128)(2,1)} reshape(bf16[8,2,110592]{2,1,0:T(2,128)(2,1)} %all_to_all.37) | data formatting | bytes 7077888
  653.9 12.5 %copy.26 = bf16[48,8,18,256]{3,0,2,1:T(8,128)(2,1)} copy(bf16[48,8,18,256]{0,2,3,1:T(8,128)(2,1)} %bitcast.103) | data formatting | bytes 7077888 | tf_op jit(solution)/shard_map/all_to_all | solution.py:97
  666.4 2.3 bitcast_select_fusion
  668.7 3.0 copy.27
  (44 shorter events, 4.5 us)
Async XLA Ops:
  0.0 0.7 copy-start
  2.3 3.4 copy-start.9
  5.8 36.7 %collective-permute-start = (bf16[48,64,256]{2,0,1:T(8,128)(2,1)S(1)}, bf16[48,64,256]{2,0,1:T(8,128)(2,1)S(1)}, u32[]{:S(2)}, u32[]{:S(2)}) collective-permute-start(bf16[48,64,256]{2,0,1:T(8,128)(2,1)S(1)} %get-tuple-element.11), channel_id=1, source_target_pairs={{0,8},{8,16},{16,24},{24,32},{32,40},{40,48},{48,56},{56,64},{64,7... | collective-permute-start | bytes 4718600 | tf_op jit(solution)/shard_map/ppermute | solution.py:18
  7.7 37.2 %collective-permute-start.1 = (bf16[48,64,256]{2,0,1:T(8,128)(2,1)S(1)}, bf16[48,64,256]{2,0,1:T(8,128)(2,1)S(1)}, u32[]{:S(2)}, u32[]{:S(2)}) collective-permute-start(bf16[48,64,256]{2,0,1:T(8,128)(2,1)S(1)} %get-tuple-element.12), channel_id=1, source_target_pairs={{8,0},{16,8},{24,16},{32,24},{40,32},{48,40},{56,48},{64,56},{72,6... | collective-permute-start | bytes 4718600 | tf_op jit(solution)/shard_map/ppermute | solution.py:20
  42.5 2.4 copy-start.7
  44.9 1.2 copy-start.8
  51.2 17.4 %copy-start.14 = (s32[2]{0:T(128)S(1)}, s32[2]{0:T(128)}, u32[]{:S(2)}) copy-start(s32[2]{0:T(128)} %param.8) | copy-start | bytes 28
  57.1 53.7 %collective-permute-start.2 = (bf16[48,272,64]{1,2,0:T(8,128)(2,1)}, bf16[48,272,64]{1,2,0:T(8,128)(2,1)}, u32[]{:S(2)}, u32[]{:S(2)}) collective-permute-start(bf16[48,272,64]{1,2,0:T(8,128)(2,1)} %copy.15), channel_id=1, source_target_pairs={{0,1},{1,2},{2,3},{3,4},{4,5},{5,6},{6,7},{8,9},{9,10},{10,11},{11... | collective-permute-start | bytes 5013512 | tf_op jit(solution)/shard_map/ppermute | solution.py:18
  67.3 97.2 %collective-permute-start.3 = (bf16[48,272,64]{1,2,0:T(8,128)(2,1)}, bf16[48,272,64]{1,2,0:T(8,128)(2,1)}, u32[]{:S(2)}, u32[]{:S(2)}) collective-permute-start(bf16[48,272,64]{1,2,0:T(8,128)(2,1)} %copy.16), channel_id=1, source_target_pairs={{1,0},{2,1},{3,2},{4,3},{5,4},{6,5},{7,6},{9,8},{10,9},{11,10},{12... | collective-permute-start | bytes 5013512 | tf_op jit(solution)/shard_map/ppermute | solution.py:20
  170.4 10.4 %copy-start.12 = (bf16[9,48,48]{2,1,0:T(8,128)(2,1)S(1)}, bf16[9,48,48]{2,1,0:T(8,128)(2,1)}, u32[]{:S(2)}) copy-start(bf16[9,48,48]{2,1,0:T(8,128)(2,1)} %param.10) | copy-start | bytes 124420
  180.8 30.3 %copy-start.2 = (bf16[48,272,384]{2,0,1:T(8,128)(2,1)}, bf16[48,272,384]{2,0,1:T(8,128)(2,1)S(1)}, u32[]{:S(2)}) copy-start(bf16[48,272,384]{2,0,1:T(8,128)(2,1)S(1)} %pad_maximum_fusion) | copy-start | bytes 30081028
  211.0 5.3 copy-start.10
  211.0 5.3 copy-start.15
  246.3 44.5 %copy-start.4 = (bf16[48,144,256]{2,0,1:T(8,128)(2,1)S(1)}, bf16[48,144,256]{2,0,1:T(8,128)(2,1)}, u32[]{:S(2)}) copy-start(bf16[48,144,256]{2,0,1:T(8,128)(2,1)} %fusion.70) | copy-start | bytes 10616836
  248.6 39.9 %collective-permute-start.4 = (bf16[48,64,256]{2,0,1:T(8,128)(2,1)S(1)}, bf16[48,64,256]{2,0,1:T(8,128)(2,1)S(1)}, u32[]{:S(2)}, u32[]{:S(2)}) collective-permute-start(bf16[48,64,256]{2,0,1:T(8,128)(2,1)S(1)} %get-tuple-element.9), channel_id=1, source_target_pairs={{0,8},{8,16},{16,24},{24,32},{32,40},{40,48},{48,56},{56,64},{64,7... | collective-permute-start | bytes 4718600 | tf_op jit(solution)/shard_map/ppermute | solution.py:18
  251.1 37.3 %collective-permute-start.5 = (bf16[48,64,256]{2,0,1:T(8,128)(2,1)S(1)}, bf16[48,64,256]{2,0,1:T(8,128)(2,1)S(1)}, u32[]{:S(2)}, u32[]{:S(2)}) collective-permute-start(bf16[48,64,256]{2,0,1:T(8,128)(2,1)S(1)} %get-tuple-element.10), channel_id=1, source_target_pairs={{8,0},{16,8},{24,16},{32,24},{40,32},{48,40},{56,48},{64,56},{72,6... | collective-permute-start | bytes 4718600 | tf_op jit(solution)/shard_map/ppermute | solution.py:20
  288.4 1.2 copy-start.5
  289.6 1.2 copy-start.6
  301.7 52.8 %collective-permute-start.6 = (bf16[48,272,64]{1,2,0:T(8,128)(2,1)}, bf16[48,272,64]{1,2,0:T(8,128)(2,1)}, u32[]{:S(2)}, u32[]{:S(2)}) collective-permute-start(bf16[48,272,64]{1,2,0:T(8,128)(2,1)} %copy.19), channel_id=1, source_target_pairs={{0,1},{1,2},{2,3},{3,4},{4,5},{5,6},{6,7},{8,9},{9,10},{10,11},{11... | collective-permute-start | bytes 5013512 | tf_op jit(solution)/shard_map/ppermute | solution.py:18
  310.2 98.9 %collective-permute-start.7 = (bf16[48,272,64]{1,2,0:T(8,128)(2,1)}, bf16[48,272,64]{1,2,0:T(8,128)(2,1)}, u32[]{:S(2)}, u32[]{:S(2)}) collective-permute-start(bf16[48,272,64]{1,2,0:T(8,128)(2,1)} %copy.20), channel_id=1, source_target_pairs={{1,0},{2,1},{3,2},{4,3},{5,4},{6,5},{7,6},{9,8},{10,9},{11,10},{12... | collective-permute-start | bytes 5013512 | tf_op jit(solution)/shard_map/ppermute | solution.py:20
  415.2 10.8 %copy-start.13 = (bf16[9,48,48]{2,1,0:T(8,128)(2,1)S(1)}, bf16[9,48,48]{2,1,0:T(8,128)(2,1)}, u32[]{:S(2)}) copy-start(bf16[9,48,48]{2,1,0:T(8,128)(2,1)} %param.12) | copy-start | bytes 124420
  426.0 30.0 %copy-start.3 = (bf16[48,272,384]{2,0,1:T(8,128)(2,1)}, bf16[48,272,384]{2,0,1:T(8,128)(2,1)S(1)}, u32[]{:S(2)}) copy-start(bf16[48,272,384]{2,0,1:T(8,128)(2,1)S(1)} %pad_maximum_fusion.1) | copy-start | bytes 30081028
  455.9 5.3 copy-start.16
  653.9 12.6 %copy-start.11 = (pred[144,256]{1,0:T(8,128)(4,1)S(1)}, pred[144,256]{1,0:T(8,128)(4,1)}, u32[]{:S(2)}) copy-start(pred[144,256]{1,0:T(8,128)(4,1)} %copy-done.9) | copy-start | bytes 110596
  653.9 17.9 %copy-start.1 = (s32[2304]{0:T(1024)S(1)}, s32[2304]{0:T(1024)}, u32[]{:S(2)}) copy-start(s32[2304]{0:T(1024)} %param.9) | copy-start | bytes 27652
where the time goes:
time: 681 us; the launch traced here: 672 us
  waiting for transfers between devices  220 us (32%)
  local copies, waits for them, and re-layouts  152 us (22%)
  matrix products  136 us (20%)
  blocking collectives  90.9 us (13%)
  other arithmetic  33.3 us (5%)
  starting transfers between devices  25.7 us (4%)
  between operations  13.7 us (2%)
    dot_general x18, matrix products, dilated_conv(): jnp.einsum('oc,crk->ork', weight[tap_index], picked, preferred_element_ty...  136 us
    ppermute x4, waiting for transfers between devices, with_halo(): lax.ppermute(tail, axis, [(i, (i + 1) % count) for i in range(ends)])  121 us
    ppermute x4, waiting for transfers between devices, with_halo(): lax.ppermute(head, axis, [((i + 1) % count, i) for i in range(ends)])  98.9 us
    unnamed x38, local copies, waits for them, and re-layouts  50.6 us
    all_to_all x1, blocking collectives, local(): lax.all_to_all(summed, 'off', split_axis=1, concat_axis=2, tiled=True)  45.9 us
    all_to_all x1, blocking collectives, local(): lax.all_to_all(averaged, 'off', split_axis=2, concat_axis=1, tiled=True)  45 us
    concatenate x4, other arithmetic, with_halo(): jnp.concatenate([lax.ppermute(tail, axis, [(i, (i + 1) % count) for i in...  22.8 us
    slice x6, local copies, waits for them, and re-layouts, with_halo(): lax.slice_in_dim(cells, cells.shape[dim] - width, cells.shape[dim], axis=...  22.6 us
  transfers between devices with their start and end apart: 8, of which 7 were waited for; matrix products, arithmetic and copies ran while one was open for 5% of the time, Pallas kernels for 0%

commit v1 on v0

v1 whole, which is shorter than its diff:
```python
import functools

import jax
import jax.numpy as jnp
from jax import lax
from jax.experimental import pallas as pl
from jax.experimental.pallas import tpu as pltpu
from jax.sharding import PartitionSpec as P

BAND = 1024
DMAX = 32
C = 48
ROWS = 144
COLS = 256
LANES = 128
HALO = DMAX
PAIR = ROWS // 2
CORNER = DMAX // 2
GROUP = CORNER // 4
CHUNK = 48
PARTS = ROWS // CHUNK
PREP = 8
AXES = ("pos", "off")

SMEM = pl.BlockSpec(memory_space=pltpu.SMEM)
VMEM = pl.BlockSpec(memory_space=pltpu.VMEM)
ANY = pl.BlockSpec(memory_space=pl.ANY)
PARAMS = pltpu.CompilerParams(vmem_limit_bytes=56 * 2**20)

PLANE_OF_FOLD = (0, 3, 2, 1)
FOLD_OF_PLANE = (0, 3, 2, 1)


def home(strip, block):
    return strip * 8 + block


def place(strip, block):
    fold = min(block, 7 - block)
    core = 1 if block >= 4 else 0
    return (2 * (strip // 2) + core) * 8 + 2 * PLANE_OF_FOLD[fold] + strip % 2


def grid_cells():
    return [(strip, block) for strip in range(16) for block in range(8)]


def moves(strip_step, block_step):
    return [
        (place(s, b), place(s + strip_step, b + block_step))
        for s, b in grid_cells()
        if 0 <= s + strip_step < 16 and 0 <= b + block_step < 8
    ]


def worked_cell():
    pos, off = lax.axis_index("pos"), lax.axis_index("off")
    strip = 2 * (pos // 2) + off % 2
    fold = jnp.array(FOLD_OF_PLANE, jnp.int32)[off // 2]
    return strip, jnp.where(pos % 2 == 1, 7 - fold, fold)


def thresholds(row_limit, strip):
    rows = strip * ROWS + jnp.arange(ROWS, dtype=jnp.int32)
    limit = lax.dynamic_slice(row_limit, (strip * ROWS,), (ROWS,))
    last = row_limit.shape[0] - 1
    return jnp.minimum(limit, jnp.minimum(2 * rows + 1, 2 * last - 2 * rows))


def offsets(col, shape):
    return jnp.abs(lax.broadcasted_iota(jnp.int32, shape, len(shape) - 1) + col)


def spans(first, count, cuts):
    out = []
    at = first
    while at < first + count:
        end = min([c for c in cuts if c > at] + [first + count])
        out.append((at, end - at))
        at = end
    return out


def enter_kernel(part, t_ref, col_ref, x_ref, out_ref):
    x = jnp.swapaxes(x_ref[...], 0, 1)
    for i in range(CHUNK):
        seen = offsets(col_ref[0], (C, COLS)) <= t_ref[part * CHUNK + i]
        out_ref[i] = jnp.where(seen, x[i], jnp.zeros((), jnp.bfloat16))


def enter(part, limits, col, band_map):
    return pl.pallas_call(
        functools.partial(enter_kernel, part),
        grid=(1,),
        in_specs=[SMEM, SMEM, pl.BlockSpec((C, CHUNK, COLS), lambda i: (0, part, 0))],
        out_specs=pl.BlockSpec((CHUNK, C, COLS), lambda i: (0, 0, 0)),
        out_shape=jax.ShapeDtypeStruct((CHUNK, C, COLS), jnp.bfloat16),
        compiler_params=PARAMS,
        name="enter",
    )(limits, col, band_map)


def pack_edges(load, top, bottom, left, right, corners):
    lane = lax.broadcasted_iota(jnp.int32, (C, LANES), 1)
    for i in range(PAIR):
        a, b = load(i), load(i + PAIR)
        left[i] = jnp.where(lane < 64, a[:, :LANES], pltpu.roll(b[:, :LANES], 64, axis=1))
        right[i] = jnp.where(lane < 64, pltpu.roll(a[:, LANES:], 64, axis=1), b[:, LANES:])
    for i in range(HALO):
        top[i] = load(i)
        bottom[i] = load(ROWS - HALO + i)
    for ref, first, side in zip(corners, (0, 0, ROWS - CORNER, ROWS - CORNER), (0, 1, 0, 1)):
        for i in range(GROUP):
            packed = None
            for g in range(4):
                cells = load(first + g * GROUP + i)
                cells = cells[:, LANES:] if side else cells[:, :LANES]
                turn = (32 * g + (32 if side else 0)) % LANES
                cells = pltpu.roll(cells, turn, axis=1) if turn else cells
                packed = cells if packed is None else jnp.where(lane < 32 * g, packed, cells)
            ref[i] = packed


EDGES = (
    [jax.ShapeDtypeStruct((HALO, C, COLS), jnp.bfloat16)] * 2
    + [jax.ShapeDtypeStruct((PAIR, C, LANES), jnp.bfloat16)] * 2
    + [jax.ShapeDtypeStruct((GROUP, C, LANES), jnp.bfloat16)] * 4
)


def pack_kernel(*refs):
    parts, edges = refs[:PARTS], refs[PARTS:]

    def load(row):
        return parts[row // CHUNK][row % CHUNK]

    pack_edges(load, *edges[:4], edges[4:])


def pack(parts):
    return pl.pallas_call(
        pack_kernel,
        in_specs=[VMEM] * PARTS,
        out_specs=[VMEM] * 8,
        out_shape=EDGES,
        compiler_params=PARAMS,
        name="pack",
    )(*parts)


def exchange(edges):
    top, bottom, left, right, up_left, up_right, down_left, down_right = edges
    send = lambda cells, step: lax.ppermute(cells, AXES, moves(*step))
    from_right = send(left, (0, -1))
    from_left = send(right, (0, 1))
    from_below = send(top, (-1, 0))
    from_above = send(bottom, (1, 0))
    corners = (
        send(down_right, (1, 1)),
        send(down_left, (1, -1)),
        send(up_right, (-1, 1)),
        send(up_left, (-1, -1)),
    )
    return from_above, from_below, from_left, from_right, corners


def conv_kernel(first, count, final, *refs):
    d_ref, col_ref, t_ref = refs[:3]
    parts = refs[3 : 3 + PARTS]
    above, below, from_left, from_right = refs[3 + PARTS : 7 + PARTS]
    corners = refs[7 + PARTS : 11 + PARTS]
    w_ref, b_ref = refs[11 + PARTS : 13 + PARTS]
    rest = refs[13 + PARTS :]
    if final:
        own_ref, out_ref, edge_ref, mid, lft, rgt, plus_ref, minus_ref, sems = rest
    else:
        out_ref, *edges = rest[:9]
        mid, lft, rgt, plus_ref, minus_ref, sems = rest[9:]

    base = first - HALO
    copies = []
    for at, size in spans(base, count + 2 * HALO, [0] + [CHUNK * i for i in range(1, PARTS + 1)]):
        if at < 0:
            src = above.at[pl.ds(at + HALO, size)]
        elif at >= ROWS:
            src = below.at[pl.ds(at - ROWS, size)]
        else:
            src = parts[at // CHUNK].at[pl.ds(at % CHUNK, size)]
        copies.append(pltpu.make_async_copy(src, mid.at[pl.ds(at - base, size)], sems.at[len(copies)]))
    for copy in copies:
        copy.start()

    for at, size in spans(first - CORNER, count + 2 * CORNER, [0, PAIR, ROWS]):
        for j in range(size):
            row = at + j
            if row < 0 or row >= ROWS:
                i = row + CORNER if row < 0 else row - ROWS
                pair = corners[:2] if row < 0 else corners[2:]
                g, i = i // GROUP, i % GROUP
                a, b = pair[0][i], pair[1][i]
                lft[row - base] = pltpu.roll(a, 96 - 32 * g, axis=1) if g != 3 else a
                rgt[row - base] = pltpu.roll(b, 128 - 32 * g, axis=1) if g else b
            elif row < PAIR:
                lft[row - base] = pltpu.roll(from_left[row], 64, axis=1)
                rgt[row - base] = from_right[row]
            else:
                lft[row - base] = from_left[row - PAIR]
                rgt[row - base] = pltpu.roll(from_right[row - PAIR], 64, axis=1)
    for copy in copies:
        copy.wait()

    d = d_ref[0]
    lo = d // 2
    hi = (d + 1) // 2
    odd = d - 2 * lo
    lane = lax.broadcasted_iota(jnp.int32, (C, LANES), 1)
    even_lane = (lane & 1) == 0

    def tiles(r):
        return [lft[r], mid[r, :, :LANES], mid[r, :, LANES:], rgt[r]]

    def onward(t, step):
        keep = lane < LANES - step
        a, b, c = [pltpu.roll(x, LANES - step, axis=1) for x in t[1:]]
        return jnp.concatenate([jnp.where(keep, a, b), jnp.where(keep, b, c)], axis=1)

    def backward(t, step):
        keep = lane < step
        a, b, c = [pltpu.roll(x, step, axis=1) for x in t[:3]]
        return jnp.concatenate([jnp.where(keep, a, b), jnp.where(keep, b, c)], axis=1)

    start = HALO - hi

    def prepare(i, _):
        for j in range(PREP):
            r = start + i * PREP + j
            x, y = tiles(r), tiles(r + odd)
            cells = [jnp.where(even_lane, b, a) for a, b in zip(x, y)]
            plus_ref[r] = onward(cells, d)
            minus_ref[r] = backward(cells, d)
        return 0

    lax.fori_loop(0, (count + d + PREP - 1) // PREP, prepare, 0)

    weight = w_ref[...]
    bias = b_ref[...]
    col = col_ref[0]
    if final:
        edge_ref[...] = jnp.zeros_like(edge_ref)

    def row(m, _):
        r = m + HALO
        x = tiles(r)
        taps = [
            mid[r - d],
            plus_ref[r - hi],
            onward(x, 2 * d),
            minus_ref[r - hi],
            mid[r],
            plus_ref[r + lo],
            backward(x, 2 * d),
            minus_ref[r + lo],
            mid[r + d],
        ]
        acc = lax.dot_general(
            weight,
            jnp.concatenate(taps, axis=0),
            (((1,), (0,)), ((), ())),
            preferred_element_type=jnp.float32,
        )
        acc = acc + bias
        if final:
            acc = acc + own_ref[m].astype(jnp.float32)
        else:
            acc = jnp.maximum(acc, 0.0)
        acc = jnp.where(offsets(col, (C, COLS)) <= t_ref[first + m], acc, 0.0).astype(jnp.bfloat16)
        out_ref[m] = acc
        if final:
            edge_ref[...] = jnp.where(lane == m, pltpu.roll(acc[:, :LANES], m, axis=1), edge_ref[...])
        return 0

    lax.fori_loop(0, count, row, 0, unroll=8)
    if not final:
        pack_edges(lambda i: out_ref[i], *edges[:4], edges[4:])


def conv(first, count, final, d, col, limits, parts, halos, weight, bias):
    above, below, from_left, from_right, corners = halos
    wide = count + 2 * HALO
    in_specs = [SMEM] * 3 + [ANY] * (PARTS + 2) + [VMEM] * 8
    args = [d, col, limits, *parts, above, below, from_left, from_right, *corners, weight, bias]
    if final:
        in_specs.append(VMEM)
        args.append(final[first // CHUNK])
    out_shape = [jax.ShapeDtypeStruct((count, C, COLS), jnp.bfloat16)]
    if final:
        out_shape.append(jax.ShapeDtypeStruct((C, LANES), jnp.bfloat16))
    else:
        out_shape += EDGES
    return pl.pallas_call(
        functools.partial(conv_kernel, first, count, bool(final)),
        in_specs=in_specs,
        out_specs=[VMEM] * len(out_shape),
        out_shape=out_shape,
        scratch_shapes=[
            pltpu.VMEM((wide, C, COLS), jnp.bfloat16),
            pltpu.VMEM((wide, C, LANES), jnp.bfloat16),
            pltpu.VMEM((wide, C, LANES), jnp.bfloat16),
            pltpu.VMEM((wide, C, COLS), jnp.bfloat16),
            pltpu.VMEM((wide, C, COLS), jnp.bfloat16),
            pltpu.SemaphoreType.DMA((PARTS + 2,)),
        ],
        compiler_params=PARAMS,
        cost_estimate=pl.CostEstimate(
            flops=2 * 9 * C * C * COLS * count * 10, bytes_accessed=wide * C * COLS * 8, transcendentals=0
        ),
        name="second" if final else "first",
    )(*args)


def mix_kernel(part, t_ref, col_ref, own_ref, twin_ref, edge_ref, out_ref, rows_ref):
    lane = lax.broadcasted_iota(jnp.int32, (C, LANES), 1)
    a = lax.broadcasted_iota(jnp.int32, (COLS, COLS), 0)
    b = lax.broadcasted_iota(jnp.int32, (COLS, COLS), 1)
    turn = ((a + b == COLS) | (a + b == 0)).astype(jnp.bfloat16)
    edge = edge_ref[...]
    for m in range(CHUNK):
        twin = twin_ref[m]
        head = pltpu.roll(edge, LANES - m, axis=1) if m else edge
        twin = jnp.concatenate([jnp.where(lane == 0, head, twin[:, :LANES]), twin[:, LANES:]], axis=1)
        mirror = jnp.dot(twin, turn, preferred_element_type=jnp.float32)
        both = 0.5 * (own_ref[m].astype(jnp.float32) + mirror)
        seen = offsets(col_ref[0], (C, COLS)) <= t_ref[part * CHUNK + m]
        rows_ref[m] = jnp.where(seen, both, 0.0).astype(jnp.bfloat16)
    out_ref[...] = jnp.swapaxes(rows_ref[...], 0, 1)


def mix(part, limits, col, own, twin, edge):
    return pl.pallas_call(
        functools.partial(mix_kernel, part),
        in_specs=[SMEM] * 2 + [VMEM] * 3,
        out_specs=VMEM,
        out_shape=jax.ShapeDtypeStruct((C, CHUNK, COLS), jnp.bfloat16),
        scratch_shapes=[pltpu.VMEM((CHUNK, C, COLS), jnp.bfloat16)],
        compiler_params=PARAMS,
        name="mix",
    )(limits, col, own, twin, edge)


def flat(weight):
    return jnp.transpose(weight, (1, 0, 2)).reshape(C, 9 * C)


def local(band_map, dilations, row_limit, weight_one, bias_one, weight_two, bias_two):
    stored_strip, stored_block = lax.axis_index("pos"), lax.axis_index("off")
    strip, block = worked_cell()
    stored_limits = thresholds(row_limit, stored_strip)
    stored_col = (stored_block * COLS - BAND).reshape(1)
    limits = thresholds(row_limit, strip)
    col = (block * COLS - BAND).reshape(1)
    there = [(home(s, b), place(s, b)) for s, b in grid_cells()]
    back = [(b, a) for a, b in there]
    mirrored = [(place(s, b), place(s, 7 - b)) for s, b in grid_cells()]
    beyond = [(place(s, b), place(s, 8 - b)) for s, b in grid_cells() if b >= 1]

    parts = [
        lax.ppermute(enter(i, stored_limits, stored_col, band_map), AXES, there) for i in range(PARTS)
    ]
    halos = exchange(pack(parts))
    hidden, *edges = conv(
        0, ROWS, None, dilations[:1], col, limits, parts, halos, flat(weight_one), bias_one[:, None]
    )
    halos = exchange(edges)
    hidden = [lax.slice_in_dim(hidden, i * CHUNK, (i + 1) * CHUNK) for i in range(PARTS)]
    weight = flat(weight_two)
    out = []
    for i in range(PARTS):
        summed, edge = conv(
            i * CHUNK, CHUNK, parts, dilations[1:], col, limits, hidden, halos, weight, bias_two[:, None]
        )
        twin = lax.ppermute(summed, AXES, mirrored)
        edge = lax.ppermute(edge, AXES, beyond)
        mixed = mix(i, limits, col, summed, twin, edge)
        out.append(lax.ppermute(mixed, AXES, back))
    return jnp.concatenate(out, axis=1)


def solution(mesh):
    in_specs = (P(None, "pos", "off"), P(), P(), P(), P(), P(), P())
    out_specs = P(None, "pos", "off")
    return jax.shard_map(local, mesh=mesh, in_specs=in_specs, out_specs=out_specs, check_vma=False)
```

time: 681 us -> 319 us (0.47)
  the two profiles are of different devices: /device:TPU:8 before, /device:TPU:19 now
where the time goes in v1:
time: 319 us; the launch traced here: 317 us
  waiting for transfers between devices  128 us (40%)
  starting transfers between devices  89 us (28%)
  Pallas kernels  78.3 us (25%)
  local copies, waits for them, and re-layouts  16.4 us (5%)
  other arithmetic  3.33 us (1%)
    ppermute x3, waiting for transfers between devices, local(): out.append(lax.ppermute(mixed, AXES, back))  61.4 us
    ppermute x16, starting transfers between devices, exchange(): send = lambda cells, step: lax.ppermute(cells, AXES, moves(*step))  57 us
    pallas_call x4, Pallas kernels, conv(): pl.pallas_call(functools.partial(conv_kernel, first, count, bool(final)),...  54 us
    ppermute x16, waiting for transfers between devices, exchange(): send = lambda cells, step: lax.ppermute(cells, AXES, moves(*step))  37.9 us
    ppermute x3, waiting for transfers between devices, local(): lax.ppermute(enter(i, stored_limits, stored_col, band_map), AXES, there)  29.1 us
    pallas_call x3, Pallas kernels, mix(): pl.pallas_call(functools.partial(mix_kernel, part), in_specs=[SMEM] * 2 +...  12 us
    ppermute x3, starting transfers between devices, local(): lax.ppermute(enter(i, stored_limits, stored_col, band_map), AXES, there)  10.5 us
    ppermute x3, starting transfers between devices, local(): out.append(lax.ppermute(mixed, AXES, back))  9.4 us
  transfers between devices with their start and end apart: 28, of which 12 were waited for; matrix products, arithmetic and copies ran while one was open for 3% of the time, Pallas kernels for 12%

profile of v1, /device:TPU:19, one launch (start us, length us, event | category | flops | bytes accessed | tf_op | source)
XLA Modules:
  0.0 317.4 jit_solution(217749646323337693)
XLA Ops:
  0.0 1.4 minimum_minimum_fusion
  1.4 2.6 enter.3
  4.1 6.2 %collective-permute-start = (bf16[48,48,256]{2,1,0:T(8,128)(2,1)}, bf16[48,48,256]{2,1,0:T(8,128)(2,1)S(1)}, u32[]{:S(2)}, u32[]{:S(2)}) collective-permute-start(bf16[48,48,256]{2,1,0:T(8,128)(2,1)} %enter.3), channel_id=1, source_target_pairs={{0,0},{1,6},{2,4},{3,2},{4,10},{5,12},{6,14},{7,8},{8,1},{9,7},{10... | collective-permute-start | bytes 3538952 | tf_op jit(solution)/shard_map/ppermute | solution.py:367
  10.3 2.6 enter.4
  12.9 1.9 collective-permute-start.1
  14.8 2.6 enter.5
  17.5 2.4 collective-permute-start.2
  19.9 3.8 %collective-permute-done.refs_0_.refs_3_.refs_16_ = bf16[48,48,256]{2,1,0:T(8,128)(2,1)S(1)} collective-permute-done((bf16[48,48,256]{2,1,0:T(8,128)(2,1)}, bf16[48,48,256]{2,1,0:T(8,128)(2,1)S(1)}, u32[]{:S(2)}, u32[]{:S(2)}) %collective-permute-start) | collective-permute-done | bytes 1179680 | tf_op jit(solution)/shard_map/ppermute | solution.py:367
  23.7 12.6 %collective-permute-done.1.refs_1_.refs_4_.refs_16_ = bf16[48,48,256]{2,1,0:T(8,128)(2,1)S(1)} collective-permute-done((bf16[48,48,256]{2,1,0:T(8,128)(2,1)}, bf16[48,48,256]{2,1,0:T(8,128)(2,1)S(1)}, u32[]{:S(2)}, u32[]{:S(2)}) %collective-permute-start.1) | collective-permute-done | bytes 1179680 | tf_op jit(solution)/shard_map/ppermute | solution.py:367
  36.4 12.6 %collective-permute-done.2.refs_2_.refs_5_.refs_16_ = bf16[48,48,256]{2,1,0:T(8,128)(2,1)S(1)} collective-permute-done((bf16[48,48,256]{2,1,0:T(8,128)(2,1)}, bf16[48,48,256]{2,1,0:T(8,128)(2,1)S(1)}, u32[]{:S(2)}, u32[]{:S(2)}) %collective-permute-start.2) | collective-permute-done | bytes 1179680 | tf_op jit(solution)/shard_map/ppermute | solution.py:367
  49.0 1.0 copy-done.2
  50.0 4.3 %pack.1 = (bf16[32,48,256]{2,1,0:T(8,128)(2,1)}, bf16[32,48,256]{2,1,0:T(8,128)(2,1)}, bf16[72,48,128]{2,1,0:T(8,128)(2,1)}, bf16[72,48,128]{2,1,0:T(8,128)(2,1)...) custom-call(bf16[48,48,256]{2,1,0:T(8,128)(2,1)} %copy-done, ...), custom_call_target="tpu_custom_call" | custom-call | tf_op jit(solution)/shard_map/pack/pallas_call | solution.py:141
  54.4 1.3 collective-permute-start.5
  55.7 5.3 %collective-permute-start.6 = (bf16[72,48,128]{2,1,0:T(8,128)(2,1)}, bf16[72,48,128]{2,1,0:T(8,128)(2,1)S(1)}, u32[]{:S(2)}, u32[]{:S(2)}) collective-permute-start(bf16[72,48,128]{2,1,0:T(8,128)(2,1)} %get-tuple-element.31), channel_id=1, source_target_pairs={{6,0},{4,6},{2,4},{10,2},{12,10},{14,12},{8,14},{7,1},{5,7},{3,5},... | collective-permute-start | bytes 2654216 | tf_op jit(solution)/shard_map/ppermute | solution.py:153
  60.9 4.4 %collective-permute-start.3 = (bf16[32,48,256]{2,1,0:T(8,128)(2,1)}, bf16[32,48,256]{2,1,0:T(8,128)(2,1)S(1)}, u32[]{:S(2)}, u32[]{:S(2)}) collective-permute-start(bf16[32,48,256]{2,1,0:T(8,128)(2,1)} %get-tuple-element.28), channel_id=1, source_target_pairs={{0,1},{6,7},{4,5},{2,3},{10,11},{12,13},{14,15},{8,9},{1,16},{7,22... | collective-permute-start | bytes 2359304 | tf_op jit(solution)/shard_map/ppermute | solution.py:153
  65.3 1.9 collective-permute-start.4
  67.2 1.3 collective-permute-start.7
  68.5 10.4 %collective-permute-done.7.refs_10_ = bf16[4,48,128]{2,1,0:T(8,128)(2,1)S(1)} collective-permute-done((bf16[4,48,128]{2,1,0:T(8,128)(2,1)}, bf16[4,48,128]{2,1,0:T(8,128)(2,1)S(1)}, u32[]{:S(2)}, u32[]{:S(2)}) %collective-permute-start.7) | collective-permute-done | bytes 49184 | tf_op jit(solution)/shard_map/ppermute | solution.py:153
  78.9 4.5 %collective-permute-start.8 = (bf16[4,48,128]{2,1,0:T(8,128)(2,1)}, bf16[4,48,128]{2,1,0:T(8,128)(2,1)S(1)}, u32[]{:S(2)}, u32[]{:S(2)}) collective-permute-start(bf16[4,48,128]{2,1,0:T(8,128)(2,1)} %get-tuple-element.33), channel_id=1, source_target_pairs={{6,1},{4,7},{2,5},{10,3},{12,11},{14,13},{8,15},{7,16},{5,22},{3,2... | collective-permute-start | bytes 147464 | tf_op jit(solution)/shard_map/ppermute | solution.py:153
  83.4 1.5 collective-permute-done.8.refs_11_
  84.9 1.3 collective-permute-start.9
  86.1 6.1 %collective-permute-done.9.refs_12_ = bf16[4,48,128]{2,1,0:T(8,128)(2,1)S(1)} collective-permute-done((bf16[4,48,128]{2,1,0:T(8,128)(2,1)}, bf16[4,48,128]{2,1,0:T(8,128)(2,1)S(1)}, u32[]{:S(2)}, u32[]{:S(2)}) %collective-permute-start.9) | collective-permute-done | bytes 49184 | tf_op jit(solution)/shard_map/ppermute | solution.py:153
  92.2 7.6 %collective-permute-start.10 = (bf16[4,48,128]{2,1,0:T(8,128)(2,1)}, bf16[4,48,128]{2,1,0:T(8,128)(2,1)S(1)}, u32[]{:S(2)}, u32[]{:S(2)}) collective-permute-start(bf16[4,48,128]{2,1,0:T(8,128)(2,1)} %get-tuple-element.35), channel_id=1, source_target_pairs={{7,0},{5,6},{3,4},{11,2},{13,10},{15,12},{9,14},{22,1},{20,7},{18,... | collective-permute-start | bytes 147464 | tf_op jit(solution)/shard_map/ppermute | solution.py:153
  99.8 0.6 fusion.1
  100.5 0.6 dynamic_slice.10
  102.6 0.7 copy.16.refs_14_
  103.3 0.7 copy.17.refs_15_
  105.5 21.8 %first.1 = (bf16[144,48,256]{2,1,0:T(8,128)(2,1)}, bf16[32,48,256]{2,1,0:T(8,128)(2,1)}, bf16[32,48,256]{2,1,0:T(8,128)(2,1)}, bf16[72,48,128]{2,1,0:T(8,128)(2,...) custom-call(s32[1]{0:T(128)} %get-tuple-element.56.refs_0_, ...), custom_call_target="tpu_custom_call" | custom-call | flops 15288238080 | bytes 20447232 | tf_op jit(solution)/shard_map/first/pallas_call | solution.py:300
  127.4 1.3 collective-permute-start.13
  128.7 5.3 %collective-permute-start.14 = (bf16[72,48,128]{2,1,0:T(8,128)(2,1)}, bf16[72,48,128]{2,1,0:T(8,128)(2,1)S(1)}, u32[]{:S(2)}, u32[]{:S(2)}) collective-permute-start(bf16[72,48,128]{2,1,0:T(8,128)(2,1)} %get-tuple-element.40), channel_id=1, source_target_pairs={{6,0},{4,6},{2,4},{10,2},{12,10},{14,12},{8,14},{7,1},{5,7},{3,5},... | collective-permute-start | bytes 2654216 | tf_op jit(solution)/shard_map/ppermute | solution.py:153
  134.0 1.9 collective-permute-start.11
  135.9 3.4 %collective-permute-start.12 = (bf16[32,48,256]{2,1,0:T(8,128)(2,1)}, bf16[32,48,256]{2,1,0:T(8,128)(2,1)}, u32[]{:S(2)}, u32[]{:S(2)}) collective-permute-start(bf16[32,48,256]{2,1,0:T(8,128)(2,1)} %get-tuple-element.38), channel_id=1, source_target_pairs={{1,0},{7,6},{5,4},{3,2},{11,10},{13,12},{15,14},{9,8},{16,1},{22,7... | collective-permute-start | bytes 2359304 | tf_op jit(solution)/shard_map/ppermute | solution.py:153
  139.3 1.3 collective-permute-start.15
  140.6 8.3 %collective-permute-done.15.refs_10_ = bf16[4,48,128]{2,1,0:T(8,128)(2,1)S(1)} collective-permute-done((bf16[4,48,128]{2,1,0:T(8,128)(2,1)}, bf16[4,48,128]{2,1,0:T(8,128)(2,1)S(1)}, u32[]{:S(2)}, u32[]{:S(2)}) %collective-permute-start.15) | collective-permute-done | bytes 49184 | tf_op jit(solution)/shard_map/ppermute | solution.py:153
  148.9 3.9 %collective-permute-start.16 = (bf16[4,48,128]{2,1,0:T(8,128)(2,1)}, bf16[4,48,128]{2,1,0:T(8,128)(2,1)S(1)}, u32[]{:S(2)}, u32[]{:S(2)}) collective-permute-start(bf16[4,48,128]{2,1,0:T(8,128)(2,1)} %get-tuple-element.42), channel_id=1, source_target_pairs={{6,1},{4,7},{2,5},{10,3},{12,11},{14,13},{8,15},{7,16},{5,22},{3,2... | collective-permute-start | bytes 147464 | tf_op jit(solution)/shard_map/ppermute | solution.py:153
  152.8 1.8 collective-permute-done.16.refs_11_
  154.6 1.3 collective-permute-start.17
  156.0 0.7 copy.19.refs_14_
  156.8 0.7 copy.20.refs_15_
  157.4 9.9 %collective-permute-done.17.refs_12_ = bf16[4,48,128]{2,1,0:T(8,128)(2,1)S(1)} collective-permute-done((bf16[4,48,128]{2,1,0:T(8,128)(2,1)}, bf16[4,48,128]{2,1,0:T(8,128)(2,1)S(1)}, u32[]{:S(2)}, u32[]{:S(2)}) %collective-permute-start.17) | collective-permute-done | bytes 49184 | tf_op jit(solution)/shard_map/ppermute | solution.py:153
  167.4 11.2 %collective-permute-start.18 = (bf16[4,48,128]{2,1,0:T(8,128)(2,1)}, bf16[4,48,128]{2,1,0:T(8,128)(2,1)S(1)}, u32[]{:S(2)}, u32[]{:S(2)}) collective-permute-start(bf16[4,48,128]{2,1,0:T(8,128)(2,1)} %get-tuple-element.44), channel_id=1, source_target_pairs={{7,0},{5,6},{3,4},{11,2},{13,10},{15,12},{9,14},{22,1},{20,7},{18,... | collective-permute-start | bytes 147464 | tf_op jit(solution)/shard_map/ppermute | solution.py:153
  178.6 3.8 %fusion = (bf16[48,48,256]{2,1,0:T(8,128)(2,1)}, bf16[48,48,256]{2,1,0:T(8,128)(2,1)}, bf16[48,48,256]{2,1,0:T(8,128)(2,1)}) fusion(bf16[144,48,256]{2,1,0:T(8,128)(2,1)} %get-tuple-element.36), kind=kLoop, calls=%fused_computation.3 | loop fusion | bytes 7077888 | tf_op jit(solution)/shard_map/slice | solution.py:374
  184.0 10.7 %second.5 = (bf16[48,48,256]{2,1,0:T(8,128)(2,1)}, bf16[48,128]{1,0:T(8,128)(2,1)}) custom-call(s32[1]{0:T(128)} %get-tuple-element.57.refs_0_, s32[1]{0:T(128)} %bitcast.1.refs_1_.col_ref, s32[144]{0:T(256)} %get-tuple-element.55.refs_2_.t_ref, bf16[48,48,256]{2,1,0:T(8,128)(2,1)} %get-tuple-element.53.refs_3_, ...), custom_call_target="tpu_custom_call" | custom-call | flops 5096079360 | bytes 11010048 | tf_op jit(solution)/shard_map/second/pallas_call | solution.py:300
  194.7 2.5 collective-permute-start.25
  197.1 10.7 %second.4 = (bf16[48,48,256]{2,1,0:T(8,128)(2,1)}, bf16[48,128]{1,0:T(8,128)(2,1)}) custom-call(s32[1]{0:T(128)} %get-tuple-element.57.refs_0_, s32[1]{0:T(128)} %bitcast.1.refs_1_.col_ref, s32[144]{0:T(256)} %get-tuple-element.55.refs_2_.t_ref, bf16[48,48,256]{2,1,0:T(8,128)(2,1)} %get-tuple-element.53.refs_3_, ...), custom_call_target="tpu_custom_call" | custom-call | flops 5096079360 | bytes 11010048 | tf_op jit(solution)/shard_map/second/pallas_call | solution.py:300
  208.0 10.7 %second.3 = (bf16[48,48,256]{2,1,0:T(8,128)(2,1)}, bf16[48,128]{1,0:T(8,128)(2,1)}) custom-call(s32[1]{0:T(128)} %get-tuple-element.57.refs_0_, s32[1]{0:T(128)} %bitcast.1.refs_1_.col_ref, s32[144]{0:T(256)} %get-tuple-element.55.refs_2_.t_ref, bf16[48,48,256]{2,1,0:T(8,128)(2,1)} %get-tuple-element.53.refs_3_, ...), custom_call_target="tpu_custom_call" | custom-call | flops 5096079360 | bytes 11010048 | tf_op jit(solution)/shard_map/second/pallas_call | solution.py:300
  219.3 2.0 collective-permute-start.26
  221.3 4.8 %collective-permute-start.23 = (bf16[48,128]{1,0:T(8,128)(2,1)S(1)}, bf16[48,128]{1,0:T(8,128)(2,1)S(1)}, u32[]{:S(2)}, u32[]{:S(2)}) collective-permute-start(bf16[48,128]{1,0:T(8,128)(2,1)S(1)} %copy-done.28), channel_id=1, source_target_pairs={{6,8},{4,14},{2,12},{10,10},{12,2},{14,4},{8,6},{7,9},{5,15},{3,13... | collective-permute-start | bytes 36872 | tf_op jit(solution)/shard_map/ppermute | solution.py:382
  226.1 2.2 collective-permute-start.20
  228.3 1.1 copy-done.5
  229.4 4.0 %mix.5 = bf16[48,48,256]{2,1,0:T(8,128)(2,1)} custom-call(s32[144]{0:T(256)} %get-tuple-element.55.refs_2_.t_ref, s32[1]{0:T(128)} %bitcast.1.refs_1_.col_ref, bf16[48,48,256]{2,1,0:T(8,128)(2,1)} %get-tuple-element.49.own_ref, bf16[48,48,256]{2,1,0:T(8,128)(2,1)} %copy-done.5, bf16[48,128]{1,0:T(8,128)(2,1)} %copy-done.10), custom_call_target="tpu_custom_call" | custom-call | tf_op jit(solution)/shard_map/mix/pallas_call | solution.py:339
  233.4 3.8 %collective-permute-start.27 = (bf16[48,48,256]{2,1,0:T(8,128)(2,1)}, bf16[48,48,256]{2,1,0:T(8,128)(2,1)S(1)}, u32[]{:S(2)}, u32[]{:S(2)}) collective-permute-start(bf16[48,48,256]{2,1,0:T(8,128)(2,1)} %mix.5), channel_id=1, source_target_pairs={{0,0},{6,1},{4,2},{2,3},{10,4},{12,5},{14,6},{8,7},{1,8},{7,9},{5,... | collective-permute-start | bytes 3538952 | tf_op jit(solution)/shard_map/ppermute | solution.py:384
  237.2 0.6 copy-done.9
  237.8 1.0 copy-done.3
  238.8 4.0 %mix.4 = bf16[48,48,256]{2,1,0:T(8,128)(2,1)} custom-call(s32[144]{0:T(256)} %get-tuple-element.55.refs_2_.t_ref, s32[1]{0:T(128)} %bitcast.1.refs_1_.col_ref, bf16[48,48,256]{2,1,0:T(8,128)(2,1)} %get-tuple-element.47.own_ref, bf16[48,48,256]{2,1,0:T(8,128)(2,1)} %copy-done.3, bf16[48,128]{1,0:T(8,128)(2,1)} %copy-done.9), custom_call_target="tpu_custom_call" | custom-call | tf_op jit(solution)/shard_map/mix/pallas_call | solution.py:339
  242.9 2.0 collective-permute-start.24
  244.9 0.6 copy-done.8
  245.5 1.0 copy-done.4
  246.5 4.0 %mix.3 = bf16[48,48,256]{2,1,0:T(8,128)(2,1)} custom-call(s32[144]{0:T(256)} %get-tuple-element.55.refs_2_.t_ref, s32[1]{0:T(128)} %bitcast.1.refs_1_.col_ref, bf16[48,48,256]{2,1,0:T(8,128)(2,1)} %get-tuple-element.45.own_ref, bf16[48,48,256]{2,1,0:T(8,128)(2,1)} %copy-done.4, bf16[48,128]{1,0:T(8,128)(2,1)} %copy-done.8), custom_call_target="tpu_custom_call" | custom-call | tf_op jit(solution)/shard_map/mix/pallas_call | solution.py:339
  250.5 3.6 %collective-permute-start.21 = (bf16[48,48,256]{2,1,0:T(8,128)(2,1)}, bf16[48,48,256]{2,1,0:T(8,128)(2,1)S(1)}, u32[]{:S(2)}, u32[]{:S(2)}) collective-permute-start(bf16[48,48,256]{2,1,0:T(8,128)(2,1)} %mix.3), channel_id=1, source_target_pairs={{0,0},{6,1},{4,2},{2,3},{10,4},{12,5},{14,6},{8,7},{1,8},{7,9},{5,... | collective-permute-start | bytes 3538952 | tf_op jit(solution)/shard_map/ppermute | solution.py:384
  254.1 36.2 %collective-permute-done.27 = bf16[48,48,256]{2,1,0:T(8,128)(2,1)S(1)} collective-permute-done((bf16[48,48,256]{2,1,0:T(8,128)(2,1)}, bf16[48,48,256]{2,1,0:T(8,128)(2,1)S(1)}, u32[]{:S(2)}, u32[]{:S(2)}) %collective-permute-start.27) | collective-permute-done | bytes 1179680 | tf_op jit(solution)/shard_map/ppermute | solution.py:384
  290.2 12.6 %collective-permute-done.24 = bf16[48,48,256]{2,1,0:T(8,128)(2,1)S(1)} collective-permute-done((bf16[48,48,256]{2,1,0:T(8,128)(2,1)}, bf16[48,48,256]{2,1,0:T(8,128)(2,1)S(1)}, u32[]{:S(2)}, u32[]{:S(2)}) %collective-permute-start.24) | collective-permute-done | bytes 1179680 | tf_op jit(solution)/shard_map/ppermute | solution.py:384
  302.9 12.6 %collective-permute-done.21 = bf16[48,48,256]{2,1,0:T(8,128)(2,1)S(1)} collective-permute-done((bf16[48,48,256]{2,1,0:T(8,128)(2,1)}, bf16[48,48,256]{2,1,0:T(8,128)(2,1)S(1)}, u32[]{:S(2)}, u32[]{:S(2)}) %collective-permute-start.21) | collective-permute-done | bytes 1179680 | tf_op jit(solution)/shard_map/ppermute | solution.py:384
  315.5 1.9 pad_maximum_fusion
  (76 shorter events, 3.9 us)
Async XLA Ops:
  4.1 19.7 %collective-permute-start = (bf16[48,48,256]{2,1,0:T(8,128)(2,1)}, bf16[48,48,256]{2,1,0:T(8,128)(2,1)S(1)}, u32[]{:S(2)}, u32[]{:S(2)}) collective-permute-start(bf16[48,48,256]{2,1,0:T(8,128)(2,1)} %enter.3), channel_id=1, source_target_pairs={{0,0},{1,6},{2,4},{3,2},{4,10},{5,12},{6,14},{7,8},{8,1},{9,7},{10... | collective-permute-start | bytes 3538952 | tf_op jit(solution)/shard_map/ppermute | solution.py:367
  12.9 23.4 %collective-permute-start.1 = (bf16[48,48,256]{2,1,0:T(8,128)(2,1)}, bf16[48,48,256]{2,1,0:T(8,128)(2,1)S(1)}, u32[]{:S(2)}, u32[]{:S(2)}) collective-permute-start(bf16[48,48,256]{2,1,0:T(8,128)(2,1)} %enter.4), channel_id=1, source_target_pairs={{0,0},{1,6},{2,4},{3,2},{4,10},{5,12},{6,14},{7,8},{8,1},{9,7},{10... | collective-permute-start | bytes 3538952 | tf_op jit(solution)/shard_map/ppermute | solution.py:367
  17.5 82.3 %copy-start.11 = (s32[2]{0:T(128)S(1)}, s32[2]{0:T(128)}, u32[]{:S(2)}) copy-start(s32[2]{0:T(128)} %param.9) | copy-start | bytes 28
  17.5 83.0 %copy-start.30 = (s32[4]{0:T(128)S(1)}, s32[4]{0:T(128)}, u32[]{:S(2)}) copy-start(s32[4]{0:T(128)} %constant.66.clone) | copy-start | bytes 52
  17.5 85.0 %copy-start.6 = (bf16[9,48,48]{2,1,0:T(8,128)(2,1)S(1)}, bf16[9,48,48]{2,1,0:T(8,128)(2,1)}, u32[]{:S(2)}) copy-start(bf16[9,48,48]{2,1,0:T(8,128)(2,1)} %param.11) | copy-start | bytes 124420
  17.5 85.9 %copy-start.12 = (f32[48]{0:T(128)S(1)}, f32[48]{0:T(128)}, u32[]{:S(2)}) copy-start(f32[48]{0:T(128)} %param.12) | copy-start | bytes 580
  17.5 31.5 %collective-permute-start.2 = (bf16[48,48,256]{2,1,0:T(8,128)(2,1)}, bf16[48,48,256]{2,1,0:T(8,128)(2,1)S(1)}, u32[]{:S(2)}, u32[]{:S(2)}) collective-permute-start(bf16[48,48,256]{2,1,0:T(8,128)(2,1)} %enter.5), channel_id=1, source_target_pairs={{0,0},{1,6},{2,4},{3,2},{4,10},{5,12},{6,14},{7,8},{8,1},{9,7},{10... | collective-permute-start | bytes 3538952 | tf_op jit(solution)/shard_map/ppermute | solution.py:367
  23.7 25.3 %copy-start = (bf16[48,48,256]{2,1,0:T(8,128)(2,1)}, bf16[48,48,256]{2,1,0:T(8,128)(2,1)S(1)}, u32[]{:S(2)}) copy-start(bf16[48,48,256]{2,1,0:T(8,128)(2,1)S(1)} %collective-permute-done.refs_0_.refs_3_.refs_16_) | copy-start | bytes 3538948
  36.4 12.6 %copy-start.1 = (bf16[48,48,256]{2,1,0:T(8,128)(2,1)}, bf16[48,48,256]{2,1,0:T(8,128)(2,1)S(1)}, u32[]{:S(2)}) copy-start(bf16[48,48,256]{2,1,0:T(8,128)(2,1)S(1)} %collective-permute-done.1.refs_1_.refs_4_.refs_16_) | copy-start | bytes 3538948
  49.0 1.0 copy-start.2
  54.4 49.7 %collective-permute-start.5 = (bf16[72,48,128]{2,1,0:T(8,128)(2,1)}, bf16[72,48,128]{2,1,0:T(8,128)(2,1)S(1)}, u32[]{:S(2)}, u32[]{:S(2)}) collective-permute-start(bf16[72,48,128]{2,1,0:T(8,128)(2,1)} %get-tuple-element.30), channel_id=1, source_target_pairs={{0,6},{6,4},{4,2},{2,10},{10,12},{12,14},{14,8},{1,7},{7,5},{5,3},... | collective-permute-start | bytes 2654216 | tf_op jit(solution)/shard_map/ppermute | solution.py:153
  55.7 48.4 %collective-permute-start.6 = (bf16[72,48,128]{2,1,0:T(8,128)(2,1)}, bf16[72,48,128]{2,1,0:T(8,128)(2,1)S(1)}, u32[]{:S(2)}, u32[]{:S(2)}) collective-permute-start(bf16[72,48,128]{2,1,0:T(8,128)(2,1)} %get-tuple-element.31), channel_id=1, source_target_pairs={{6,0},{4,6},{2,4},{10,2},{12,10},{14,12},{8,14},{7,1},{5,7},{3,5},... | collective-permute-start | bytes 2654216 | tf_op jit(solution)/shard_map/ppermute | solution.py:153
  60.9 43.1 %collective-permute-start.3 = (bf16[32,48,256]{2,1,0:T(8,128)(2,1)}, bf16[32,48,256]{2,1,0:T(8,128)(2,1)S(1)}, u32[]{:S(2)}, u32[]{:S(2)}) collective-permute-start(bf16[32,48,256]{2,1,0:T(8,128)(2,1)} %get-tuple-element.28), channel_id=1, source_target_pairs={{0,1},{6,7},{4,5},{2,3},{10,11},{12,13},{14,15},{8,9},{1,16},{7,22... | collective-permute-start | bytes 2359304 | tf_op jit(solution)/shard_map/ppermute | solution.py:153
  65.3 38.7 %collective-permute-start.4 = (bf16[32,48,256]{2,1,0:T(8,128)(2,1)}, bf16[32,48,256]{2,1,0:T(8,128)(2,1)}, u32[]{:S(2)}, u32[]{:S(2)}) collective-permute-start(bf16[32,48,256]{2,1,0:T(8,128)(2,1)} %get-tuple-element.29), channel_id=1, source_target_pairs={{1,0},{7,6},{5,4},{3,2},{11,10},{13,12},{15,14},{9,8},{16,1},{22,7... | collective-permute-start | bytes 2359304 | tf_op jit(solution)/shard_map/ppermute | solution.py:153
  67.2 11.7 %collective-permute-start.7 = (bf16[4,48,128]{2,1,0:T(8,128)(2,1)}, bf16[4,48,128]{2,1,0:T(8,128)(2,1)S(1)}, u32[]{:S(2)}, u32[]{:S(2)}) collective-permute-start(bf16[4,48,128]{2,1,0:T(8,128)(2,1)} %get-tuple-element.32), channel_id=1, source_target_pairs={{0,7},{6,5},{4,3},{2,11},{10,13},{12,15},{14,9},{1,22},{7,20},{5,1... | collective-permute-start | bytes 147464 | tf_op jit(solution)/shard_map/ppermute | solution.py:153
  78.9 25.2 %copy-start.20 = (bf16[4,48,128]{2,1,0:T(8,128)(2,1)}, bf16[4,48,128]{2,1,0:T(8,128)(2,1)S(1)}, u32[]{:S(2)}) copy-start(bf16[4,48,128]{2,1,0:T(8,128)(2,1)S(1)} %collective-permute-done.7.refs_10_) | copy-start | bytes 147460
  78.9 5.9 %collective-permute-start.8 = (bf16[4,48,128]{2,1,0:T(8,128)(2,1)}, bf16[4,48,128]{2,1,0:T(8,128)(2,1)S(1)}, u32[]{:S(2)}, u32[]{:S(2)}) collective-permute-start(bf16[4,48,128]{2,1,0:T(8,128)(2,1)} %get-tuple-element.33), channel_id=1, source_target_pairs={{6,1},{4,7},{2,5},{10,3},{12,11},{14,13},{8,15},{7,16},{5,22},{3,2... | collective-permute-start | bytes 147464 | tf_op jit(solution)/shard_map/ppermute | solution.py:153
  84.9 19.3 %copy-start.21 = (bf16[4,48,128]{2,1,0:T(8,128)(2,1)}, bf16[4,48,128]{2,1,0:T(8,128)(2,1)S(1)}, u32[]{:S(2)}) copy-start(bf16[4,48,128]{2,1,0:T(8,128)(2,1)S(1)} %collective-permute-done.8.refs_11_) | copy-start | bytes 147460
  84.9 7.3 %collective-permute-start.9 = (bf16[4,48,128]{2,1,0:T(8,128)(2,1)}, bf16[4,48,128]{2,1,0:T(8,128)(2,1)S(1)}, u32[]{:S(2)}, u32[]{:S(2)}) collective-permute-start(bf16[4,48,128]{2,1,0:T(8,128)(2,1)} %get-tuple-element.34), channel_id=1, source_target_pairs={{1,6},{7,4},{5,2},{3,10},{11,12},{13,14},{15,8},{16,7},{22,5},{20,... | collective-permute-start | bytes 147464 | tf_op jit(solution)/shard_map/ppermute | solution.py:153
  92.2 11.9 %copy-start.22 = (bf16[4,48,128]{2,1,0:T(8,128)(2,1)}, bf16[4,48,128]{2,1,0:T(8,128)(2,1)S(1)}, u32[]{:S(2)}) copy-start(bf16[4,48,128]{2,1,0:T(8,128)(2,1)S(1)} %collective-permute-done.9.refs_12_) | copy-start | bytes 147460
  92.2 11.8 %collective-permute-start.10 = (bf16[4,48,128]{2,1,0:T(8,128)(2,1)}, bf16[4,48,128]{2,1,0:T(8,128)(2,1)S(1)}, u32[]{:S(2)}, u32[]{:S(2)}) collective-permute-start(bf16[4,48,128]{2,1,0:T(8,128)(2,1)} %get-tuple-element.35), channel_id=1, source_target_pairs={{7,0},{5,6},{3,4},{11,2},{13,10},{15,12},{9,14},{22,1},{20,7},{18,... | collective-permute-start | bytes 147464 | tf_op jit(solution)/shard_map/ppermute | solution.py:153
  104.0 0.6 copy-start.23
  104.0 0.9 copy-start.18
  104.1 1.2 copy-start.14
  104.1 1.5 copy-start.15
  105.5 50.3 %copy-start.7 = (bf16[9,48,48]{2,1,0:T(8,128)(2,1)S(1)}, bf16[9,48,48]{2,1,0:T(8,128)(2,1)}, u32[]{:S(2)}) copy-start(bf16[9,48,48]{2,1,0:T(8,128)(2,1)} %param.13) | copy-start | bytes 124420
  105.5 51.2 %copy-start.13 = (f32[48]{0:T(128)S(1)}, f32[48]{0:T(128)}, u32[]{:S(2)}) copy-start(f32[48]{0:T(128)} %param.14) | copy-start | bytes 580
  127.4 55.0 %collective-permute-start.13 = (bf16[72,48,128]{2,1,0:T(8,128)(2,1)}, bf16[72,48,128]{2,1,0:T(8,128)(2,1)S(1)}, u32[]{:S(2)}, u32[]{:S(2)}) collective-permute-start(bf16[72,48,128]{2,1,0:T(8,128)(2,1)} %get-tuple-element.39), channel_id=1, source_target_pairs={{0,6},{6,4},{4,2},{2,10},{10,12},{12,14},{14,8},{1,7},{7,5},{5,3},... | collective-permute-start | bytes 2654216 | tf_op jit(solution)/shard_map/ppermute | solution.py:153
  128.7 53.8 %collective-permute-start.14 = (bf16[72,48,128]{2,1,0:T(8,128)(2,1)}, bf16[72,48,128]{2,1,0:T(8,128)(2,1)S(1)}, u32[]{:S(2)}, u32[]{:S(2)}) collective-permute-start(bf16[72,48,128]{2,1,0:T(8,128)(2,1)} %get-tuple-element.40), channel_id=1, source_target_pairs={{6,0},{4,6},{2,4},{10,2},{12,10},{14,12},{8,14},{7,1},{5,7},{3,5},... | collective-permute-start | bytes 2654216 | tf_op jit(solution)/shard_map/ppermute | solution.py:153
  134.0 48.5 %collective-permute-start.11 = (bf16[32,48,256]{2,1,0:T(8,128)(2,1)}, bf16[32,48,256]{2,1,0:T(8,128)(2,1)S(1)}, u32[]{:S(2)}, u32[]{:S(2)}) collective-permute-start(bf16[32,48,256]{2,1,0:T(8,128)(2,1)} %get-tuple-element.37), channel_id=1, source_target_pairs={{0,1},{6,7},{4,5},{2,3},{10,11},{12,13},{14,15},{8,9},{1,16},{7,22... | collective-permute-start | bytes 2359304 | tf_op jit(solution)/shard_map/ppermute | solution.py:153
  135.9 46.5 %collective-permute-start.12 = (bf16[32,48,256]{2,1,0:T(8,128)(2,1)}, bf16[32,48,256]{2,1,0:T(8,128)(2,1)}, u32[]{:S(2)}, u32[]{:S(2)}) collective-permute-start(bf16[32,48,256]{2,1,0:T(8,128)(2,1)} %get-tuple-element.38), channel_id=1, source_target_pairs={{1,0},{7,6},{5,4},{3,2},{11,10},{13,12},{15,14},{9,8},{16,1},{22,7... | collective-permute-start | bytes 2359304 | tf_op jit(solution)/shard_map/ppermute | solution.py:153
  139.3 9.6 %collective-permute-start.15 = (bf16[4,48,128]{2,1,0:T(8,128)(2,1)}, bf16[4,48,128]{2,1,0:T(8,128)(2,1)S(1)}, u32[]{:S(2)}, u32[]{:S(2)}) collective-permute-start(bf16[4,48,128]{2,1,0:T(8,128)(2,1)} %get-tuple-element.41), channel_id=1, source_target_pairs={{0,7},{6,5},{4,3},{2,11},{10,13},{12,15},{14,9},{1,22},{7,20},{5,1... | collective-permute-start | bytes 147464 | tf_op jit(solution)/shard_map/ppermute | solution.py:153
  148.9 33.5 %copy-start.24 = (bf16[4,48,128]{2,1,0:T(8,128)(2,1)}, bf16[4,48,128]{2,1,0:T(8,128)(2,1)S(1)}, u32[]{:S(2)}) copy-start(bf16[4,48,128]{2,1,0:T(8,128)(2,1)S(1)} %collective-permute-done.15.refs_10_) | copy-start | bytes 147460
  148.9 5.7 %collective-permute-start.16 = (bf16[4,48,128]{2,1,0:T(8,128)(2,1)}, bf16[4,48,128]{2,1,0:T(8,128)(2,1)S(1)}, u32[]{:S(2)}, u32[]{:S(2)}) collective-permute-start(bf16[4,48,128]{2,1,0:T(8,128)(2,1)} %get-tuple-element.42), channel_id=1, source_target_pairs={{6,1},{4,7},{2,5},{10,3},{12,11},{14,13},{8,15},{7,16},{5,22},{3,2... | collective-permute-start | bytes 147464 | tf_op jit(solution)/shard_map/ppermute | solution.py:153
  154.6 27.8 %copy-start.25 = (bf16[4,48,128]{2,1,0:T(8,128)(2,1)}, bf16[4,48,128]{2,1,0:T(8,128)(2,1)S(1)}, u32[]{:S(2)}) copy-start(bf16[4,48,128]{2,1,0:T(8,128)(2,1)S(1)} %collective-permute-done.16.refs_11_) | copy-start | bytes 147460
  154.6 12.8 %collective-permute-start.17 = (bf16[4,48,128]{2,1,0:T(8,128)(2,1)}, bf16[4,48,128]{2,1,0:T(8,128)(2,1)S(1)}, u32[]{:S(2)}, u32[]{:S(2)}) collective-permute-start(bf16[4,48,128]{2,1,0:T(8,128)(2,1)} %get-tuple-element.43), channel_id=1, source_target_pairs={{1,6},{7,4},{5,2},{3,10},{11,12},{13,14},{15,8},{16,7},{22,5},{20,... | collective-permute-start | bytes 147464 | tf_op jit(solution)/shard_map/ppermute | solution.py:153
  167.4 15.0 %copy-start.26 = (bf16[4,48,128]{2,1,0:T(8,128)(2,1)}, bf16[4,48,128]{2,1,0:T(8,128)(2,1)S(1)}, u32[]{:S(2)}) copy-start(bf16[4,48,128]{2,1,0:T(8,128)(2,1)S(1)} %collective-permute-done.17.refs_12_) | copy-start | bytes 147460
  167.4 15.0 %collective-permute-start.18 = (bf16[4,48,128]{2,1,0:T(8,128)(2,1)}, bf16[4,48,128]{2,1,0:T(8,128)(2,1)S(1)}, u32[]{:S(2)}, u32[]{:S(2)}) collective-permute-start(bf16[4,48,128]{2,1,0:T(8,128)(2,1)} %get-tuple-element.44), channel_id=1, source_target_pairs={{7,0},{5,6},{3,4},{11,2},{13,10},{15,12},{9,14},{22,1},{20,7},{18,... | collective-permute-start | bytes 147464 | tf_op jit(solution)/shard_map/ppermute | solution.py:153
  182.4 0.6 copy-start.27
  182.4 0.9 copy-start.19
  182.5 1.2 copy-start.16
  182.5 1.5 copy-start.17
  194.7 33.6 %collective-permute-start.25 = (bf16[48,48,256]{2,1,0:T(8,128)(2,1)}, bf16[48,48,256]{2,1,0:T(8,128)(2,1)S(1)}, u32[]{:S(2)}, u32[]{:S(2)}) collective-permute-start(bf16[48,48,256]{2,1,0:T(8,128)(2,1)} %get-tuple-element.49.own_ref), channel_id=1, source_target_pairs={{0,8},{6,14},{4,12},{2,10},{10,2},{12,4},{14,6},{8,0},{1,9},{7,15}... | collective-permute-start | bytes 3538952 | tf_op jit(solution)/shard_map/ppermute | solution.py:381
  207.9 11.4 %copy-start.29 = (bf16[48,128]{1,0:T(8,128)(2,1)S(1)}, bf16[48,128]{1,0:T(8,128)(2,1)}, u32[]{:S(2)}) copy-start(bf16[48,128]{1,0:T(8,128)(2,1)} %get-tuple-element.50) | copy-start | bytes 36868
  207.9 13.4 %copy-start.28 = (bf16[48,128]{1,0:T(8,128)(2,1)S(1)}, bf16[48,128]{1,0:T(8,128)(2,1)}, u32[]{:S(2)}) copy-start(bf16[48,128]{1,0:T(8,128)(2,1)} %get-tuple-element.48) | copy-start | bytes 36868
  207.9 29.3 %collective-permute-start.22 = (bf16[48,48,256]{2,1,0:T(8,128)(2,1)}, bf16[48,48,256]{2,1,0:T(8,128)(2,1)S(1)}, u32[]{:S(2)}, u32[]{:S(2)}) collective-permute-start(bf16[48,48,256]{2,1,0:T(8,128)(2,1)} %get-tuple-element.47.own_ref), channel_id=1, source_target_pairs={{0,8},{6,14},{4,12},{2,10},{10,2},{12,4},{14,6},{8,0},{1,9},{7,15}... | collective-permute-start | bytes 3538952 | tf_op jit(solution)/shard_map/ppermute | solution.py:381
  218.7 26.2 %collective-permute-start.19 = (bf16[48,48,256]{2,1,0:T(8,128)(2,1)}, bf16[48,48,256]{2,1,0:T(8,128)(2,1)S(1)}, u32[]{:S(2)}, u32[]{:S(2)}) collective-permute-start(bf16[48,48,256]{2,1,0:T(8,128)(2,1)} %get-tuple-element.45.own_ref), channel_id=1, source_target_pairs={{0,8},{6,14},{4,12},{2,10},{10,2},{12,4},{14,6},{8,0},{1,9},{7,15}... | collective-permute-start | bytes 3538952 | tf_op jit(solution)/shard_map/ppermute | solution.py:381
  219.3 6.8 %collective-permute-start.26 = (bf16[48,128]{1,0:T(8,128)(2,1)S(1)}, bf16[48,128]{1,0:T(8,128)(2,1)S(1)}, u32[]{:S(2)}, u32[]{:S(2)}) collective-permute-start(bf16[48,128]{1,0:T(8,128)(2,1)S(1)} %copy-done.29), channel_id=1, source_target_pairs={{6,8},{4,14},{2,12},{10,10},{12,2},{14,4},{8,6},{7,9},{5,15},{3,13... | collective-permute-start | bytes 36872 | tf_op jit(solution)/shard_map/ppermute | solution.py:382
  221.3 15.9 %collective-permute-start.23 = (bf16[48,128]{1,0:T(8,128)(2,1)S(1)}, bf16[48,128]{1,0:T(8,128)(2,1)S(1)}, u32[]{:S(2)}, u32[]{:S(2)}) collective-permute-start(bf16[48,128]{1,0:T(8,128)(2,1)S(1)} %copy-done.28), channel_id=1, source_target_pairs={{6,8},{4,14},{2,12},{10,10},{12,2},{14,4},{8,6},{7,9},{5,15},{3,13... | collective-permute-start | bytes 36872 | tf_op jit(solution)/shard_map/ppermute | solution.py:382
  226.1 2.2 copy-start.10
  226.1 18.8 %collective-permute-start.20 = (bf16[48,128]{1,0:T(8,128)(2,1)}, bf16[48,128]{1,0:T(8,128)(2,1)S(1)}, u32[]{:S(2)}, u32[]{:S(2)}) collective-permute-start(bf16[48,128]{1,0:T(8,128)(2,1)} %get-tuple-element.46), channel_id=1, source_target_pairs={{6,8},{4,14},{2,12},{10,10},{12,2},{14,4},{8,6},{7,9},{5,15},{3,13... | collective-permute-start | bytes 36872 | tf_op jit(solution)/shard_map/ppermute | solution.py:382
  228.3 1.1 copy-start.5
  233.4 56.9 %collective-permute-start.27 = (bf16[48,48,256]{2,1,0:T(8,128)(2,1)}, bf16[48,48,256]{2,1,0:T(8,128)(2,1)S(1)}, u32[]{:S(2)}, u32[]{:S(2)}) collective-permute-start(bf16[48,48,256]{2,1,0:T(8,128)(2,1)} %mix.5), channel_id=1, source_target_pairs={{0,0},{6,1},{4,2},{2,3},{10,4},{12,5},{14,6},{8,7},{1,8},{7,9},{5,... | collective-permute-start | bytes 3538952 | tf_op jit(solution)/shard_map/ppermute | solution.py:384
  237.2 0.6 copy-start.9
  237.8 1.0 copy-start.3
  242.9 60.0 %collective-permute-start.24 = (bf16[48,48,256]{2,1,0:T(8,128)(2,1)}, bf16[48,48,256]{2,1,0:T(8,128)(2,1)S(1)}, u32[]{:S(2)}, u32[]{:S(2)}) collective-permute-start(bf16[48,48,256]{2,1,0:T(8,128)(2,1)} %mix.4), channel_id=1, source_target_pairs={{0,0},{6,1},{4,2},{2,3},{10,4},{12,5},{14,6},{8,7},{1,8},{7,9},{5,... | collective-permute-start | bytes 3538952 | tf_op jit(solution)/shard_map/ppermute | solution.py:384
  244.9 0.6 copy-start.8
  245.5 1.0 copy-start.4
  250.5 65.0 %collective-permute-start.21 = (bf16[48,48,256]{2,1,0:T(8,128)(2,1)}, bf16[48,48,256]{2,1,0:T(8,128)(2,1)S(1)}, u32[]{:S(2)}, u32[]{:S(2)}) collective-permute-start(bf16[48,48,256]{2,1,0:T(8,128)(2,1)} %mix.3), channel_id=1, source_target_pairs={{0,0},{6,1},{4,2},{2,3},{10,4},{12,5},{14,6},{8,7},{1,8},{7,9},{5,... | collective-permute-start | bytes 3538952 | tf_op jit(solution)/shard_map/ppermute | solution.py:384

commit v2 on v0

v2 whole, which is shorter than its diff:
```python
import functools

import jax
import jax.numpy as jnp
from jax import lax
from jax.experimental import pallas as pl
from jax.experimental.pallas import tpu as pltpu
from jax.sharding import PartitionSpec as P

BAND = 1024
DMAX = 32
C = 48
ROWS = 72
COLS = 256
WIDE = 2 * COLS
LANES = 128
HALO = DMAX
CORNER = DMAX // 2
SPAN = ROWS + 2 * HALO
PREP = 4
UNROLL = 4
STACK = 8
AXES = ("pos", "off")

SMEM = pl.BlockSpec(memory_space=pltpu.SMEM)
VMEM = pl.BlockSpec(memory_space=pltpu.VMEM)
ANY = pl.BlockSpec(memory_space=pl.ANY)
PARAMS = pltpu.CompilerParams(vmem_limit_bytes=56 * 2**20)


def device(pair, x, z, core):
    return (2 * pair + core) * 8 + 2 * z + x


def home(stored, block):
    return device(stored // 2, block % 2, block // 2, stored % 2)


def place(strip, fold):
    stored = strip // 2
    return device(stored // 2, stored % 2, (4 - fold) % 4, strip % 2)


def lead(stored, fold):
    return (fold == 1) & (stored % 2 == 0) | (fold == 3) & (stored % 2 == 1)


CELLS = [(strip, fold) for strip in range(32) for fold in range(4)]


def routes(turn):
    out = []
    for strip, fold in CELLS:
        core, stored = strip % 2, strip // 2
        first = (core == int(lead(stored, fold))) == (turn == 0)
        out.append((home(stored, fold if first else 7 - fold), place(strip, fold)))
    return out


VIA = {(0, 1): (0, 0, 0), (0, 7): (0, 3, 0), (1, 2): (1, 1, 1), (1, 4): (1, 2, 1)}
STAY = ((0, 0), (0, 6), (1, 3), (1, 5))


def moves(strip_step, fold_step):
    return [
        (place(s, f), place(s + strip_step, f + fold_step))
        for s, f in CELLS
        if 0 <= s + strip_step < 32 and 0 <= f + fold_step < 4
    ]


def whereabouts():
    pos, off = lax.axis_index("pos"), lax.axis_index("off")
    fold = jnp.minimum(off, 7 - off)
    early = jnp.where(off < 4, 0, 1) ^ lead(pos, fold).astype(jnp.int32)
    stored = 2 * (pos // 2) + off % 2
    core = pos % 2
    work = (4 - off // 2) % 4
    order = core ^ lead(stored, work).astype(jnp.int32)
    values = (pos * 2 * ROWS, off, early, stored * 2 * ROWS + core * ROWS, work, order, core)
    return [v.astype(jnp.int32) for v in values]


STORED_ROW, STORED_BLOCK, EARLY, ROW, FOLD, ORDER, CORE = range(7)


def threshold(limit_ref, row):
    last = limit_ref.shape[0] - 1
    return jnp.minimum(limit_ref[row], jnp.minimum(2 * row + 1, 2 * last - 2 * row))


def offsets(block, dims):
    return jnp.abs(lax.broadcasted_iota(jnp.int32, dims, len(dims) - 1) + (block * COLS - BAND))


def both_offsets(fold):
    return jnp.concatenate([offsets(fold, (C, COLS)), offsets(7 - fold, (C, COLS))], axis=1)


def cost(micros):
    return pl.CostEstimate(flops=0, bytes_accessed=int(micros * 3.69e6), transcendentals=0)


def shape(*dims):
    return jax.ShapeDtypeStruct(dims, jnp.bfloat16)


def enter_kernel(turn, at_ref, limit_ref, x_ref, *rest):
    out_ref = rest[-1]
    x = jnp.swapaxes(x_ref[...], 0, 1)
    away = offsets(at_ref[STORED_BLOCK], (C, COLS))
    row0 = at_ref[STORED_ROW] + (at_ref[EARLY] ^ turn) * ROWS
    for i in range(ROWS):
        seen = away <= threshold(limit_ref, row0 + i)
        out_ref[i] = jnp.where(seen, x[i], jnp.zeros((), jnp.bfloat16))


def enter(turn, at, row_limit, band_map, after):
    return pl.pallas_call(
        functools.partial(enter_kernel, turn),
        grid_spec=pltpu.PrefetchScalarGridSpec(
            num_scalar_prefetch=1,
            grid=(1,),
            in_specs=[SMEM, pl.BlockSpec((C, ROWS, COLS), lambda i, at_ref: (0, at_ref[EARLY] ^ turn, 0))]
            + [ANY] * len(after),
            out_specs=pl.BlockSpec((ROWS, C, COLS), lambda i, at_ref: (0, 0, 0)),
        ),
        out_shape=shape(ROWS, C, COLS),
        compiler_params=PARAMS,
        cost_estimate=cost(4.0),
        name="enter",
    )(at, row_limit, band_map, *after)


EDGES = [shape(ROWS, C, LANES)] * 2 + [shape(HALO, C, WIDE)] * 2


def pack_edges(cells, inward, outward, top, bottom):
    lane = lax.broadcasted_iota(jnp.int32, (C, LANES), 1)
    for i in range(ROWS):
        inward[i] = jnp.where(lane < 64, cells[i, :, 2 * LANES : 3 * LANES], cells[i, :, LANES : 2 * LANES])
        outward[i] = jnp.where(lane < 64, cells[i, :, :LANES], cells[i, :, 3 * LANES :])
    top[...] = cells[pl.ds(0, HALO)]
    bottom[...] = cells[pl.ds(ROWS - HALO, HALO)]


def pack_kernel(at_ref, early_ref, late_ref, out_ref, *edges):
    @pl.when(at_ref[ORDER] == 0)
    def _():
        out_ref[:, :, :COLS] = early_ref[...]
        out_ref[:, :, COLS:] = late_ref[...]

    @pl.when(at_ref[ORDER] != 0)
    def _():
        out_ref[:, :, :COLS] = late_ref[...]
        out_ref[:, :, COLS:] = early_ref[...]

    pack_edges(out_ref, *edges)


def pack(at, early, late):
    out = [shape(ROWS, C, WIDE)] + EDGES
    return pl.pallas_call(
        pack_kernel,
        in_specs=[SMEM, VMEM, VMEM],
        out_specs=[VMEM] * len(out),
        out_shape=out,
        compiler_params=PARAMS,
        cost_estimate=cost(4.0),
        name="pack",
    )(at, early, late)


def send(cells, strip_step, fold_step):
    return lax.ppermute(cells, AXES, moves(strip_step, fold_step))


def exchange(at, inward, outward, top, bottom):
    previous = send(inward, 0, 1)
    following = send(outward, 0, -1)
    below = send(top, -1, 0)
    above = send(bottom, 1, 0)
    following = jnp.where(at[FOLD] == 3, inward, following)
    ends = lambda first: jnp.concatenate(
        [lax.slice_in_dim(x, first, first + CORNER) for x in (previous, following)], axis=0
    )
    corner_below = send(ends(0), -1, 0)
    corner_above = send(ends(ROWS - CORNER), 1, 0)
    return previous, following, above, below, corner_above, corner_below


def conv_kernel(final, at_ref, d_ref, limit_ref, cells, *refs):
    previous, following, above, below, corner_above, corner_below, w_ref, b_ref = refs[:8]
    if final:
        own_ref, first_ref, second_ref, edge_ref, other_ref = refs[8:13]
        out_ref, rest = refs[13], refs[14:]
    else:
        out_ref, edges, rest = refs[8], refs[9:13], refs[13:]
    mid, before, behind, plus_ref, minus_ref, sems = rest

    copies = [
        (above, mid.at[pl.ds(0, HALO)]),
        (cells, mid.at[pl.ds(HALO, ROWS)]),
        (below, mid.at[pl.ds(HALO + ROWS, HALO)]),
        (previous, before.at[pl.ds(HALO, ROWS)]),
        (following, behind.at[pl.ds(HALO, ROWS)]),
        (corner_above.at[pl.ds(0, CORNER)], before.at[pl.ds(HALO - CORNER, CORNER)]),
        (corner_above.at[pl.ds(CORNER, CORNER)], behind.at[pl.ds(HALO - CORNER, CORNER)]),
        (corner_below.at[pl.ds(0, CORNER)], before.at[pl.ds(HALO + ROWS, CORNER)]),
        (corner_below.at[pl.ds(CORNER, CORNER)], behind.at[pl.ds(HALO + ROWS, CORNER)]),
    ]
    copies = [pltpu.make_async_copy(src, dst, sems.at[i]) for i, (src, dst) in enumerate(copies)]
    for copy in copies:
        copy.start()
    for copy in copies:
        copy.wait()

    d = d_ref[0]
    lo = d // 2
    hi = (d + 1) // 2
    odd = d - 2 * lo
    lane = lax.broadcasted_iota(jnp.int32, (C, LANES), 1)
    even_lane = (lane & 1) == 0

    def tiles(r):
        own = [mid[r, :, LANES * i : LANES * (i + 1)] for i in range(4)]
        return [before[r], *own[:2], behind[r], *own[2:]]

    def shifted(t, step, back):
        keep = lane < (step if back else LANES - step)
        turn = step if back else LANES - step
        left, a, b, right, c, e = t
        runs = ((left, a, b), (right, c, e)) if back else ((a, b, right), (c, e, left))
        out = []
        for run in runs:
            x, y, z = [pltpu.roll(v, turn, axis=1) for v in run]
            out += [jnp.where(keep, x, y), jnp.where(keep, y, z)]
        return jnp.concatenate(out, axis=1)

    start = HALO - hi

    def prepare(i, _):
        for j in range(PREP):
            r = start + i * PREP + j
            x, y = tiles(r), tiles(r + odd)
            both = [jnp.where(even_lane, b, a) for a, b in zip(x, y)]
            plus_ref[r] = shifted(both, d, False)
            minus_ref[r] = shifted(both, d, True)
        return 0

    lax.fori_loop(0, (ROWS + d + PREP - 1) // PREP, prepare, 0)

    weight = w_ref[...]
    bias = b_ref[...]
    away = both_offsets(at_ref[FOLD])
    row0 = at_ref[ROW]

    def row(m, _):
        r = m + HALO
        x = tiles(r)
        taps = [
            mid[r - d],
            plus_ref[r - hi],
            shifted(x, 2 * d, False),
            minus_ref[r - hi],
            mid[r],
            plus_ref[r + lo],
            shifted(x, 2 * d, True),
            minus_ref[r + lo],
            mid[r + d],
        ]
        acc = lax.dot_general(
            weight,
            jnp.concatenate(taps, axis=0),
            (((1,), (0,)), ((), ())),
            preferred_element_type=jnp.float32,
        )
        acc = acc + bias
        if final:
            acc = acc + own_ref[m].astype(jnp.float32)
        else:
            acc = jnp.maximum(acc, 0.0)
        out_ref[m] = jnp.where(away <= threshold(limit_ref, row0 + m), acc, 0.0).astype(jnp.bfloat16)
        return 0

    lax.fori_loop(0, ROWS, row, 0, unroll=UNROLL)
    if final:
        mix(at_ref, limit_ref, out_ref, first_ref, second_ref, edge_ref, other_ref, plus_ref)
    else:
        pack_edges(out_ref, *edges)


def mix(at_ref, limit_ref, summed, first_ref, second_ref, edge_ref, other_ref, rows_ref):
    a = lax.broadcasted_iota(jnp.int32, (COLS, COLS), 0)
    b = lax.broadcasted_iota(jnp.int32, (COLS, COLS), 1)
    turn = (a + b == COLS).astype(jnp.bfloat16)
    lane = lax.broadcasted_iota(jnp.int32, (C, LANES), 1)
    away = both_offsets(at_ref[FOLD])
    row0 = at_ref[ROW]
    edges = [jnp.zeros((C, LANES), jnp.bfloat16)] * 2
    for group in range(ROWS // STACK):
        at = group * STACK
        cells = summed[pl.ds(at, STACK)].reshape(STACK * C, WIDE)
        blocks = cells[:, :COLS], cells[:, COLS:]
        turned = [jnp.dot(x, turn, preferred_element_type=jnp.float32) for x in blocks]
        for i in range(2):
            mean = 0.5 * (blocks[i].astype(jnp.float32) + turned[1 - i])
            for j in range(STACK):
                m = at + j
                part = slice(C * j, C * (j + 1))
                seen = away[:, COLS * i : COLS * (i + 1)] <= threshold(limit_ref, row0 + m)
                rows_ref[m, :, COLS * i : COLS * (i + 1)] = jnp.where(seen, mean[part], 0.0).astype(jnp.bfloat16)
                tile = blocks[i][part, :LANES]
                tile = pltpu.roll(tile, m, axis=1) if m else tile
                edges[i] = jnp.where(lane == m, tile, edges[i])
    swap = at_ref[CORE] == 0
    edge_ref[...] = jnp.where(swap, edges[1], edges[0])
    other_ref[...] = jnp.where(swap, edges[0], edges[1])
    early = at_ref[ORDER] == 0

    @pl.when(early)
    def _():
        first_ref[...] = jnp.swapaxes(rows_ref[pl.ds(0, ROWS), :, :COLS], 0, 1)
        second_ref[...] = jnp.swapaxes(rows_ref[pl.ds(0, ROWS), :, COLS:], 0, 1)

    @pl.when(jnp.logical_not(early))
    def _():
        first_ref[...] = jnp.swapaxes(rows_ref[pl.ds(0, ROWS), :, COLS:], 0, 1)
        second_ref[...] = jnp.swapaxes(rows_ref[pl.ds(0, ROWS), :, :COLS], 0, 1)


def conv(own, at, d, row_limit, cells, halos, weight, bias):
    final = own is not None
    in_specs = [SMEM] * 3 + [ANY] * 7 + [VMEM] * (3 if final else 2)
    args = [at, d, row_limit, cells, *halos, weight, bias] + ([own] if final else [])
    scratch = [pltpu.VMEM((ROWS, C, WIDE), jnp.bfloat16)] if final else []
    out_shape = [shape(C, ROWS, COLS)] * 2 + [shape(C, LANES)] * 2 if final else [shape(ROWS, C, WIDE)] + EDGES
    return pl.pallas_call(
        functools.partial(conv_kernel, final),
        in_specs=in_specs,
        out_specs=[VMEM] * len(out_shape),
        out_shape=out_shape,
        scratch_shapes=scratch
        + [
            pltpu.VMEM((SPAN, C, WIDE), jnp.bfloat16),
            pltpu.VMEM((SPAN, C, LANES), jnp.bfloat16),
            pltpu.VMEM((SPAN, C, LANES), jnp.bfloat16),
            pltpu.VMEM((SPAN, C, WIDE), jnp.bfloat16),
            pltpu.VMEM((SPAN, C, WIDE), jnp.bfloat16),
            pltpu.SemaphoreType.DMA((9,)),
        ],
        compiler_params=PARAMS,
        cost_estimate=cost(25.0 if final else 20.0),
        name="second" if final else "first",
    )(*args)


def flat(weight):
    return jnp.transpose(weight, (1, 0, 2)).reshape(C, 9 * C)


def local(band_map, dilations, row_limit, weight_one, bias_one, weight_two, bias_two):
    at = whereabouts()
    vector = jnp.stack(at)
    early, late = routes(0), routes(1)

    first = enter(0, vector, row_limit, band_map, [])
    second = enter(1, vector, row_limit, band_map, [first])
    first = lax.ppermute(first, AXES, early)
    second = lax.ppermute(second, AXES, late)
    cells, *edges = pack(vector, first, second)
    halos = exchange(at, *edges)
    hidden, *edges = conv(
        None, vector, dilations[:1], row_limit, cells, halos, flat(weight_one), bias_one[:, None]
    )
    halos = exchange(at, *edges)
    first, second, edge, other = conv(
        cells, vector, dilations[1:], row_limit, hidden, halos, flat(weight_two), bias_two[:, None]
    )

    pos, off = lax.axis_index("pos"), lax.axis_index("off")
    here = lambda pairs: functools.reduce(jnp.logical_or, [(pos % 2 == s) & (off == b) for s, b in pairs])
    stays, relayed = here(STAY), here(VIA)
    leave, arrive = [], []
    for to, at_work in early:
        stored, block = to // 8, to % 8
        if (stored % 2, block) in VIA:
            via = device(stored // 2, *VIA[stored % 2, block])
            leave.append((at_work, via))
            arrive.append((via, to))
        elif at_work != to:
            leave.append((at_work, to))
    passed = lax.ppermute(first, AXES, leave)
    direct = lax.ppermute(second, AXES, [(b, a) for a, b in late])
    ended = lax.ppermute(passed, AXES, arrive)

    to_first = lambda core: [(place(s, f), home(s // 2, f + 1)) for s, f in CELLS if s % 2 == core]
    to_second = lambda core: [(place(s, f), home(s // 2, 8 - f)) for s, f in CELLS if s % 2 == core and f]
    edge = lax.ppermute(edge, AXES, to_first(0) + to_second(1))
    other = lax.ppermute(other, AXES, to_second(0) + to_first(1))
    low = off <= 4
    top_edge, bottom_edge = jnp.where(low, edge, other), jnp.where(low, other, edge)

    got = jnp.where(stays, first, jnp.where(relayed, ended, passed))
    top_first = vector[EARLY] == 0
    column = lax.broadcasted_iota(jnp.int32, (1, 1, COLS), 2)

    def whole(cells, edge):
        more = cells.astype(jnp.float32) + 0.5 * edge[:, :ROWS, None].astype(jnp.float32)
        return jnp.where(column == 0, more.astype(jnp.bfloat16), cells)

    return jnp.concatenate(
        [
            whole(jnp.where(top_first, got, direct), top_edge),
            whole(jnp.where(top_first, direct, got), bottom_edge),
        ],
        axis=1,
    )


def solution(mesh):
    in_specs = (P(None, "pos", "off"), P(), P(), P(), P(), P(), P())
    out_specs = P(None, "pos", "off")
    return jax.shard_map(local, mesh=mesh, in_specs=in_specs, out_specs=out_specs, check_vma=False)
```

time: 681 us -> 280 us (0.41)
  the two profiles are of different devices: /device:TPU:8 before, /device:TPU:118 now
where the time goes in v2:
time: 280 us; the launch traced here: 277 us
  waiting for transfers between devices  151 us (54%)
  Pallas kernels  62 us (22%)
  starting transfers between devices  45.1 us (16%)
  local copies, waits for them, and re-layouts  9.81 us (4%)
  other arithmetic  9.18 us (3%)
    ppermute x1, waiting for transfers between devices, local(): passed = lax.ppermute(first, AXES, leave)  56.3 us
    pallas_call x2, Pallas kernels, conv(): pl.pallas_call(functools.partial(conv_kernel, final), in_specs=in_specs,...  48.2 us
    ppermute x12, waiting for transfers between devices, send(): return lax.ppermute(cells, AXES, moves(strip_step, fold_step))  38 us
    ppermute x12, starting transfers between devices, send(): return lax.ppermute(cells, AXES, moves(strip_step, fold_step))  31.5 us
    ppermute x1, waiting for transfers between devices, local(): second = lax.ppermute(second, AXES, late)  20.2 us
    ppermute x1, waiting for transfers between devices, local(): first = lax.ppermute(first, AXES, early)  19.6 us
    ppermute x1, waiting for transfers between devices, local(): other = lax.ppermute(other, AXES, to_second(0) + to_first(1))  16.9 us
    pallas_call x2, Pallas kernels, enter(): pl.pallas_call(functools.partial(enter_kernel, turn), grid_spec=pltpu.Pre...  7.87 us
  transfers between devices with their start and end apart: 19, of which 10 were waited for; matrix products, arithmetic and copies ran while one was open for 4% of the time, Pallas kernels for 0%

profile of v2, /device:TPU:118, one launch (start us, length us, event | category | flops | bytes accessed | tf_op | source)
XLA Modules:
  0.0 277.5 jit_solution(9452623436225260275)
XLA Ops:
  0.0 0.7 stack.31.at_ref
  0.7 3.9 %enter.2.rest_0_ = bf16[72,48,256]{2,1,0:T(8,128)(2,1)} custom-call(s32[7]{0:T(128)} %stack.31.at_ref, s32[2304]{0:T(1024)} %limit_ref.7, bf16[48,144,256]{2,1,0:T(8,128)(2,1)} %x_ref.3), custom_call_target="tpu_custom_call" | custom-call | bytes 14760000 | tf_op jit(solution)/shard_map/enter/pallas_call | solution.py:119
  4.5 4.0 %enter.3 = bf16[72,48,256]{2,1,0:T(8,128)(2,1)} custom-call(s32[7]{0:T(128)} %stack.31.at_ref, s32[2304]{0:T(1024)} %limit_ref.7, bf16[48,144,256]{2,1,0:T(8,128)(2,1)} %x_ref.3, bf16[72,48,256]{2,1,0:T(8,128)(2,1)} %enter.2.rest_0_), custom_call_target="tpu_custom_call" | custom-call | bytes 14760000 | tf_op jit(solution)/shard_map/enter/pallas_call | solution.py:119
  8.6 0.0 collective-permute-start.1
  8.6 1.9 collective-permute-start
  10.5 20.2 %collective-permute-done.1.late_ref = bf16[72,48,256]{2,1,0:T(8,128)(2,1)S(1)} collective-permute-done((bf16[72,48,256]{2,1,0:T(8,128)(2,1)}, bf16[72,48,256]{2,1,0:T(8,128)(2,1)S(1)}, u32[]{:S(2)}, u32[]{:S(2)}) %collective-permute-start.1) | collective-permute-done | bytes 1769504 | tf_op jit(solution)/shard_map/ppermute | solution.py:370
  30.7 19.6 %collective-permute-done.early_ref = bf16[72,48,256]{2,1,0:T(8,128)(2,1)S(1)} collective-permute-done((bf16[72,48,256]{2,1,0:T(8,128)(2,1)S(1)}, bf16[72,48,256]{2,1,0:T(8,128)(2,1)S(1)}, u32[]{:S(2)}, u32[]{:S(2)}) %collective-permute-start) | collective-permute-done | bytes 1769504 | tf_op jit(solution)/shard_map/ppermute | solution.py:369
  50.3 1.2 copy-done.6
  51.6 5.9 %pack.1 = (bf16[72,48,512]{2,1,0:T(8,128)(2,1)}, bf16[72,48,128]{2,1,0:T(8,128)(2,1)}, bf16[72,48,128]{2,1,0:T(8,128)(2,1)}, bf16[32,48,512]{2,1,0:T(8,128)(2,1)}, bf16[32,48,512]{2,1,0:T(8,128)(2,1)}) custom-call(s32[7]{0:T(128)} %stack.31.at_ref, bf16[72,48,256]{2,1,0:T(8,128)(2,1)} %copy-done.6, bf16[72,48,256]{2,1,0:T(8,128)(2,1)} %copy-done.5), custom_call_target="tpu_custom_call" | custom-call | bytes 14760000 | tf_op jit(solution)/shard_map/pack/pallas_call | solution.py:163
  57.5 2.9 %collective-permute-start.3 = (bf16[72,48,128]{2,1,0:T(8,128)(2,1)}, bf16[72,48,128]{2,1,0:T(8,128)(2,1)S(1)}, u32[]{:S(2)}, u32[]{:S(2)}) collective-permute-start(bf16[72,48,128]{2,1,0:T(8,128)(2,1)} %get-tuple-element.21), channel_id=1, source_target_pairs={{6,0},{4,6},{2,4},{14,8},{12,14},{10,12},{7,1},{5,7},{3,5},{15,9},... | collective-permute-start | bytes 2654216 | tf_op jit(solution)/shard_map/ppermute | solution.py:175
  60.3 3.0 %collective-permute-start.2 = (bf16[72,48,128]{2,1,0:T(8,128)(2,1)}, bf16[72,48,128]{2,1,0:T(8,128)(2,1)S(1)}, u32[]{:S(2)}, u32[]{:S(2)}) collective-permute-start(bf16[72,48,128]{2,1,0:T(8,128)(2,1)} %get-tuple-element.20), channel_id=1, source_target_pairs={{0,6},{6,4},{4,2},{8,14},{14,12},{12,10},{1,7},{7,5},{5,3},{9,15},... | collective-permute-start | bytes 2654216 | tf_op jit(solution)/shard_map/ppermute | solution.py:175
  63.3 1.9 collective-permute-start.4
  65.2 3.7 %collective-permute-start.5 = (bf16[32,48,512]{2,1,0:T(8,128)(2,1)}, bf16[32,48,512]{2,1,0:T(8,128)(2,1)}, u32[]{:S(2)}, u32[]{:S(2)}) collective-permute-start(bf16[32,48,512]{2,1,0:T(8,128)(2,1)} %get-tuple-element.23), channel_id=1, source_target_pairs={{8,0},{14,6},{12,4},{10,2},{1,8},{7,14},{5,12},{3,10},{9,1},{15,7}... | collective-permute-start | bytes 4718600 | tf_op jit(solution)/shard_map/ppermute | solution.py:175
  69.0 11.6 %collective-permute-done.3 = bf16[72,48,128]{2,1,0:T(8,128)(2,1)S(1)} collective-permute-done((bf16[72,48,128]{2,1,0:T(8,128)(2,1)}, bf16[72,48,128]{2,1,0:T(8,128)(2,1)S(1)}, u32[]{:S(2)}, u32[]{:S(2)}) %collective-permute-start.3) | collective-permute-done | bytes 884768 | tf_op jit(solution)/shard_map/ppermute | solution.py:175
  80.6 0.1 broadcast_select_fusion.1.refs_1_
  80.7 0.0 copy-start.10
  80.7 0.0 copy-start.9
  80.8 3.3 %collective-permute-done.2.refs_0_ = bf16[72,48,128]{2,1,0:T(8,128)(2,1)S(1)} collective-permute-done((bf16[72,48,128]{2,1,0:T(8,128)(2,1)}, bf16[72,48,128]{2,1,0:T(8,128)(2,1)S(1)}, u32[]{:S(2)}, u32[]{:S(2)}) %collective-permute-start.2) | collective-permute-done | bytes 884768 | tf_op jit(solution)/shard_map/ppermute | solution.py:175
  84.1 0.9 pad_maximum_fusion.2
  85.0 1.9 collective-permute-start.7
  87.0 0.8 pad_maximum_fusion.1
  87.8 2.4 collective-permute-start.6
  90.2 1.0 copy.12
  91.2 0.7 copy.13.refs_6_
  91.9 0.7 copy.14.refs_7_
  92.6 0.6 fusion.6
  93.2 0.0 collective-permute-done.7.refs_5_
  93.2 4.0 %collective-permute-done.6.refs_4_ = bf16[32,48,128]{2,1,0:T(8,128)(2,1)} collective-permute-done((bf16[32,48,128]{2,1,0:T(8,128)(2,1)}, bf16[32,48,128]{2,1,0:T(8,128)(2,1)}, u32[]{:S(2)}, u32[]{:S(2)}) %collective-permute-start.6) | collective-permute-done | bytes 393248 | tf_op jit(solution)/shard_map/ppermute | solution.py:175
  97.2 1.2 copy-done.8
  98.4 23.3 %first.1 = (bf16[72,48,512]{2,1,0:T(8,128)(2,1)}, bf16[72,48,128]{2,1,0:T(8,128)(2,1)}, bf16[72,48,128]{2,1,0:T(8,128)(2,1)}, bf16[32,48,512]{2,1,0:T(8,128)(2,1)}, bf16[32,48,512]{2,1,0:T(8,128)(2,1)}) custom-call(s32[7]{0:T(128)} %stack.31.at_ref, s32[1]{0:T(128)} %get-tuple-element.45.d_ref, s32[2304]{0:T(1024)} %limit_ref.7, ...), custom_call_target="tpu_custom_call" | custom-call | bytes 73800000 | tf_op jit(solution)/shard_map/first/pallas_call | solution.py:338
  121.7 1.9 collective-permute-start.9
  123.7 3.9 %collective-permute-start.8 = (bf16[72,48,128]{2,1,0:T(8,128)(2,1)}, bf16[72,48,128]{2,1,0:T(8,128)(2,1)S(1)}, u32[]{:S(2)}, u32[]{:S(2)}) collective-permute-start(bf16[72,48,128]{2,1,0:T(8,128)(2,1)} %get-tuple-element.25), channel_id=1, source_target_pairs={{0,6},{6,4},{4,2},{8,14},{14,12},{12,10},{1,7},{7,5},{5,3},{9,15},... | collective-permute-start | bytes 2654216 | tf_op jit(solution)/shard_map/ppermute | solution.py:175
  127.6 1.9 collective-permute-start.10
  129.5 3.6 %collective-permute-start.11 = (bf16[32,48,512]{2,1,0:T(8,128)(2,1)}, bf16[32,48,512]{2,1,0:T(8,128)(2,1)}, u32[]{:S(2)}, u32[]{:S(2)}) collective-permute-start(bf16[32,48,512]{2,1,0:T(8,128)(2,1)} %get-tuple-element.28), channel_id=1, source_target_pairs={{8,0},{14,6},{12,4},{10,2},{1,8},{7,14},{5,12},{3,10},{9,1},{15,7}... | collective-permute-start | bytes 4718600 | tf_op jit(solution)/shard_map/ppermute | solution.py:175
  133.2 11.5 %collective-permute-done.9 = bf16[72,48,128]{2,1,0:T(8,128)(2,1)S(1)} collective-permute-done((bf16[72,48,128]{2,1,0:T(8,128)(2,1)}, bf16[72,48,128]{2,1,0:T(8,128)(2,1)S(1)}, u32[]{:S(2)}, u32[]{:S(2)}) %collective-permute-start.9) | collective-permute-done | bytes 884768 | tf_op jit(solution)/shard_map/ppermute | solution.py:175
  144.7 0.1 broadcast_select_fusion.refs_1_
  144.8 0.0 copy-start.11
  144.8 3.0 %collective-permute-done.8.refs_0_ = bf16[72,48,128]{2,1,0:T(8,128)(2,1)S(1)} collective-permute-done((bf16[72,48,128]{2,1,0:T(8,128)(2,1)}, bf16[72,48,128]{2,1,0:T(8,128)(2,1)S(1)}, u32[]{:S(2)}, u32[]{:S(2)}) %collective-permute-start.8) | collective-permute-done | bytes 884768 | tf_op jit(solution)/shard_map/ppermute | solution.py:175
  147.9 0.9 pad_maximum_fusion.4
  148.7 1.9 collective-permute-start.13
  150.6 0.8 pad_maximum_fusion.3
  151.4 2.4 collective-permute-start.12
  153.8 1.0 copy.15
  154.9 0.7 copy.16.refs_6_
  155.6 0.7 copy.17.refs_7_
  156.3 0.0 collective-permute-done.13.refs_5_
  156.3 4.6 %collective-permute-done.12.refs_4_ = bf16[32,48,128]{2,1,0:T(8,128)(2,1)} collective-permute-done((bf16[32,48,128]{2,1,0:T(8,128)(2,1)}, bf16[32,48,128]{2,1,0:T(8,128)(2,1)}, u32[]{:S(2)}, u32[]{:S(2)}) %collective-permute-start.12) | collective-permute-done | bytes 393248 | tf_op jit(solution)/shard_map/ppermute | solution.py:175
  160.8 0.0 collective-permute-done.10.refs_2_
  160.9 1.1 copy-done.7
  162.0 24.9 %second.1 = (bf16[48,72,256]{2,1,0:T(8,128)(2,1)}, bf16[48,72,256]{2,1,0:T(8,128)(2,1)}, bf16[48,128]{1,0:T(8,128)(2,1)}, bf16[48,128]{1,0:T(8,128)(2,1)}) custom-call(s32[7]{0:T(128)} %stack.31.at_ref, s32[1]{0:T(128)} %get-tuple-element.46.d_ref, s32[2304]{0:T(1024)} %limit_ref.7, bf16[72,48,512]{2,1,0:T(8,128)(2,1)} %get-tuple-element.24.cells, ...), custom_call_target="tpu_custom_call" | custom-call | bytes 92250000 | tf_op jit(solution)/shard_map/second/pallas_call | solution.py:338
  186.9 3.8 %collective-permute-start.14 = (bf16[48,72,256]{2,1,0:T(8,128)(2,1)}, bf16[48,72,256]{2,1,0:T(8,128)(2,1)S(1)}, u32[]{:S(2)}, u32[]{:S(2)}) collective-permute-start(bf16[48,72,256]{2,1,0:T(8,128)(2,1)} %get-tuple-element.29), channel_id=1, source_target_pairs={{4,2},{2,3},{8,6},{14,0},{12,5},{10,4},{1,8},{7,9},{5,11},{3,13},{... | collective-permute-start | bytes 5308424 | tf_op jit(solution)/shard_map/ppermute | solution.py:393
  190.7 0.1 collective-permute-start.16
  190.8 56.3 %collective-permute-done.14 = bf16[48,72,256]{2,1,0:T(8,128)(2,1)S(1)} collective-permute-done((bf16[48,72,256]{2,1,0:T(8,128)(2,1)}, bf16[48,72,256]{2,1,0:T(8,128)(2,1)S(1)}, u32[]{:S(2)}, u32[]{:S(2)}) %collective-permute-start.14) | collective-permute-done | bytes 1769504 | tf_op jit(solution)/shard_map/ppermute | solution.py:393
  247.1 1.3 collective-permute-start.15
  248.4 2.6 collective-permute-start.17
  251.0 3.9 %collective-permute-start.18 = (bf16[48,128]{1,0:T(8,128)(2,1)}, bf16[48,128]{1,0:T(8,128)(2,1)}, u32[]{:S(2)}, u32[]{:S(2)}) collective-permute-start(bf16[48,128]{1,0:T(8,128)(2,1)} %get-tuple-element.32), channel_id=1, source_target_pairs={{6,7},{4,6},{2,5},{7,15},{5,14},{3,13},{22,23},{20,22},{18,21},{23... | collective-permute-start | bytes 36872 | tf_op jit(solution)/shard_map/ppermute | solution.py:400
  255.0 0.0 collective-permute-done.17
  255.0 16.9 %collective-permute-done.18 = bf16[48,128]{1,0:T(8,128)(2,1)} collective-permute-done((bf16[48,128]{1,0:T(8,128)(2,1)}, bf16[48,128]{1,0:T(8,128)(2,1)}, u32[]{:S(2)}, u32[]{:S(2)}) %collective-permute-start.18) | collective-permute-done | bytes 12320 | tf_op jit(solution)/shard_map/ppermute | solution.py:400
  271.9 0.7 convert_multiply_fusion.1
  272.6 0.0 collective-permute-done.16
  272.6 0.0 collective-permute-done.15
  272.6 2.0 fusion
  274.7 0.7 fusion.1
  275.4 2.0 pad_maximum_fusion
  (26 shorter events, 0.2 us)
Async XLA Ops:
  4.5 4.0 %copy-start = (bf16[72,48,256]{2,1,0:T(8,128)(2,1)S(1)}, bf16[72,48,256]{2,1,0:T(8,128)(2,1)}, u32[]{:S(2)}) copy-start(bf16[72,48,256]{2,1,0:T(8,128)(2,1)} %enter.2.rest_0_) | copy-start | bytes 5308420
  8.6 22.2 %collective-permute-start.1 = (bf16[72,48,256]{2,1,0:T(8,128)(2,1)}, bf16[72,48,256]{2,1,0:T(8,128)(2,1)S(1)}, u32[]{:S(2)}, u32[]{:S(2)}) collective-permute-start(bf16[72,48,256]{2,1,0:T(8,128)(2,1)} %enter.3), channel_id=1, source_target_pairs={{7,0},{1,6},{5,4},{4,2},{0,8},{6,14},{2,12},{3,10},{15,1},{14,7},{... | collective-permute-start | bytes 5308424 | tf_op jit(solution)/shard_map/ppermute | solution.py:370
  8.6 41.8 %collective-permute-start = (bf16[72,48,256]{2,1,0:T(8,128)(2,1)S(1)}, bf16[72,48,256]{2,1,0:T(8,128)(2,1)S(1)}, u32[]{:S(2)}, u32[]{:S(2)}) collective-permute-start(bf16[72,48,256]{2,1,0:T(8,128)(2,1)S(1)} %copy-done), channel_id=1, source_target_pairs={{0,0},{6,6},{2,4},{3,2},{7,8},{1,14},{5,12},{4,10},{8,1},{9,7},{10... | collective-permute-start | bytes 5308424 | tf_op jit(solution)/shard_map/ppermute | solution.py:369
  30.7 19.6 %copy-start.5 = (bf16[72,48,256]{2,1,0:T(8,128)(2,1)}, bf16[72,48,256]{2,1,0:T(8,128)(2,1)S(1)}, u32[]{:S(2)}) copy-start(bf16[72,48,256]{2,1,0:T(8,128)(2,1)S(1)} %collective-permute-done.1.late_ref) | copy-start | bytes 5308420
  50.3 1.2 copy-start.6
  57.5 23.1 %collective-permute-start.3 = (bf16[72,48,128]{2,1,0:T(8,128)(2,1)}, bf16[72,48,128]{2,1,0:T(8,128)(2,1)S(1)}, u32[]{:S(2)}, u32[]{:S(2)}) collective-permute-start(bf16[72,48,128]{2,1,0:T(8,128)(2,1)} %get-tuple-element.21), channel_id=1, source_target_pairs={{6,0},{4,6},{2,4},{14,8},{12,14},{10,12},{7,1},{5,7},{3,5},{15,9},... | collective-permute-start | bytes 2654216 | tf_op jit(solution)/shard_map/ppermute | solution.py:175
  60.3 23.7 %collective-permute-start.2 = (bf16[72,48,128]{2,1,0:T(8,128)(2,1)}, bf16[72,48,128]{2,1,0:T(8,128)(2,1)S(1)}, u32[]{:S(2)}, u32[]{:S(2)}) collective-permute-start(bf16[72,48,128]{2,1,0:T(8,128)(2,1)} %get-tuple-element.20), channel_id=1, source_target_pairs={{0,6},{6,4},{4,2},{8,14},{14,12},{12,10},{1,7},{7,5},{5,3},{9,15},... | collective-permute-start | bytes 2654216 | tf_op jit(solution)/shard_map/ppermute | solution.py:175
  63.3 33.9 %collective-permute-start.4 = (bf16[32,48,512]{2,1,0:T(8,128)(2,1)}, bf16[32,48,512]{2,1,0:T(8,128)(2,1)S(1)}, u32[]{:S(2)}, u32[]{:S(2)}) collective-permute-start(bf16[32,48,512]{2,1,0:T(8,128)(2,1)} %get-tuple-element.22), channel_id=1, source_target_pairs={{0,8},{6,14},{4,12},{2,10},{8,1},{14,7},{12,5},{10,3},{1,9},{7,15}... | collective-permute-start | bytes 4718600 | tf_op jit(solution)/shard_map/ppermute | solution.py:175
  65.2 31.9 %collective-permute-start.5 = (bf16[32,48,512]{2,1,0:T(8,128)(2,1)}, bf16[32,48,512]{2,1,0:T(8,128)(2,1)}, u32[]{:S(2)}, u32[]{:S(2)}) collective-permute-start(bf16[32,48,512]{2,1,0:T(8,128)(2,1)} %get-tuple-element.23), channel_id=1, source_target_pairs={{8,0},{14,6},{12,4},{10,2},{1,8},{7,14},{5,12},{3,10},{9,1},{15,7}... | collective-permute-start | bytes 4718600 | tf_op jit(solution)/shard_map/ppermute | solution.py:175
  80.7 11.2 %copy-start.2 = (bf16[72,48,128]{2,1,0:T(8,128)(2,1)}, bf16[72,48,128]{2,1,0:T(8,128)(2,1)S(1)}, u32[]{:S(2)}) copy-start(bf16[72,48,128]{2,1,0:T(8,128)(2,1)S(1)} %broadcast_select_fusion.1.refs_1_) | copy-start | bytes 2654212
  80.7 11.2 %copy-start.10 = (f32[48]{0:T(128)S(1)}, f32[48]{0:T(128)}, u32[]{:S(2)}) copy-start(f32[48]{0:T(128)} %param.11) | copy-start | bytes 580
  80.7 11.9 %copy-start.9 = (s32[2]{0:T(128)S(1)}, s32[2]{0:T(128)}, u32[]{:S(2)}) copy-start(s32[2]{0:T(128)} %param.8) | copy-start | bytes 28
  84.1 13.1 %copy-start.4 = (bf16[72,48,128]{2,1,0:T(8,128)(2,1)}, bf16[72,48,128]{2,1,0:T(8,128)(2,1)S(1)}, u32[]{:S(2)}) copy-start(bf16[72,48,128]{2,1,0:T(8,128)(2,1)S(1)} %collective-permute-done.2.refs_0_) | copy-start | bytes 2654212
  85.0 8.2 %collective-permute-start.7 = (bf16[32,48,128]{2,1,0:T(8,128)(2,1)}, bf16[32,48,128]{2,1,0:T(8,128)(2,1)}, u32[]{:S(2)}, u32[]{:S(2)}) collective-permute-start(bf16[32,48,128]{2,1,0:T(8,128)(2,1)} %pad_maximum_fusion.2), channel_id=1, source_target_pairs={{8,0},{14,6},{12,4},{10,2},{1,8},{7,14},{5,12},{3,10},{9,1},{15,7}... | collective-permute-start | bytes 1179656 | tf_op jit(solution)/shard_map/ppermute | solution.py:175
  87.8 9.4 %collective-permute-start.6 = (bf16[32,48,128]{2,1,0:T(8,128)(2,1)}, bf16[32,48,128]{2,1,0:T(8,128)(2,1)}, u32[]{:S(2)}, u32[]{:S(2)}) collective-permute-start(bf16[32,48,128]{2,1,0:T(8,128)(2,1)} %pad_maximum_fusion.1), channel_id=1, source_target_pairs={{0,8},{6,14},{4,12},{2,10},{8,1},{14,7},{12,5},{10,3},{1,9},{7,15}... | collective-permute-start | bytes 1179656 | tf_op jit(solution)/shard_map/ppermute | solution.py:175
  97.2 1.2 copy-start.8
  121.7 23.0 %collective-permute-start.9 = (bf16[72,48,128]{2,1,0:T(8,128)(2,1)}, bf16[72,48,128]{2,1,0:T(8,128)(2,1)S(1)}, u32[]{:S(2)}, u32[]{:S(2)}) collective-permute-start(bf16[72,48,128]{2,1,0:T(8,128)(2,1)} %get-tuple-element.26), channel_id=1, source_target_pairs={{6,0},{4,6},{2,4},{14,8},{12,14},{10,12},{7,1},{5,7},{3,5},{15,9},... | collective-permute-start | bytes 2654216 | tf_op jit(solution)/shard_map/ppermute | solution.py:175
  123.7 24.2 %collective-permute-start.8 = (bf16[72,48,128]{2,1,0:T(8,128)(2,1)}, bf16[72,48,128]{2,1,0:T(8,128)(2,1)S(1)}, u32[]{:S(2)}, u32[]{:S(2)}) collective-permute-start(bf16[72,48,128]{2,1,0:T(8,128)(2,1)} %get-tuple-element.25), channel_id=1, source_target_pairs={{0,6},{6,4},{4,2},{8,14},{14,12},{12,10},{1,7},{7,5},{5,3},{9,15},... | collective-permute-start | bytes 2654216 | tf_op jit(solution)/shard_map/ppermute | solution.py:175
  127.6 33.3 %collective-permute-start.10 = (bf16[32,48,512]{2,1,0:T(8,128)(2,1)}, bf16[32,48,512]{2,1,0:T(8,128)(2,1)S(1)}, u32[]{:S(2)}, u32[]{:S(2)}) collective-permute-start(bf16[32,48,512]{2,1,0:T(8,128)(2,1)} %get-tuple-element.27), channel_id=1, source_target_pairs={{0,8},{6,14},{4,12},{2,10},{8,1},{14,7},{12,5},{10,3},{1,9},{7,15}... | collective-permute-start | bytes 4718600 | tf_op jit(solution)/shard_map/ppermute | solution.py:175
  129.5 31.3 %collective-permute-start.11 = (bf16[32,48,512]{2,1,0:T(8,128)(2,1)}, bf16[32,48,512]{2,1,0:T(8,128)(2,1)}, u32[]{:S(2)}, u32[]{:S(2)}) collective-permute-start(bf16[32,48,512]{2,1,0:T(8,128)(2,1)} %get-tuple-element.28), channel_id=1, source_target_pairs={{8,0},{14,6},{12,4},{10,2},{1,8},{7,14},{5,12},{3,10},{9,1},{15,7}... | collective-permute-start | bytes 4718600 | tf_op jit(solution)/shard_map/ppermute | solution.py:175
  144.8 10.8 %copy-start.1 = (bf16[72,48,128]{2,1,0:T(8,128)(2,1)}, bf16[72,48,128]{2,1,0:T(8,128)(2,1)S(1)}, u32[]{:S(2)}) copy-start(bf16[72,48,128]{2,1,0:T(8,128)(2,1)S(1)} %broadcast_select_fusion.refs_1_) | copy-start | bytes 2654212
  144.8 10.8 %copy-start.11 = (f32[48]{0:T(128)S(1)}, f32[48]{0:T(128)}, u32[]{:S(2)}) copy-start(f32[48]{0:T(128)} %param.13) | copy-start | bytes 580
  147.8 13.0 %copy-start.3 = (bf16[72,48,128]{2,1,0:T(8,128)(2,1)}, bf16[72,48,128]{2,1,0:T(8,128)(2,1)S(1)}, u32[]{:S(2)}) copy-start(bf16[72,48,128]{2,1,0:T(8,128)(2,1)S(1)} %collective-permute-done.8.refs_0_) | copy-start | bytes 2654212
  148.7 7.6 %collective-permute-start.13 = (bf16[32,48,128]{2,1,0:T(8,128)(2,1)}, bf16[32,48,128]{2,1,0:T(8,128)(2,1)}, u32[]{:S(2)}, u32[]{:S(2)}) collective-permute-start(bf16[32,48,128]{2,1,0:T(8,128)(2,1)} %pad_maximum_fusion.4), channel_id=1, source_target_pairs={{8,0},{14,6},{12,4},{10,2},{1,8},{7,14},{5,12},{3,10},{9,1},{15,7}... | collective-permute-start | bytes 1179656 | tf_op jit(solution)/shard_map/ppermute | solution.py:175
  151.4 9.4 %collective-permute-start.12 = (bf16[32,48,128]{2,1,0:T(8,128)(2,1)}, bf16[32,48,128]{2,1,0:T(8,128)(2,1)}, u32[]{:S(2)}, u32[]{:S(2)}) collective-permute-start(bf16[32,48,128]{2,1,0:T(8,128)(2,1)} %pad_maximum_fusion.3), channel_id=1, source_target_pairs={{0,8},{6,14},{4,12},{2,10},{8,1},{14,7},{12,5},{10,3},{1,9},{7,15}... | collective-permute-start | bytes 1179656 | tf_op jit(solution)/shard_map/ppermute | solution.py:175
  160.9 1.2 copy-start.7
  186.9 60.2 %collective-permute-start.14 = (bf16[48,72,256]{2,1,0:T(8,128)(2,1)}, bf16[48,72,256]{2,1,0:T(8,128)(2,1)S(1)}, u32[]{:S(2)}, u32[]{:S(2)}) collective-permute-start(bf16[48,72,256]{2,1,0:T(8,128)(2,1)} %get-tuple-element.29), channel_id=1, source_target_pairs={{4,2},{2,3},{8,6},{14,0},{12,5},{10,4},{1,8},{7,9},{5,11},{3,13},{... | collective-permute-start | bytes 5308424 | tf_op jit(solution)/shard_map/ppermute | solution.py:393
  190.7 81.9 %collective-permute-start.16 = (bf16[48,72,256]{2,1,0:T(8,128)(2,1)}, bf16[48,72,256]{2,1,0:T(8,128)(2,1)S(1)}, u32[]{:S(2)}, u32[]{:S(2)}) collective-permute-start(bf16[48,72,256]{2,1,0:T(8,128)(2,1)} %get-tuple-element.30), channel_id=1, source_target_pairs={{0,7},{6,1},{4,5},{2,4},{8,0},{14,6},{12,2},{10,3},{1,15},{7,14},{... | collective-permute-start | bytes 5308424 | tf_op jit(solution)/shard_map/ppermute | solution.py:394
  247.1 25.5 %collective-permute-start.15 = (bf16[48,72,256]{2,1,0:T(8,128)(2,1)S(1)}, bf16[48,72,256]{2,1,0:T(8,128)(2,1)}, u32[]{:S(2)}, u32[]{:S(2)}) collective-permute-start(bf16[48,72,256]{2,1,0:T(8,128)(2,1)S(1)} %collective-permute-done.14), channel_id=1, source_target_pairs={{6,7},{0,1},{11,10},{13,12},{22,23},{16,17},{27,26},{29,28},{38,39... | collective-permute-start | bytes 5308424 | tf_op jit(solution)/shard_map/ppermute | solution.py:395
  248.4 6.6 %collective-permute-start.17 = (bf16[48,128]{1,0:T(8,128)(2,1)}, bf16[48,128]{1,0:T(8,128)(2,1)S(1)}, u32[]{:S(2)}, u32[]{:S(2)}) collective-permute-start(bf16[48,128]{1,0:T(8,128)(2,1)} %get-tuple-element.31), channel_id=1, source_target_pairs={{0,1},{6,2},{4,3},{2,4},{1,9},{7,10},{5,11},{3,12},{16,17},{22,18}... | collective-permute-start | bytes 36872 | tf_op jit(solution)/shard_map/ppermute | solution.py:399
  251.0 20.9 %collective-permute-start.18 = (bf16[48,128]{1,0:T(8,128)(2,1)}, bf16[48,128]{1,0:T(8,128)(2,1)}, u32[]{:S(2)}, u32[]{:S(2)}) collective-permute-start(bf16[48,128]{1,0:T(8,128)(2,1)} %get-tuple-element.32), channel_id=1, source_target_pairs={{6,7},{4,6},{2,5},{7,15},{5,14},{3,13},{22,23},{20,22},{18,21},{23... | collective-permute-start | bytes 36872 | tf_op jit(solution)/shard_map/ppermute | solution.py:400

commit v3 on v2

v3 whole, which is shorter than its diff:
```python
import functools

import jax
import jax.numpy as jnp
from jax import lax
from jax.experimental import pallas as pl
from jax.experimental.pallas import tpu as pltpu
from jax.sharding import PartitionSpec as P

BAND = 1024
DMAX = 32
C = 48
ROWS = 72
COLS = 256
WIDE = 2 * COLS
LANES = 128
HALO = DMAX
CORNER = DMAX // 2
CHUNK = 24
PARTS = ((0, 24), (24, 48))
PREP = 8
UNROLL = 8
STACK = 8
AXES = ("pos", "off")

SMEM = pl.BlockSpec(memory_space=pltpu.SMEM)
VMEM = pl.BlockSpec(memory_space=pltpu.VMEM)
ANY = pl.BlockSpec(memory_space=pl.ANY)
HBM = pl.BlockSpec(memory_space=pltpu.HBM)
PARAMS = pltpu.CompilerParams(vmem_limit_bytes=63 * 2**20)


def device(pair, x, z, core):
    return (2 * pair + core) * 8 + 2 * z + x


def home(stored, block):
    return device(stored // 2, block % 2, block // 2, stored % 2)


def place(strip, fold):
    stored = strip // 2
    return device(stored // 2, stored % 2, (4 - fold) % 4, strip % 2)


def lead(stored, fold):
    return (fold == 1) & (stored % 2 == 0) | (fold == 3) & (stored % 2 == 1)


CELLS = [(strip, fold) for strip in range(32) for fold in range(4)]


def routes(turn):
    out = []
    for strip, fold in CELLS:
        core, stored = strip % 2, strip // 2
        first = (core == int(lead(stored, fold))) == (turn == 0)
        out.append((home(stored, fold if first else 7 - fold), place(strip, fold)))
    return out


VIA = {(0, 1): (0, 0, 0), (0, 7): (0, 3, 0), (1, 2): (1, 1, 1), (1, 4): (1, 2, 1)}
STAY = ((0, 0), (0, 6), (1, 3), (1, 5))


def moves(strip_step, fold_step):
    return [
        (place(s, f), place(s + strip_step, f + fold_step))
        for s, f in CELLS
        if 0 <= s + strip_step < 32 and 0 <= f + fold_step < 4
    ]


def whereabouts():
    pos, off = lax.axis_index("pos"), lax.axis_index("off")
    fold = jnp.minimum(off, 7 - off)
    early = jnp.where(off < 4, 0, 1) ^ lead(pos, fold).astype(jnp.int32)
    stored = 2 * (pos // 2) + off % 2
    core = pos % 2
    work = (4 - off // 2) % 4
    order = core ^ lead(stored, work).astype(jnp.int32)
    values = (pos * 2 * ROWS, off, early, stored * 2 * ROWS + core * ROWS, work, order, core)
    return [v.astype(jnp.int32) for v in values]


STORED_ROW, STORED_BLOCK, EARLY, ROW, FOLD, ORDER, CORE = range(7)


def threshold(limit_ref, row):
    last = limit_ref.shape[0] - 1
    return jnp.minimum(limit_ref[row], jnp.minimum(2 * row + 1, 2 * last - 2 * row))


def offsets(block, dims):
    return jnp.abs(lax.broadcasted_iota(jnp.int32, dims, len(dims) - 1) + (block * COLS - BAND))


def both_offsets(fold):
    return jnp.concatenate([offsets(fold, (C, COLS)), offsets(7 - fold, (C, COLS))], axis=1)


def shape(*dims):
    return jax.ShapeDtypeStruct(dims, jnp.bfloat16)


def enter_kernel(turn, at_ref, limit_ref, x_ref, out_ref):
    x = jnp.swapaxes(x_ref[...], 0, 1)
    away = offsets(at_ref[STORED_BLOCK], (C, COLS))
    row0 = at_ref[STORED_ROW] + (at_ref[EARLY] ^ turn) * ROWS
    for i in range(ROWS):
        seen = away <= threshold(limit_ref, row0 + i)
        out_ref[i] = jnp.where(seen, x[i], jnp.zeros((), jnp.bfloat16))


def enter(turn, at, row_limit, band_map):
    return pl.pallas_call(
        functools.partial(enter_kernel, turn),
        grid_spec=pltpu.PrefetchScalarGridSpec(
            num_scalar_prefetch=1,
            grid=(1,),
            in_specs=[SMEM, pl.BlockSpec((C, ROWS, COLS), lambda i, at_ref: (0, at_ref[EARLY] ^ turn, 0))],
            out_specs=pl.BlockSpec((ROWS, C, COLS), lambda i, at_ref: (0, 0, 0)),
        ),
        out_shape=shape(ROWS, C, COLS),
        compiler_params=PARAMS,
        name="enter",
    )(at, row_limit, band_map)


EDGES = [shape(ROWS, C, LANES)] * 2 + [shape(HALO, C, WIDE)] * 2


def edge_copies(cells, first, count, top, bottom):
    out = []
    for target, at in ((top, 0), (bottom, ROWS - HALO)):
        low, high = max(first, at), min(first + count, at + HALO)
        if low < high:
            out.append((cells.at[pl.ds(low - first, high - low)], target.at[pl.ds(low - at, high - low)]))
    return out


def inward_outward(cells, lane):
    return (
        jnp.where(lane < 64, cells[:, 2 * LANES : 3 * LANES], cells[:, LANES : 2 * LANES]),
        jnp.where(lane < 64, cells[:, :LANES], cells[:, 3 * LANES :]),
    )


def pack_kernel(at_ref, early_ref, late_ref, *refs):
    out_ref, inward, outward, top, bottom, blocks, into, back, sems = refs[-9:]
    lane = lax.broadcasted_iota(jnp.int32, (C, LANES), 1)
    runs = [pl.ds(i, CHUNK) for i in range(0, ROWS, CHUNK)]

    def work(first, second):
        n = 0

        def copy(src, dst):
            nonlocal n
            n += 1
            made = pltpu.make_async_copy(src, dst, sems.at[n - 1])
            made.start()
            return made

        here = [[copy(x.at[run], blocks.at[i, run]) for i, x in enumerate((first, second))] for run in runs]
        sent = []
        for at, run, loads in zip(range(0, ROWS, CHUNK), runs, here):
            for load in loads:
                load.wait()
            for i in range(at, at + CHUNK):
                a, b = blocks[0, i], blocks[1, i]
                into[i] = jnp.where(lane < 64, b[:, :LANES], a[:, LANES:])
                back[i] = jnp.where(lane < 64, a[:, :LANES], b[:, LANES:])
            sent += [copy(into.at[run], inward.at[run]), copy(back.at[run], outward.at[run])]
            for i in range(2):
                lanes = pl.ds(i * COLS, COLS)
                pairs = [(blocks.at[i, run], out_ref.at[run, :, lanes])]
                for src, dst in edge_copies(blocks.at[i, run], at, CHUNK, top, bottom):
                    pairs.append((src, dst.at[:, :, lanes]))
                sent += [copy(src, dst) for src, dst in pairs]
        for done in sent:
            done.wait()

    @pl.when(at_ref[ORDER] == 0)
    def _():
        work(early_ref, late_ref)

    @pl.when(at_ref[ORDER] != 0)
    def _():
        work(late_ref, early_ref)


def pack(at, early, late, after):
    out = [shape(ROWS, C, WIDE)] + EDGES
    return pl.pallas_call(
        pack_kernel,
        in_specs=[SMEM] + [ANY] * (2 + len(after)),
        out_specs=[HBM] * len(out),
        out_shape=out,
        scratch_shapes=[
            pltpu.VMEM((2, ROWS, C, COLS), jnp.bfloat16),
            pltpu.VMEM((ROWS, C, LANES), jnp.bfloat16),
            pltpu.VMEM((ROWS, C, LANES), jnp.bfloat16),
            pltpu.SemaphoreType.DMA((32,)),
        ],
        compiler_params=PARAMS,
        name="pack",
    )(at, early, late, *after)


def send(cells, strip_step, fold_step):
    return lax.ppermute(cells, AXES, moves(strip_step, fold_step))


def exchange(at, inward, outward, top, bottom):
    previous = send(inward, 0, 1)
    following = send(outward, 0, -1)
    below = send(top, -1, 0)
    above = send(bottom, 1, 0)
    following = jnp.where(at[FOLD] == 3, inward, following)
    ends = lambda first: jnp.concatenate(
        [lax.slice_in_dim(x, first, first + CORNER) for x in (previous, following)], axis=0
    )
    corner_below = send(ends(0), -1, 0)
    corner_above = send(ends(ROWS - CORNER), 1, 0)
    return previous, following, above, below, corner_above, corner_below


def conv_kernel(which, first, count, extra, at_ref, d_ref, limit_ref, cells, *refs):
    final = which == 1
    previous, following, above, below, corner_above, corner_below, w_ref, b_ref = refs[:8]
    refs = refs[8:]
    if final:
        own_ref, carried, refs = refs[0], refs[1 : 1 + extra], refs[1 + extra :]
        outs, scratch = refs[:4], refs[4:]
        out_ref, own, mid, before, behind, plus_ref, minus_ref, sems = scratch
    else:
        outs, scratch = refs[:5], refs[5:]
        out_ref, in_ref, back_ref, mid, before, behind, plus_ref, minus_ref, sems = scratch

    base = first - HALO
    started = []

    def fetch(src, low, high, target, shift):
        low, high = max(low, base), min(high, first + count + HALO)
        if low < high:
            started.append(
                pltpu.make_async_copy(
                    src.at[pl.ds(low - shift, high - low)],
                    target.at[pl.ds(low - base, high - low)],
                    sems.at[len(started)],
                )
            )

    fetch(above, -HALO, 0, mid, -HALO)
    fetch(corner_above, -CORNER, 0, before, -CORNER)
    fetch(corner_above, -CORNER, 0, behind, -2 * CORNER)
    fetch(cells, 0, ROWS, mid, 0)
    fetch(previous, 0, ROWS, before, 0)
    fetch(following, 0, ROWS, behind, 0)
    fetch(below, ROWS, ROWS + HALO, mid, ROWS)
    fetch(corner_below, ROWS, ROWS + CORNER, before, ROWS)
    fetch(corner_below, ROWS, ROWS + CORNER, behind, ROWS - CORNER)
    if final:
        late = pltpu.make_async_copy(own_ref.at[pl.ds(first, count)], own, sems.at[len(started)])
    for copy in started:
        copy.start()
    if final:
        late.start()
    for copy in started:
        copy.wait()

    d = d_ref[which]
    lo = d // 2
    hi = (d + 1) // 2
    odd = d - 2 * lo
    lane = lax.broadcasted_iota(jnp.int32, (C, LANES), 1)
    even_lane = (lane & 1) == 0

    def tiles(r):
        own = [mid[r, :, LANES * i : LANES * (i + 1)] for i in range(4)]
        return [before[r], *own[:2], behind[r], *own[2:]]

    def shifted(t, step, back):
        keep = lane < (step if back else LANES - step)
        turn = step if back else LANES - step
        left, a, b, right, c, e = t
        runs = ((left, a, b), (right, c, e)) if back else ((a, b, right), (c, e, left))
        out = []
        for run in runs:
            x, y, z = [pltpu.roll(v, turn, axis=1) for v in run]
            out += [jnp.where(keep, x, y), jnp.where(keep, y, z)]
        return jnp.concatenate(out, axis=1)

    start = HALO - hi

    def prepare(i, _):
        for j in range(PREP):
            r = start + i * PREP + j
            x, y = tiles(r), tiles(r + odd)
            both = [jnp.where(even_lane, b, a) for a, b in zip(x, y)]
            plus_ref[r] = shifted(both, d, False)
            minus_ref[r] = shifted(both, d, True)
        return 0

    lax.fori_loop(0, (count + d + PREP - 1) // PREP, prepare, 0)

    if final:
        late.wait()
    weight = w_ref[...]
    bias = b_ref[...]
    away = both_offsets(at_ref[FOLD])
    row0 = at_ref[ROW] + first

    def row(m, _):
        r = m + HALO
        x = tiles(r)
        taps = [
            mid[r - d],
            plus_ref[r - hi],
            shifted(x, 2 * d, False),
            minus_ref[r - hi],
            mid[r],
            plus_ref[r + lo],
            shifted(x, 2 * d, True),
            minus_ref[r + lo],
            mid[r + d],
        ]
        acc = lax.dot_general(
            weight,
            jnp.concatenate(taps, axis=0),
            (((1,), (0,)), ((), ())),
            preferred_element_type=jnp.float32,
        )
        acc = acc + bias
        if final:
            acc = acc + own[m].astype(jnp.float32)
        else:
            acc = jnp.maximum(acc, 0.0)
        acc = jnp.where(away <= threshold(limit_ref, row0 + m), acc, 0.0).astype(jnp.bfloat16)
        out_ref[m] = acc
        if not final:
            in_ref[m], back_ref[m] = inward_outward(acc, lane)
        return 0

    if final:
        lax.fori_loop(0, count, row, 0, unroll=UNROLL)
        mix(at_ref, limit_ref, first, count, out_ref, carried, *outs, plus_ref)
        return
    hidden, into, back, top, bottom = outs
    copies = []
    for at in range(0, ROWS, CHUNK):
        lax.fori_loop(at, at + CHUNK, row, 0, unroll=UNROLL)
        run = pl.ds(at, CHUNK)
        pairs = [(a.at[run], b.at[run]) for a, b in ((out_ref, hidden), (in_ref, into), (back_ref, back))]
        pairs += edge_copies(out_ref.at[run], at, CHUNK, top, bottom)
        for a, b in pairs:
            copies.append(pltpu.make_async_copy(a, b, sems.at[len(started) + len(copies)]))
            copies[-1].start()
    for copy in copies:
        copy.wait()


def mix(at_ref, limit_ref, first, count, summed, carried, first_ref, second_ref, edge_ref, other_ref, rows_ref):
    a = lax.broadcasted_iota(jnp.int32, (COLS, COLS), 0)
    b = lax.broadcasted_iota(jnp.int32, (COLS, COLS), 1)
    turn = (a + b == COLS).astype(jnp.bfloat16)
    lane = lax.broadcasted_iota(jnp.int32, (C, LANES), 1)
    away = both_offsets(at_ref[FOLD])
    row0 = at_ref[ROW] + first
    swap = at_ref[CORE] == 0
    edges = [jnp.zeros((C, LANES), jnp.bfloat16)] * 2
    if carried:
        edge, other = carried[0][...], carried[1][...]
        edges = [jnp.where(swap, other, edge), jnp.where(swap, edge, other)]
    for group in range(count // STACK):
        at = group * STACK
        cells = summed[pl.ds(at, STACK)].reshape(STACK * C, WIDE)
        blocks = cells[:, :COLS], cells[:, COLS:]
        turned = [jnp.dot(x, turn, preferred_element_type=jnp.float32) for x in blocks]
        for i in range(2):
            mean = 0.5 * (blocks[i].astype(jnp.float32) + turned[1 - i])
            for j in range(STACK):
                m = at + j
                part = slice(C * j, C * (j + 1))
                seen = away[:, COLS * i : COLS * (i + 1)] <= threshold(limit_ref, row0 + m)
                rows_ref[m, :, COLS * i : COLS * (i + 1)] = jnp.where(seen, mean[part], 0.0).astype(jnp.bfloat16)
                tile = blocks[i][part, :LANES]
                tile = pltpu.roll(tile, first + m, axis=1) if first + m else tile
                edges[i] = jnp.where(lane == first + m, tile, edges[i])
    edge_ref[...] = jnp.where(swap, edges[1], edges[0])
    other_ref[...] = jnp.where(swap, edges[0], edges[1])
    early = at_ref[ORDER] == 0

    @pl.when(early)
    def _():
        first_ref[...] = jnp.swapaxes(rows_ref[pl.ds(0, count), :, :COLS], 0, 1)
        second_ref[...] = jnp.swapaxes(rows_ref[pl.ds(0, count), :, COLS:], 0, 1)

    @pl.when(jnp.logical_not(early))
    def _():
        first_ref[...] = jnp.swapaxes(rows_ref[pl.ds(0, count), :, COLS:], 0, 1)
        second_ref[...] = jnp.swapaxes(rows_ref[pl.ds(0, count), :, :COLS], 0, 1)


def conv(own, at, d, row_limit, cells, halos, weight, bias, rows=(0, ROWS), carried=()):
    final = own is not None
    first, count = rows
    span = count + 2 * HALO
    in_specs = [SMEM] * 3 + [ANY] * 7 + [VMEM] * 2 + [ANY] * int(final) + [VMEM] * len(carried)
    args = [at, d, row_limit, cells, *halos, weight, bias] + ([own] if final else []) + list(carried)
    out_shape = [shape(C, count, COLS)] * 2 + [shape(C, LANES)] * 2 if final else [shape(ROWS, C, WIDE)] + EDGES
    scratch = [pltpu.VMEM((count, C, n), jnp.bfloat16) for n in ((WIDE, WIDE) if final else (WIDE, LANES, LANES))]
    return pl.pallas_call(
        functools.partial(conv_kernel, int(final), first, count, len(carried)),
        in_specs=in_specs,
        out_specs=[VMEM if final else HBM] * len(out_shape),
        out_shape=out_shape,
        scratch_shapes=scratch
        + [pltpu.VMEM((span, C, n), jnp.bfloat16) for n in (WIDE, LANES, LANES, WIDE, WIDE)]
        + [pltpu.SemaphoreType.DMA((32,))],
        compiler_params=PARAMS,
        name="second" if final else "first",
    )(*args)


def behind_kernel(*refs):
    del refs


def behind(cells, others):
    return pl.pallas_call(
        behind_kernel,
        in_specs=[ANY] * (len(cells) + len(others)),
        out_specs=[ANY] * len(cells),
        out_shape=[shape(*x.shape) for x in cells],
        input_output_aliases={i: i for i in range(len(cells))},
        compiler_params=PARAMS,
        name="behind",
    )(*cells, *others)


def flat(weight):
    return jnp.transpose(weight, (1, 0, 2)).reshape(C, 9 * C)


def local(band_map, dilations, row_limit, weight_one, bias_one, weight_two, bias_two):
    at = whereabouts()
    vector = jnp.stack(at)
    early, late = routes(0), routes(1)

    first = lax.ppermute(enter(0, vector, row_limit, band_map), AXES, early)
    second = lax.ppermute(enter(1, vector, row_limit, band_map), AXES, late)
    weights = [flat(weight_one), flat(weight_two)]
    biases = [bias_one[:, None], bias_two[:, None]]
    cells, *edges = pack(vector, first, second, weights + biases)
    halos = exchange(at, *edges)
    hidden, *edges = conv(None, vector, dilations, row_limit, cells, halos, weights[0], biases[0])
    halos = exchange(at, *edges)

    pos, off = lax.axis_index("pos"), lax.axis_index("off")
    here = lambda pairs: functools.reduce(jnp.logical_or, [(pos % 2 == s) & (off == b) for s, b in pairs])
    stays, relayed = here(STAY), here(VIA)
    leave, arrive = [], []
    for to, at_work in early:
        stored, block = to // 8, to % 8
        if (stored % 2, block) in VIA:
            via = device(stored // 2, *VIA[stored % 2, block])
            leave.append((at_work, via))
            arrive.append((via, to))
        elif at_work != to:
            leave.append((at_work, to))

    gots, directs, sent, carried = [], [], (), []
    for rows in PARTS:
        first, second, *carried = conv(
            cells, vector, dilations, row_limit, hidden, halos, weights[1], biases[1], rows, carried
        )
        if sent:
            first, second, *carried = behind((first, second, *carried), sent)
        passed = lax.ppermute(first, AXES, leave)
        directs.append(lax.ppermute(second, AXES, [(b, a) for a, b in late]))
        ended = lax.ppermute(passed, AXES, arrive)
        gots.append(jnp.where(stays, first, jnp.where(relayed, ended, passed)))
        sent = (passed, directs[-1])
    edge, other = carried

    to_first = lambda core: [(place(s, f), home(s // 2, f + 1)) for s, f in CELLS if s % 2 == core]
    to_second = lambda core: [(place(s, f), home(s // 2, 8 - f)) for s, f in CELLS if s % 2 == core and f]
    edge = lax.ppermute(edge, AXES, to_first(0) + to_second(1))
    other = lax.ppermute(other, AXES, to_second(0) + to_first(1))
    low = at[STORED_BLOCK] <= 4
    halves = jnp.where(low, edge, other), jnp.where(low, other, edge)
    top_first = at[EARLY] == 0
    column = lax.broadcasted_iota(jnp.int32, (1, 1, COLS), 2)
    out = []
    for half in range(2):
        for (start, count), *pair in zip(PARTS, gots, directs):
            got = jnp.where(top_first, *(pair if half == 0 else pair[::-1]))
            edge = lax.slice_in_dim(halves[half], start, start + count, axis=1)[:, :, None]
            more = (got.astype(jnp.float32) + 0.5 * edge.astype(jnp.float32)).astype(jnp.bfloat16)
            out.append(jnp.where(column == 0, more, got))
    return jnp.concatenate(out, axis=1)


def solution(mesh):
    in_specs = (P(None, "pos", "off"), P(), P(), P(), P(), P(), P())
    out_specs = P(None, "pos", "off")
    return jax.shard_map(local, mesh=mesh, in_specs=in_specs, out_specs=out_specs, check_vma=False)
```

time: 280 us -> 247 us (0.88)
  waiting for transfers between devices: 151 us -> 109 us
  starting transfers between devices: 45.1 us -> 67.1 us
  local copies, waits for them, and re-layouts: 9.81 us -> 4.69 us
  Pallas kernels: 62 us -> 57.4 us
  other arithmetic: 9.18 us -> 5.02 us
    ppermute x1 -> x2, waiting for transfers between devices: 56.3 us -> 26.7 us  [local(): passed = lax.ppermute(first, AXES, leave)]
    ppermute x3 -> x4, waiting for transfers between devices: 39.8 us -> 21.3 us  [the longest x1 17.2 us: local(): second = lax.ppermute(enter(1, vector, row_limit, band_map), AXES, late)]
    ppermute x1, waiting for transfers between devices: 16.9 us -> 0.69 us  [local(): other = lax.ppermute(other, AXES, to_second(0) + to_first(1))]
    ppermute x1 -> x2, waiting for transfers between devices: 0.01 us -> 15 us  [local(): ended = lax.ppermute(passed, AXES, arrive)]
    ppermute x3 -> x4, starting transfers between devices: 2 us -> 15.8 us  [the longest x1 12.4 us: local(): second = lax.ppermute(enter(1, vector, row_limit, band_map), AXES, late)]
    ppermute x1 -> x2, starting transfers between devices: 3.82 us -> 12.5 us  [local(): passed = lax.ppermute(first, AXES, leave)]
    ppermute x12, waiting for transfers between devices: 38 us -> 45 us  [send(): return lax.ppermute(cells, AXES, moves(strip_step, fold_step))]
    pallas_call x3 -> x5, Pallas kernels: 54.2 us -> 49.6 us  [the longest x3 44 us: conv(): pl.pallas_call(functools.partial(conv_kernel, int(final), first, count, l...]
  transfers between devices with their start and end apart: 19 -> 22, of which waited for: 10 -> 14; matrix products, arithmetic and copies ran while one was open for 4% -> 2% of each run, Pallas kernels for 0% -> 8%
where the time goes in v3:
time: 247 us; the launch traced here: 243 us
  waiting for transfers between devices  109 us (44%)
  starting transfers between devices  67.1 us (27%)
  Pallas kernels  57.4 us (23%)
  other arithmetic  5.02 us (2%)
  local copies, waits for them, and re-layouts  4.69 us (2%)
    ppermute x12, waiting for transfers between devices, send(): return lax.ppermute(cells, AXES, moves(strip_step, fold_step))  45 us
    pallas_call x3, Pallas kernels, conv(): pl.pallas_call(functools.partial(conv_kernel, int(final), first, count, l...  44 us
    ppermute x12, starting transfers between devices, send(): return lax.ppermute(cells, AXES, moves(strip_step, fold_step))  31.9 us
    ppermute x2, waiting for transfers between devices, local(): passed = lax.ppermute(first, AXES, leave)  26.7 us
    ppermute x1, waiting for transfers between devices, local(): second = lax.ppermute(enter(1, vector, row_limit, band_map), AXES, late)  17.2 us
    ppermute x2, waiting for transfers between devices, local(): ended = lax.ppermute(passed, AXES, arrive)  15 us
    ppermute x2, starting transfers between devices, local(): passed = lax.ppermute(first, AXES, leave)  12.5 us
    ppermute x1, starting transfers between devices, local(): second = lax.ppermute(enter(1, vector, row_limit, band_map), AXES, late)  12.4 us
  transfers between devices with their start and end apart: 22, of which 14 were waited for; matrix products, arithmetic and copies ran while one was open for 2% of the time, Pallas kernels for 8%

profile of v3, /device:TPU:118, one launch (start us, length us, event | category | flops | bytes accessed | tf_op | source)
XLA Modules:
  0.0 243.3 jit_solution(3350776168666018135)
XLA Ops:
  0.0 0.7 stack.31.at_ref
  0.7 3.9 %enter.2 = bf16[72,48,256]{2,1,0:T(8,128)(2,1)} custom-call(s32[7]{0:T(128)} %stack.31.at_ref, s32[2304]{0:T(1024)} %limit_ref.9, bf16[48,144,256]{2,1,0:T(8,128)(2,1)} %x_ref.3), custom_call_target="tpu_custom_call" | custom-call | tf_op jit(solution)/shard_map/enter/pallas_call | solution.py:116
  4.5 2.1 collective-permute-start
  6.6 3.9 %enter.3 = bf16[72,48,256]{2,1,0:T(8,128)(2,1)} custom-call(s32[7]{0:T(128)} %stack.31.at_ref, s32[2304]{0:T(1024)} %limit_ref.9, bf16[48,144,256]{2,1,0:T(8,128)(2,1)} %x_ref.3), custom_call_target="tpu_custom_call" | custom-call | tf_op jit(solution)/shard_map/enter/pallas_call | solution.py:116
  10.5 12.4 %collective-permute-start.1 = (bf16[72,48,256]{2,1,0:T(8,128)(2,1)}, bf16[72,48,256]{2,1,0:T(8,128)(2,1)}, u32[]{:S(2)}, u32[]{:S(2)}) collective-permute-start(bf16[72,48,256]{2,1,0:T(8,128)(2,1)} %enter.3), channel_id=1, source_target_pairs={{7,0},{1,6},{5,4},{4,2},{0,8},{6,14},{2,12},{3,10},{15,1},{14,7},{... | collective-permute-start | bytes 5308424 | tf_op jit(solution)/shard_map/ppermute | solution.py:452
  22.8 0.1 copy.20
  23.0 0.7 copy.22.refs_1_.refs_6_
  23.7 0.7 copy.24.refs_3_.refs_7_
  24.4 0.1 copy.19
  24.5 0.7 copy.21.refs_0_.refs_6_
  25.2 0.7 copy.23.refs_2_.refs_7_
  25.9 4.1 %collective-permute-done.early_ref = bf16[72,48,256]{2,1,0:T(8,128)(2,1)} collective-permute-done((bf16[72,48,256]{2,1,0:T(8,128)(2,1)}, bf16[72,48,256]{2,1,0:T(8,128)(2,1)}, u32[]{:S(2)}, u32[]{:S(2)}) %collective-permute-start) | collective-permute-done | bytes 1769504 | tf_op jit(solution)/shard_map/ppermute | solution.py:451
  30.0 17.2 %collective-permute-done.1.late_ref = bf16[72,48,256]{2,1,0:T(8,128)(2,1)} collective-permute-done((bf16[72,48,256]{2,1,0:T(8,128)(2,1)}, bf16[72,48,256]{2,1,0:T(8,128)(2,1)}, u32[]{:S(2)}, u32[]{:S(2)}) %collective-permute-start.1) | collective-permute-done | bytes 1769504 | tf_op jit(solution)/shard_map/ppermute | solution.py:452
  47.2 5.6 %pack.1 = (bf16[72,48,512]{2,1,0:T(8,128)(2,1)}, bf16[72,48,128]{2,1,0:T(8,128)(2,1)}, bf16[72,48,128]{2,1,0:T(8,128)(2,1)}, bf16[32,48,512]{2,1,0:T(8,128)(2,1)}, bf16[32,48,512]{2,1,0:T(8,128)(2,1)}) custom-call(s32[7]{0:T(128)} %stack.31.at_ref, bf16[72,48,256]{2,1,0:T(8,128)(2,1)} %collective-permute-done.early_ref, ...), custom_call_target="tpu_custom_call" | custom-call | tf_op jit(solution)/shard_map/pack/pallas_call | solution.py:194
  52.9 3.5 %collective-permute-start.3 = (bf16[72,48,128]{2,1,0:T(8,128)(2,1)}, bf16[72,48,128]{2,1,0:T(8,128)(2,1)S(1)}, u32[]{:S(2)}, u32[]{:S(2)}) collective-permute-start(bf16[72,48,128]{2,1,0:T(8,128)(2,1)} %get-tuple-element.29), channel_id=1, source_target_pairs={{6,0},{4,6},{2,4},{14,8},{12,14},{10,12},{7,1},{5,7},{3,5},{15,9},... | collective-permute-start | bytes 2654216 | tf_op jit(solution)/shard_map/ppermute | solution.py:211
  56.4 2.3 collective-permute-start.2
  58.7 3.0 %collective-permute-start.4 = (bf16[32,48,512]{2,1,0:T(8,128)(2,1)}, bf16[32,48,512]{2,1,0:T(8,128)(2,1)}, u32[]{:S(2)}, u32[]{:S(2)}) collective-permute-start(bf16[32,48,512]{2,1,0:T(8,128)(2,1)} %get-tuple-element.30), channel_id=1, source_target_pairs={{0,8},{6,14},{4,12},{2,10},{8,1},{14,7},{12,5},{10,3},{1,9},{7,15}... | collective-permute-start | bytes 4718600 | tf_op jit(solution)/shard_map/ppermute | solution.py:211
  61.7 2.6 %collective-permute-start.5 = (bf16[32,48,512]{2,1,0:T(8,128)(2,1)}, bf16[32,48,512]{2,1,0:T(8,128)(2,1)}, u32[]{:S(2)}, u32[]{:S(2)}) collective-permute-start(bf16[32,48,512]{2,1,0:T(8,128)(2,1)} %get-tuple-element.31), channel_id=1, source_target_pairs={{8,0},{14,6},{12,4},{10,2},{1,8},{7,14},{5,12},{3,10},{9,1},{15,7}... | collective-permute-start | bytes 4718600 | tf_op jit(solution)/shard_map/ppermute | solution.py:211
  64.3 12.6 %collective-permute-done.3 = bf16[72,48,128]{2,1,0:T(8,128)(2,1)S(1)} collective-permute-done((bf16[72,48,128]{2,1,0:T(8,128)(2,1)}, bf16[72,48,128]{2,1,0:T(8,128)(2,1)S(1)}, u32[]{:S(2)}, u32[]{:S(2)}) %collective-permute-start.3) | collective-permute-done | bytes 884768 | tf_op jit(solution)/shard_map/ppermute | solution.py:211
  76.9 0.1 broadcast_select_fusion.1.refs_1_
  77.1 4.2 %collective-permute-done.2.refs_0_ = bf16[72,48,128]{2,1,0:T(8,128)(2,1)S(1)} collective-permute-done((bf16[72,48,128]{2,1,0:T(8,128)(2,1)}, bf16[72,48,128]{2,1,0:T(8,128)(2,1)S(1)}, u32[]{:S(2)}, u32[]{:S(2)}) %collective-permute-start.2) | collective-permute-done | bytes 884768 | tf_op jit(solution)/shard_map/ppermute | solution.py:211
  81.3 1.9 collective-permute-start.7
  83.3 2.4 collective-permute-start.6
  85.7 2.8 %collective-permute-done.7.refs_5_ = bf16[32,48,128]{2,1,0:T(8,128)(2,1)} collective-permute-done((bf16[32,48,128]{2,1,0:T(8,128)(2,1)S(1)}, bf16[32,48,128]{2,1,0:T(8,128)(2,1)}, u32[]{:S(2)}, u32[]{:S(2)}) %collective-permute-start.7) | collective-permute-done | bytes 393248 | tf_op jit(solution)/shard_map/ppermute | solution.py:211
  88.5 4.0 %collective-permute-done.6.refs_4_ = bf16[32,48,128]{2,1,0:T(8,128)(2,1)} collective-permute-done((bf16[32,48,128]{2,1,0:T(8,128)(2,1)S(1)}, bf16[32,48,128]{2,1,0:T(8,128)(2,1)}, u32[]{:S(2)}, u32[]{:S(2)}) %collective-permute-start.6) | collective-permute-done | bytes 393248 | tf_op jit(solution)/shard_map/ppermute | solution.py:211
  92.5 0.0 collective-permute-done.4.refs_2_
  92.5 0.0 collective-permute-done.5.refs_3_
  92.5 18.7 %first.1 = (bf16[72,48,512]{2,1,0:T(8,128)(2,1)}, bf16[72,48,128]{2,1,0:T(8,128)(2,1)}, bf16[72,48,128]{2,1,0:T(8,128)(2,1)}, bf16[32,48,512]{2,1,0:T(8,128)(2,1)}, bf16[32,48,512]{2,1,0:T(8,128)(2,1)}) custom-call(s32[7]{0:T(128)} %stack.31.at_ref, s32[2]{0:T(128)} %d_ref.5, s32[2304]{0:T(1024)} %limit_ref.9, ...), custom_call_target="tpu_custom_call" | custom-call | tf_op jit(solution)/shard_map/first/pallas_call | solution.py:413
  111.3 1.9 collective-permute-start.9
  113.2 3.9 %collective-permute-start.8 = (bf16[72,48,128]{2,1,0:T(8,128)(2,1)}, bf16[72,48,128]{2,1,0:T(8,128)(2,1)S(1)}, u32[]{:S(2)}, u32[]{:S(2)}) collective-permute-start(bf16[72,48,128]{2,1,0:T(8,128)(2,1)} %get-tuple-element.33), channel_id=1, source_target_pairs={{0,6},{6,4},{4,2},{8,14},{14,12},{12,10},{1,7},{7,5},{5,3},{9,15},... | collective-permute-start | bytes 2654216 | tf_op jit(solution)/shard_map/ppermute | solution.py:211
  117.1 2.0 collective-permute-start.10
  119.1 3.6 %collective-permute-start.11 = (bf16[32,48,512]{2,1,0:T(8,128)(2,1)}, bf16[32,48,512]{2,1,0:T(8,128)(2,1)}, u32[]{:S(2)}, u32[]{:S(2)}) collective-permute-start(bf16[32,48,512]{2,1,0:T(8,128)(2,1)} %get-tuple-element.36), channel_id=1, source_target_pairs={{8,0},{14,6},{12,4},{10,2},{1,8},{7,14},{5,12},{3,10},{9,1},{15,7}... | collective-permute-start | bytes 4718600 | tf_op jit(solution)/shard_map/ppermute | solution.py:211
  122.7 12.7 %collective-permute-done.9 = bf16[72,48,128]{2,1,0:T(8,128)(2,1)S(1)} collective-permute-done((bf16[72,48,128]{2,1,0:T(8,128)(2,1)}, bf16[72,48,128]{2,1,0:T(8,128)(2,1)S(1)}, u32[]{:S(2)}, u32[]{:S(2)}) %collective-permute-start.9) | collective-permute-done | bytes 884768 | tf_op jit(solution)/shard_map/ppermute | solution.py:211
  135.4 0.1 broadcast_select_fusion.refs_1_
  135.6 2.3 collective-permute-done.8.refs_0_
  138.0 1.9 collective-permute-start.13
  140.0 2.8 %collective-permute-start.12 = (bf16[32,48,128]{2,1,0:T(8,128)(2,1)S(1)}, bf16[32,48,128]{2,1,0:T(8,128)(2,1)}, u32[]{:S(2)}, u32[]{:S(2)}) collective-permute-start(bf16[32,48,128]{2,1,0:T(8,128)(2,1)S(1)} %pad_maximum_fusion.3), channel_id=1, source_target_pairs={{0,8},{6,14},{4,12},{2,10},{8,1},{14,7},{12,5},{10,3},{1,9},{7,15}... | collective-permute-start | bytes 1179656 | tf_op jit(solution)/shard_map/ppermute | solution.py:211
  142.8 2.4 collective-permute-done.13.refs_5_
  145.2 4.0 %collective-permute-done.12.refs_4_ = bf16[32,48,128]{2,1,0:T(8,128)(2,1)} collective-permute-done((bf16[32,48,128]{2,1,0:T(8,128)(2,1)S(1)}, bf16[32,48,128]{2,1,0:T(8,128)(2,1)}, u32[]{:S(2)}, u32[]{:S(2)}) %collective-permute-start.12) | collective-permute-done | bytes 393248 | tf_op jit(solution)/shard_map/ppermute | solution.py:211
  149.2 9.9 %second.2 = (bf16[48,24,256]{2,1,0:T(8,128)(2,1)}, bf16[48,24,256]{2,1,0:T(8,128)(2,1)}, bf16[48,128]{1,0:T(8,128)(2,1)}, bf16[48,128]{1,0:T(8,128)(2,1)}) custom-call(s32[7]{0:T(128)} %stack.31.at_ref, s32[2]{0:T(128)} %d_ref.5, s32[2304]{0:T(1024)} %limit_ref.9, bf16[72,48,512]{2,1,0:T(8,128)(2,1)} %get-tuple-element.32.cells, ...), custom_call_target="tpu_custom_call" | custom-call | tf_op jit(solution)/shard_map/second/pallas_call | solution.py:413
  159.1 7.0 %collective-permute-start.14 = (bf16[48,24,256]{2,1,0:T(8,128)(2,1)}, bf16[48,24,256]{2,1,0:T(8,128)(2,1)}, u32[]{:S(2)}, u32[]{:S(2)}) collective-permute-start(bf16[48,24,256]{2,1,0:T(8,128)(2,1)} %get-tuple-element.37), channel_id=1, source_target_pairs={{4,2},{2,3},{8,6},{14,0},{12,5},{10,4},{1,8},{7,9},{5,11},{3,13},{... | collective-permute-start | bytes 1769480 | tf_op jit(solution)/shard_map/ppermute | solution.py:480
  166.1 0.0 collective-permute-start.16
  166.2 15.3 %second.3 = (bf16[48,48,256]{2,1,0:T(8,128)(2,1)}, bf16[48,48,256]{2,1,0:T(8,128)(2,1)}, bf16[48,128]{1,0:T(8,128)(2,1)}, bf16[48,128]{1,0:T(8,128)(2,1)}) custom-call(s32[7]{0:T(128)} %stack.31.at_ref, s32[2]{0:T(128)} %d_ref.5, s32[2304]{0:T(1024)} %limit_ref.9, bf16[72,48,512]{2,1,0:T(8,128)(2,1)} %get-tuple-element.32.cells, ...), custom_call_target="tpu_custom_call" | custom-call | tf_op jit(solution)/shard_map/second/pallas_call | solution.py:413
  181.5 1.1 collective-permute-done.14.refs_4_
  182.6 0.0 collective-permute-done.16.refs_5_
  182.6 0.8 copy-done.1
  183.4 5.5 %collective-permute-start.19 = (bf16[48,48,256]{2,1,0:T(8,128)(2,1)}, bf16[48,48,256]{2,1,0:T(8,128)(2,1)S(1)}, u32[]{:S(2)}, u32[]{:S(2)}) collective-permute-start(bf16[48,48,256]{2,1,0:T(8,128)(2,1)} %get-tuple-element.47), channel_id=1, source_target_pairs={{4,2},{2,3},{8,6},{14,0},{12,5},{10,4},{1,8},{7,9},{5,11},{3,13},{... | collective-permute-start | bytes 3538952 | tf_op jit(solution)/shard_map/ppermute | solution.py:480
  188.9 1.9 collective-permute-start.17
  190.8 2.4 collective-permute-start.18
  193.3 1.4 collective-permute-start.21
  194.6 1.3 collective-permute-start.15
  195.9 0.0 collective-permute-done.17
  195.9 0.7 collective-permute-done.18
  196.7 25.6 %collective-permute-done.19 = bf16[48,48,256]{2,1,0:T(8,128)(2,1)S(1)} collective-permute-done((bf16[48,48,256]{2,1,0:T(8,128)(2,1)}, bf16[48,48,256]{2,1,0:T(8,128)(2,1)S(1)}, u32[]{:S(2)}, u32[]{:S(2)}) %collective-permute-start.19) | collective-permute-done | bytes 1179680 | tf_op jit(solution)/shard_map/ppermute | solution.py:480
  222.3 1.3 collective-permute-start.20
  223.6 0.1 convert_multiply_fusion.2
  223.7 0.1 convert_multiply_fusion
  223.7 1.4 fusion.2
  225.2 0.2 fusion.3
  225.4 0.0 collective-permute-done.21
  225.4 15.0 %collective-permute-done.20 = bf16[48,48,256]{2,1,0:T(8,128)(2,1)S(1)} collective-permute-done((bf16[48,48,256]{2,1,0:T(8,128)(2,1)S(1)}, bf16[48,48,256]{2,1,0:T(8,128)(2,1)S(1)}, u32[]{:S(2)}, u32[]{:S(2)}) %collective-permute-start.20) | collective-permute-done | bytes 1179680 | tf_op jit(solution)/shard_map/ppermute | solution.py:482
  240.4 0.5 fusion
  240.9 0.4 fusion.1
  241.3 1.9 pad_maximum_fusion
  (37 shorter events, 0.3 us)
Async XLA Ops:
  4.5 18.3 %copy-start.7 = (bf16[9,48,48]{2,1,0:T(8,128)(2,1)S(1)}, bf16[9,48,48]{2,1,0:T(8,128)(2,1)}, u32[]{:S(2)}) copy-start(bf16[9,48,48]{2,1,0:T(8,128)(2,1)} %param.12) | copy-start | bytes 124420
  4.5 19.2 %copy-start.9 = (f32[48]{0:T(128)S(1)}, f32[48]{0:T(128)}, u32[]{:S(2)}) copy-start(f32[48]{0:T(128)} %param.13) | copy-start | bytes 580
  4.5 19.9 %copy-start.8 = (bf16[9,48,48]{2,1,0:T(8,128)(2,1)S(1)}, bf16[9,48,48]{2,1,0:T(8,128)(2,1)}, u32[]{:S(2)}) copy-start(bf16[9,48,48]{2,1,0:T(8,128)(2,1)} %param.10) | copy-start | bytes 124420
  4.5 20.7 %copy-start.10 = (f32[48]{0:T(128)S(1)}, f32[48]{0:T(128)}, u32[]{:S(2)}) copy-start(f32[48]{0:T(128)} %param.11) | copy-start | bytes 580
  4.5 25.5 %collective-permute-start = (bf16[72,48,256]{2,1,0:T(8,128)(2,1)}, bf16[72,48,256]{2,1,0:T(8,128)(2,1)}, u32[]{:S(2)}, u32[]{:S(2)}) collective-permute-start(bf16[72,48,256]{2,1,0:T(8,128)(2,1)} %enter.2), channel_id=1, source_target_pairs={{0,0},{6,6},{2,4},{3,2},{7,8},{1,14},{5,12},{4,10},{8,1},{9,7},{10... | collective-permute-start | bytes 5308424 | tf_op jit(solution)/shard_map/ppermute | solution.py:451
  10.5 36.7 %collective-permute-start.1 = (bf16[72,48,256]{2,1,0:T(8,128)(2,1)}, bf16[72,48,256]{2,1,0:T(8,128)(2,1)}, u32[]{:S(2)}, u32[]{:S(2)}) collective-permute-start(bf16[72,48,256]{2,1,0:T(8,128)(2,1)} %enter.3), channel_id=1, source_target_pairs={{7,0},{1,6},{5,4},{4,2},{0,8},{6,14},{2,12},{3,10},{15,1},{14,7},{... | collective-permute-start | bytes 5308424 | tf_op jit(solution)/shard_map/ppermute | solution.py:452
  52.9 24.1 %collective-permute-start.3 = (bf16[72,48,128]{2,1,0:T(8,128)(2,1)}, bf16[72,48,128]{2,1,0:T(8,128)(2,1)S(1)}, u32[]{:S(2)}, u32[]{:S(2)}) collective-permute-start(bf16[72,48,128]{2,1,0:T(8,128)(2,1)} %get-tuple-element.29), channel_id=1, source_target_pairs={{6,0},{4,6},{2,4},{14,8},{12,14},{10,12},{7,1},{5,7},{3,5},{15,9},... | collective-permute-start | bytes 2654216 | tf_op jit(solution)/shard_map/ppermute | solution.py:211
  56.4 24.9 %collective-permute-start.2 = (bf16[72,48,128]{2,1,0:T(8,128)(2,1)}, bf16[72,48,128]{2,1,0:T(8,128)(2,1)S(1)}, u32[]{:S(2)}, u32[]{:S(2)}) collective-permute-start(bf16[72,48,128]{2,1,0:T(8,128)(2,1)} %get-tuple-element.28), channel_id=1, source_target_pairs={{0,6},{6,4},{4,2},{8,14},{14,12},{12,10},{1,7},{7,5},{5,3},{9,15},... | collective-permute-start | bytes 2654216 | tf_op jit(solution)/shard_map/ppermute | solution.py:211
  58.7 33.8 %collective-permute-start.4 = (bf16[32,48,512]{2,1,0:T(8,128)(2,1)}, bf16[32,48,512]{2,1,0:T(8,128)(2,1)}, u32[]{:S(2)}, u32[]{:S(2)}) collective-permute-start(bf16[32,48,512]{2,1,0:T(8,128)(2,1)} %get-tuple-element.30), channel_id=1, source_target_pairs={{0,8},{6,14},{4,12},{2,10},{8,1},{14,7},{12,5},{10,3},{1,9},{7,15}... | collective-permute-start | bytes 4718600 | tf_op jit(solution)/shard_map/ppermute | solution.py:211
  61.7 30.9 %collective-permute-start.5 = (bf16[32,48,512]{2,1,0:T(8,128)(2,1)}, bf16[32,48,512]{2,1,0:T(8,128)(2,1)}, u32[]{:S(2)}, u32[]{:S(2)}) collective-permute-start(bf16[32,48,512]{2,1,0:T(8,128)(2,1)} %get-tuple-element.31), channel_id=1, source_target_pairs={{8,0},{14,6},{12,4},{10,2},{1,8},{7,14},{5,12},{3,10},{9,1},{15,7}... | collective-permute-start | bytes 4718600 | tf_op jit(solution)/shard_map/ppermute | solution.py:211
  77.0 6.3 %copy-start.3 = (bf16[72,48,128]{2,1,0:T(8,128)(2,1)}, bf16[72,48,128]{2,1,0:T(8,128)(2,1)S(1)}, u32[]{:S(2)}) copy-start(bf16[72,48,128]{2,1,0:T(8,128)(2,1)S(1)} %broadcast_select_fusion.1.refs_1_) | copy-start | bytes 2654212
  81.3 11.3 %copy-start.6 = (bf16[72,48,128]{2,1,0:T(8,128)(2,1)}, bf16[72,48,128]{2,1,0:T(8,128)(2,1)S(1)}, u32[]{:S(2)}) copy-start(bf16[72,48,128]{2,1,0:T(8,128)(2,1)S(1)} %collective-permute-done.2.refs_0_) | copy-start | bytes 2654212
  81.3 7.2 %collective-permute-start.7 = (bf16[32,48,128]{2,1,0:T(8,128)(2,1)S(1)}, bf16[32,48,128]{2,1,0:T(8,128)(2,1)}, u32[]{:S(2)}, u32[]{:S(2)}) collective-permute-start(bf16[32,48,128]{2,1,0:T(8,128)(2,1)S(1)} %pad_maximum_fusion.2), channel_id=1, source_target_pairs={{8,0},{14,6},{12,4},{10,2},{1,8},{7,14},{5,12},{3,10},{9,1},{15,7}... | collective-permute-start | bytes 1179656 | tf_op jit(solution)/shard_map/ppermute | solution.py:211
  83.3 9.2 %collective-permute-start.6 = (bf16[32,48,128]{2,1,0:T(8,128)(2,1)S(1)}, bf16[32,48,128]{2,1,0:T(8,128)(2,1)}, u32[]{:S(2)}, u32[]{:S(2)}) collective-permute-start(bf16[32,48,128]{2,1,0:T(8,128)(2,1)S(1)} %pad_maximum_fusion.1), channel_id=1, source_target_pairs={{0,8},{6,14},{4,12},{2,10},{8,1},{14,7},{12,5},{10,3},{1,9},{7,15}... | collective-permute-start | bytes 1179656 | tf_op jit(solution)/shard_map/ppermute | solution.py:211
  111.3 24.2 %collective-permute-start.9 = (bf16[72,48,128]{2,1,0:T(8,128)(2,1)}, bf16[72,48,128]{2,1,0:T(8,128)(2,1)S(1)}, u32[]{:S(2)}, u32[]{:S(2)}) collective-permute-start(bf16[72,48,128]{2,1,0:T(8,128)(2,1)} %get-tuple-element.34), channel_id=1, source_target_pairs={{6,0},{4,6},{2,4},{14,8},{12,14},{10,12},{7,1},{5,7},{3,5},{15,9},... | collective-permute-start | bytes 2654216 | tf_op jit(solution)/shard_map/ppermute | solution.py:211
  113.2 24.7 %collective-permute-start.8 = (bf16[72,48,128]{2,1,0:T(8,128)(2,1)}, bf16[72,48,128]{2,1,0:T(8,128)(2,1)S(1)}, u32[]{:S(2)}, u32[]{:S(2)}) collective-permute-start(bf16[72,48,128]{2,1,0:T(8,128)(2,1)} %get-tuple-element.33), channel_id=1, source_target_pairs={{0,6},{6,4},{4,2},{8,14},{14,12},{12,10},{1,7},{7,5},{5,3},{9,15},... | collective-permute-start | bytes 2654216 | tf_op jit(solution)/shard_map/ppermute | solution.py:211
  117.1 32.1 %collective-permute-start.10 = (bf16[32,48,512]{2,1,0:T(8,128)(2,1)}, bf16[32,48,512]{2,1,0:T(8,128)(2,1)}, u32[]{:S(2)}, u32[]{:S(2)}) collective-permute-start(bf16[32,48,512]{2,1,0:T(8,128)(2,1)} %get-tuple-element.35), channel_id=1, source_target_pairs={{0,8},{6,14},{4,12},{2,10},{8,1},{14,7},{12,5},{10,3},{1,9},{7,15}... | collective-permute-start | bytes 4718600 | tf_op jit(solution)/shard_map/ppermute | solution.py:211
  119.1 30.1 %collective-permute-start.11 = (bf16[32,48,512]{2,1,0:T(8,128)(2,1)}, bf16[32,48,512]{2,1,0:T(8,128)(2,1)}, u32[]{:S(2)}, u32[]{:S(2)}) collective-permute-start(bf16[32,48,512]{2,1,0:T(8,128)(2,1)} %get-tuple-element.36), channel_id=1, source_target_pairs={{8,0},{14,6},{12,4},{10,2},{1,8},{7,14},{5,12},{3,10},{9,1},{15,7}... | collective-permute-start | bytes 4718600 | tf_op jit(solution)/shard_map/ppermute | solution.py:211
  135.5 4.4 %copy-start = (bf16[72,48,128]{2,1,0:T(8,128)(2,1)}, bf16[72,48,128]{2,1,0:T(8,128)(2,1)S(1)}, u32[]{:S(2)}) copy-start(bf16[72,48,128]{2,1,0:T(8,128)(2,1)S(1)} %broadcast_select_fusion.refs_1_) | copy-start | bytes 2654212
  137.9 11.3 %copy-start.4 = (bf16[72,48,128]{2,1,0:T(8,128)(2,1)}, bf16[72,48,128]{2,1,0:T(8,128)(2,1)S(1)}, u32[]{:S(2)}) copy-start(bf16[72,48,128]{2,1,0:T(8,128)(2,1)S(1)} %collective-permute-done.8.refs_0_) | copy-start | bytes 2654212
  138.0 7.2 %collective-permute-start.13 = (bf16[32,48,128]{2,1,0:T(8,128)(2,1)S(1)}, bf16[32,48,128]{2,1,0:T(8,128)(2,1)}, u32[]{:S(2)}, u32[]{:S(2)}) collective-permute-start(bf16[32,48,128]{2,1,0:T(8,128)(2,1)S(1)} %pad_maximum_fusion.4), channel_id=1, source_target_pairs={{8,0},{14,6},{12,4},{10,2},{1,8},{7,14},{5,12},{3,10},{9,1},{15,7}... | collective-permute-start | bytes 1179656 | tf_op jit(solution)/shard_map/ppermute | solution.py:211
  140.0 9.2 %collective-permute-start.12 = (bf16[32,48,128]{2,1,0:T(8,128)(2,1)S(1)}, bf16[32,48,128]{2,1,0:T(8,128)(2,1)}, u32[]{:S(2)}, u32[]{:S(2)}) collective-permute-start(bf16[32,48,128]{2,1,0:T(8,128)(2,1)S(1)} %pad_maximum_fusion.3), channel_id=1, source_target_pairs={{0,8},{6,14},{4,12},{2,10},{8,1},{14,7},{12,5},{10,3},{1,9},{7,15}... | collective-permute-start | bytes 1179656 | tf_op jit(solution)/shard_map/ppermute | solution.py:211
  159.1 23.4 %collective-permute-start.14 = (bf16[48,24,256]{2,1,0:T(8,128)(2,1)}, bf16[48,24,256]{2,1,0:T(8,128)(2,1)}, u32[]{:S(2)}, u32[]{:S(2)}) collective-permute-start(bf16[48,24,256]{2,1,0:T(8,128)(2,1)} %get-tuple-element.37), channel_id=1, source_target_pairs={{4,2},{2,3},{8,6},{14,0},{12,5},{10,4},{1,8},{7,9},{5,11},{3,13},{... | collective-permute-start | bytes 1769480 | tf_op jit(solution)/shard_map/ppermute | solution.py:480
  166.1 16.4 %collective-permute-start.16 = (bf16[48,24,256]{2,1,0:T(8,128)(2,1)}, bf16[48,24,256]{2,1,0:T(8,128)(2,1)S(1)}, u32[]{:S(2)}, u32[]{:S(2)}) collective-permute-start(bf16[48,24,256]{2,1,0:T(8,128)(2,1)} %get-tuple-element.38), channel_id=1, source_target_pairs={{0,7},{6,1},{4,5},{2,4},{8,0},{14,6},{12,2},{10,3},{1,15},{7,14},{... | collective-permute-start | bytes 1769480 | tf_op jit(solution)/shard_map/ppermute | solution.py:481
  182.6 0.8 copy-start.1
  183.4 38.9 %collective-permute-start.19 = (bf16[48,48,256]{2,1,0:T(8,128)(2,1)}, bf16[48,48,256]{2,1,0:T(8,128)(2,1)S(1)}, u32[]{:S(2)}, u32[]{:S(2)}) collective-permute-start(bf16[48,48,256]{2,1,0:T(8,128)(2,1)} %get-tuple-element.47), channel_id=1, source_target_pairs={{4,2},{2,3},{8,6},{14,0},{12,5},{10,4},{1,8},{7,9},{5,11},{3,13},{... | collective-permute-start | bytes 3538952 | tf_op jit(solution)/shard_map/ppermute | solution.py:480
  188.9 7.0 %collective-permute-start.17 = (bf16[48,128]{1,0:T(8,128)(2,1)}, bf16[48,128]{1,0:T(8,128)(2,1)S(1)}, u32[]{:S(2)}, u32[]{:S(2)}) collective-permute-start(bf16[48,128]{1,0:T(8,128)(2,1)} %get-tuple-element.45), channel_id=1, source_target_pairs={{0,1},{6,2},{4,3},{2,4},{1,9},{7,10},{5,11},{3,12},{16,17},{22,18}... | collective-permute-start | bytes 36872 | tf_op jit(solution)/shard_map/ppermute | solution.py:489
  190.8 5.8 %collective-permute-start.18 = (bf16[48,128]{1,0:T(8,128)(2,1)}, bf16[48,128]{1,0:T(8,128)(2,1)S(1)}, u32[]{:S(2)}, u32[]{:S(2)}) collective-permute-start(bf16[48,128]{1,0:T(8,128)(2,1)} %get-tuple-element.46), channel_id=1, source_target_pairs={{6,7},{4,6},{2,5},{7,15},{5,14},{3,13},{22,23},{20,22},{18,21},{23... | collective-permute-start | bytes 36872 | tf_op jit(solution)/shard_map/ppermute | solution.py:490
  193.3 32.1 %collective-permute-start.21 = (bf16[48,48,256]{2,1,0:T(8,128)(2,1)}, bf16[48,48,256]{2,1,0:T(8,128)(2,1)S(1)}, u32[]{:S(2)}, u32[]{:S(2)}) collective-permute-start(bf16[48,48,256]{2,1,0:T(8,128)(2,1)} %get-tuple-element.48), channel_id=1, source_target_pairs={{0,7},{6,1},{4,5},{2,4},{8,0},{14,6},{12,2},{10,3},{1,15},{7,14},{... | collective-permute-start | bytes 3538952 | tf_op jit(solution)/shard_map/ppermute | solution.py:481
  194.6 29.1 %collective-permute-start.15 = (bf16[48,24,256]{2,1,0:T(8,128)(2,1)}, bf16[48,24,256]{2,1,0:T(8,128)(2,1)S(1)}, u32[]{:S(2)}, u32[]{:S(2)}) collective-permute-start(bf16[48,24,256]{2,1,0:T(8,128)(2,1)} %collective-permute-done.14.refs_4_), channel_id=1, source_target_pairs={{6,7},{0,1},{11,10},{13,12},{22,23},{16,17},{27,26},{29,28},{38,39... | collective-permute-start | bytes 1769480 | tf_op jit(solution)/shard_map/ppermute | solution.py:482
  222.3 18.1 %collective-permute-start.20 = (bf16[48,48,256]{2,1,0:T(8,128)(2,1)S(1)}, bf16[48,48,256]{2,1,0:T(8,128)(2,1)S(1)}, u32[]{:S(2)}, u32[]{:S(2)}) collective-permute-start(bf16[48,48,256]{2,1,0:T(8,128)(2,1)S(1)} %collective-permute-done.19), channel_id=1, source_target_pairs={{6,7},{0,1},{11,10},{13,12},{22,23},{16,17},{27,26},{29,28},{38,39... | collective-permute-start | bytes 3538952 | tf_op jit(solution)/shard_map/ppermute | solution.py:482
  223.7 1.4 copy-start.2
  225.1 15.2 %copy-start.5 = (bf16[48,48,256]{2,1,0:T(8,128)(2,1)S(1)}, bf16[48,48,256]{2,1,0:T(8,128)(2,1)}, u32[]{:S(2)}) copy-start(bf16[48,48,256]{2,1,0:T(8,128)(2,1)} %get-tuple-element.47) | copy-start | bytes 3538948

commit v4 on v3

v4 whole, which is shorter than its diff:
```python
import functools

import jax
import jax.numpy as jnp
from jax import lax
from jax.experimental import pallas as pl
from jax.experimental.pallas import tpu as pltpu
from jax.sharding import PartitionSpec as P

BAND = 1024
DMAX = 32
C = 48
ROWS = 72
COLS = 256
WIDE = 2 * COLS
LANES = 128
HALO = DMAX
CORNER = DMAX // 2
CHUNK = 24
PARTS = (((0, 24),), ((24, 48),))
PREP = 8
UNROLL = 8
STACK = 8
AXES = ("pos", "off")

SMEM = pl.BlockSpec(memory_space=pltpu.SMEM)
VMEM = pl.BlockSpec(memory_space=pltpu.VMEM)
ANY = pl.BlockSpec(memory_space=pl.ANY)
HBM = pl.BlockSpec(memory_space=pltpu.HBM)
PARAMS = pltpu.CompilerParams(vmem_limit_bytes=63 * 2**20)


def device(pair, x, z, core):
    return (2 * pair + core) * 8 + 2 * z + x


def home(stored, block):
    return device(stored // 2, block % 2, block // 2, stored % 2)


def place(strip, fold):
    stored = strip // 2
    return device(stored // 2, stored % 2, (4 - fold) % 4, strip % 2)


def lead(stored, fold):
    return (fold == 1) & (stored % 2 == 0) | (fold == 3) & (stored % 2 == 1)


CELLS = [(strip, fold) for strip in range(32) for fold in range(4)]


def routes(turn):
    out = []
    for strip, fold in CELLS:
        core, stored = strip % 2, strip // 2
        first = (core == int(lead(stored, fold))) == (turn == 0)
        out.append((home(stored, fold if first else 7 - fold), place(strip, fold)))
    return out


VIA = {(0, 1): (0, 0, 0), (0, 7): (0, 3, 0), (1, 2): (1, 1, 1), (1, 4): (1, 2, 1)}
STAY = ((0, 0), (0, 6), (1, 3), (1, 5))


def whereabouts():
    pos, off = lax.axis_index("pos"), lax.axis_index("off")
    fold = jnp.minimum(off, 7 - off)
    early = jnp.where(off < 4, 0, 1) ^ lead(pos, fold).astype(jnp.int32)
    stored = 2 * (pos // 2) + off % 2
    core = pos % 2
    work = (4 - off // 2) % 4
    order = core ^ lead(stored, work).astype(jnp.int32)
    values = (pos * 2 * ROWS, off, early, stored * 2 * ROWS + core * ROWS, work, order, core)
    values += (jnp.where(work == 3, 2, work % 2), core + 2 * (work % 2))
    return [v.astype(jnp.int32) for v in values]


STORED_ROW, STORED_BLOCK, EARLY, ROW, FOLD, ORDER, CORE, SIDE, KIND = range(9)


def choose(at_ref, index, cases):
    for value, case in enumerate(cases):
        pl.when(at_ref[index] == value)(case)


def threshold(limit_ref, row):
    last = limit_ref.shape[0] - 1
    return jnp.minimum(limit_ref[row], jnp.minimum(2 * row + 1, 2 * last - 2 * row))


def offsets(block, dims):
    return jnp.abs(lax.broadcasted_iota(jnp.int32, dims, len(dims) - 1) + (block * COLS - BAND))


def both_offsets(fold):
    return jnp.concatenate([offsets(fold, (C, COLS)), offsets(7 - fold, (C, COLS))], axis=1)


def shape(*dims):
    return jax.ShapeDtypeStruct(dims, jnp.bfloat16)


def enter_kernel(turn, at_ref, limit_ref, x_ref, out_ref):
    x = jnp.swapaxes(x_ref[...], 0, 1)
    away = offsets(at_ref[STORED_BLOCK], (C, COLS))
    row0 = at_ref[STORED_ROW] + (at_ref[EARLY] ^ turn) * ROWS
    for i in range(ROWS):
        seen = away <= threshold(limit_ref, row0 + i)
        out_ref[i] = jnp.where(seen, x[i], jnp.zeros((), jnp.bfloat16))


def enter(turn, at, row_limit, band_map):
    return pl.pallas_call(
        functools.partial(enter_kernel, turn),
        grid_spec=pltpu.PrefetchScalarGridSpec(
            num_scalar_prefetch=1,
            grid=(1,),
            in_specs=[SMEM, pl.BlockSpec((C, ROWS, COLS), lambda i, at_ref: (0, at_ref[EARLY] ^ turn, 0))],
            out_specs=pl.BlockSpec((ROWS, C, COLS), lambda i, at_ref: (0, 0, 0)),
        ),
        out_shape=shape(ROWS, C, COLS),
        compiler_params=PARAMS,
        name="enter",
    )(at, row_limit, band_map)


EDGES = [shape(ROWS, C, LANES)] * 2 + [shape(HALO, C, WIDE)] * 2


def edge_copies(cells, first, count, top, bottom):
    out = []
    for target, at in ((top, 0), (bottom, ROWS - HALO)):
        low, high = max(first, at), min(first + count, at + HALO)
        if low < high:
            out.append((cells.at[pl.ds(low - first, high - low)], target.at[pl.ds(low - at, high - low)]))
    return out


def inward_outward(cells, lane):
    return (
        jnp.where(lane < 64, cells[:, 2 * LANES : 3 * LANES], cells[:, LANES : 2 * LANES]),
        jnp.where(lane < 64, cells[:, :LANES], cells[:, 3 * LANES :]),
    )


def pack_kernel(at_ref, early_ref, late_ref, *refs):
    near, far, mate, other, blocks, into, back, sems = refs[-8:]
    lane = lax.broadcasted_iota(jnp.int32, (C, LANES), 1)
    runs = [pl.ds(i, CHUNK) for i in range(0, ROWS, CHUNK)]

    def work(first, second, inward, outward, top, bottom):
        n = 0

        def copy(src, dst):
            nonlocal n
            n += 1
            made = pltpu.make_async_copy(src, dst, sems.at[n - 1])
            made.start()
            return made

        here = [[copy(x.at[run], blocks.at[i, run]) for i, x in enumerate((first, second))] for run in runs]
        sent = []
        for at, run, loads in zip(range(0, ROWS, CHUNK), runs, here):
            for load in loads:
                load.wait()
            for i in range(at, at + CHUNK):
                a, b = blocks[0, i], blocks[1, i]
                into[i] = jnp.where(lane < 64, b[:, :LANES], a[:, LANES:])
                back[i] = jnp.where(lane < 64, a[:, :LANES], b[:, LANES:])
            sent += [copy(into.at[run], inward.at[run]), copy(back.at[run], outward.at[run])]
            for i in range(2):
                lanes = pl.ds(i * COLS, COLS)
                for src, dst in edge_copies(blocks.at[i, run], at, CHUNK, top, bottom):
                    sent.append(copy(src, dst.at[:, :, lanes]))
        for done in sent:
            done.wait()

    for order in range(2):

        def case(kind):
            cells = (late_ref, early_ref) if order else (early_ref, late_ref)
            edges = (far, near) if kind // 2 else (near, far)
            rows = (mate, other) if kind % 2 else (other, mate)
            return lambda: work(*cells, *edges, *rows)

        @pl.when(at_ref[ORDER] == order)
        def _():
            choose(at_ref, KIND, [case(kind) for kind in range(4)])


def pack(at, early, late, after):
    return pl.pallas_call(
        pack_kernel,
        in_specs=[SMEM] + [ANY] * (2 + len(after)),
        out_specs=[HBM] * 4,
        out_shape=EDGES,
        scratch_shapes=[
            pltpu.VMEM((2, ROWS, C, COLS), jnp.bfloat16),
            pltpu.VMEM((ROWS, C, LANES), jnp.bfloat16),
            pltpu.VMEM((ROWS, C, LANES), jnp.bfloat16),
            pltpu.SemaphoreType.DMA((96,)),
        ],
        compiler_params=PARAMS,
        name="pack",
    )(at, early, late, *after)


MATES = [(place(s, f), place(s ^ 1, f)) for s, f in CELLS]
OTHERS = [(place(s, f), place(t, f)) for s, f in CELLS for t in [s + 1 if s % 2 else s - 1] if 0 <= t < 32]
NEAR = [(place(s, f), place(s, f ^ 1)) for s, f in CELLS]
FAR = [(place(s, f), place(s, 3 - f)) for s, f in CELLS if f in (1, 2)]


def exchange(at, near, far, mate, other):
    beside = far
    near = lax.ppermute(near, AXES, NEAR)
    far = lax.ppermute(far, AXES, FAR)
    mate = lax.ppermute(mate, AXES, MATES)
    other = lax.ppermute(other, AXES, OTHERS)
    ends = lambda first: jnp.concatenate(
        [
            lax.dynamic_slice_in_dim(near, first, CORNER),
            jnp.where(at[FOLD] == 3, *[lax.dynamic_slice_in_dim(x, first, CORNER) for x in (beside, far)]),
        ],
        axis=0,
    )
    down = at[CORE] == 0
    corner_mate = lax.ppermute(ends(jnp.where(down, ROWS - CORNER, 0)), AXES, MATES)
    corner_other = lax.ppermute(ends(jnp.where(down, 0, ROWS - CORNER)), AXES, OTHERS)
    return (near, far, beside, mate, other), (corner_mate, corner_other)


def reach(runs):
    return runs[0][0] - HALO, sum(runs[-1]) + HALO


def needs_corners(runs):
    low, high = reach(runs)
    return low < CORNER - HALO or high > ROWS + HALO - CORNER


def conv_kernel(which, runs, extra, at_ref, d_ref, limit_ref, early_ref, late_ref, *refs):
    final = which == 1
    near, far, beside, mate, other, w_ref, b_ref = refs[:7]
    refs = refs[7:]
    if needs_corners(runs):
        (corner_mate, corner_other), refs = refs[:2], refs[2:]
    if final:
        hidden_ref, carried, refs = refs[0], refs[1 : 1 + extra], refs[1 + extra :]
        outs, scratch = refs[:4], refs[4:]
        out_ref, own, mid, before, behind, plus_ref, minus_ref, sems = scratch
    else:
        outs, scratch = refs[:5], refs[5:]
        out_ref, in_ref, back_ref, mid, before, behind, plus_ref, minus_ref, sems = scratch

    base, end = reach(runs)
    made = []

    def copy(src, dst):
        made.append(pltpu.make_async_copy(src, dst, sems.at[len(made)]))
        return made[-1]

    def fetch(src, low, high, target, shift):
        low, high = max(low, base), min(high, end)
        if low >= high:
            return []
        return [copy(src.at[pl.ds(low - shift, high - low)], target.at[pl.ds(low - base, high - low)])]

    def own_cells(low, count, target, at):
        rows, to = pl.ds(low, count), pl.ds(at, count)
        lanes = [pl.ds(i * COLS, COLS) for i in range(2)]
        return [
            [copy(x.at[rows], target.at[to, :, lane]) for x, lane in zip(pair, lanes)]
            for pair in ((early_ref, late_ref), (late_ref, early_ref))
        ]

    def each(choice, act):
        index, groups = choice

        def case(group):
            return lambda: [act(c) for c in group] and None

        choose(at_ref, index, [case(group) for group in groups])

    rows = [
        fetch(above, -HALO, 0, mid, -HALO) + fetch(below, ROWS, ROWS + HALO, mid, ROWS)
        for above, below in ((other, mate), (mate, other))
    ]
    sides = [
        fetch(near, 0, ROWS, a, 0) + fetch(x, 0, ROWS, b, 0)
        for a, b, x in ((behind, before, far), (before, behind, far), (before, behind, beside))
    ]
    choices = [(CORE, rows), (SIDE, sides)]
    if needs_corners(runs):
        ends = []
        for kind in range(4):
            above, below = (corner_mate, corner_other) if kind % 2 else (corner_other, corner_mate)
            a, b = (before, behind) if kind // 2 else (behind, before)
            ends.append(
                fetch(above, -CORNER, 0, a, -CORNER)
                + fetch(above, -CORNER, 0, b, -2 * CORNER)
                + fetch(below, ROWS, ROWS + CORNER, a, ROWS)
                + fetch(below, ROWS, ROWS + CORNER, b, ROWS - CORNER)
            )
        choices.append((KIND, ends))
    always = []
    later = []
    if final:
        always = fetch(hidden_ref, 0, ROWS, mid, 0)
        at = 0
        for first, count in runs:
            later.append((ORDER, own_cells(first, count, own, at)))
            at += count
    else:
        low, high = max(base, 0), min(end, ROWS)
        choices.append((ORDER, own_cells(low, high - low, mid, low - base)))
    for c in always:
        c.start()
    for choice in choices + later:
        each(choice, lambda c: c.start())
    for c in always:
        c.wait()
    for choice in choices:
        each(choice, lambda c: c.wait())

    d = d_ref[which]
    lo = d // 2
    hi = (d + 1) // 2
    odd = d - 2 * lo
    lane = lax.broadcasted_iota(jnp.int32, (C, LANES), 1)
    even_lane = (lane & 1) == 0

    def tiles(r):
        own = [mid[r, :, LANES * i : LANES * (i + 1)] for i in range(4)]
        return [before[r], *own[:2], behind[r], *own[2:]]

    def shifted(t, step, back):
        keep = lane < (step if back else LANES - step)
        turn = step if back else LANES - step
        left, a, b, right, c, e = t
        runs = ((left, a, b), (right, c, e)) if back else ((a, b, right), (c, e, left))
        out = []
        for run in runs:
            x, y, z = [pltpu.roll(v, turn, axis=1) for v in run]
            out += [jnp.where(keep, x, y), jnp.where(keep, y, z)]
        return jnp.concatenate(out, axis=1)

    for first, count in runs:
        start = first - base - hi

        def prepare(i, _):
            for j in range(PREP):
                r = start + i * PREP + j
                x, y = tiles(r), tiles(r + odd)
                both = [jnp.where(even_lane, b, a) for a, b in zip(x, y)]
                plus_ref[r] = shifted(both, d, False)
                minus_ref[r] = shifted(both, d, True)
            return 0

        lax.fori_loop(0, (count + d + PREP - 1) // PREP, prepare, 0)

    for choice in later:
        each(choice, lambda c: c.wait())
    weight = w_ref[...]
    bias = b_ref[...]
    away = both_offsets(at_ref[FOLD])
    row0 = at_ref[ROW]

    def row(ahead, m, _):
        r = m + ahead - base
        x = tiles(r)
        taps = [
            mid[r - d],
            plus_ref[r - hi],
            shifted(x, 2 * d, False),
            minus_ref[r - hi],
            mid[r],
            plus_ref[r + lo],
            shifted(x, 2 * d, True),
            minus_ref[r + lo],
            mid[r + d],
        ]
        acc = lax.dot_general(
            weight,
            jnp.concatenate(taps, axis=0),
            (((1,), (0,)), ((), ())),
            preferred_element_type=jnp.float32,
        )
        acc = acc + bias
        if final:
            acc = acc + own[m].astype(jnp.float32)
        else:
            acc = jnp.maximum(acc, 0.0)
        acc = jnp.where(away <= threshold(limit_ref, row0 + ahead + m), acc, 0.0).astype(jnp.bfloat16)
        out_ref[m] = acc
        if not final:
            in_ref[m], back_ref[m] = inward_outward(acc, lane)
        return 0

    if final:
        at = 0
        for first, count in runs:
            lax.fori_loop(at, at + count, functools.partial(row, first - at), 0, unroll=UNROLL)
            at += count
        mix(at_ref, limit_ref, runs, out_ref, carried, *outs, plus_ref)
        return
    hidden, to_near, to_far, to_mate, to_other = outs
    copies, ways = [], [[] for _ in range(4)]
    for at in range(0, ROWS, CHUNK):
        lax.fori_loop(at, at + CHUNK, functools.partial(row, 0), 0, unroll=UNROLL)
        run = pl.ds(at, CHUNK)
        copies.append(copy(out_ref.at[run], hidden.at[run]))
        copies[-1].start()
        more = []
        for kind in range(4):
            top, bottom = (to_mate, to_other) if kind % 2 else (to_other, to_mate)
            inward, outward = (to_far, to_near) if kind // 2 else (to_near, to_far)
            pairs = [(in_ref.at[run], inward.at[run]), (back_ref.at[run], outward.at[run])]
            pairs += edge_copies(out_ref.at[run], at, CHUNK, top, bottom)
            more.append([copy(a, b) for a, b in pairs])
        each((KIND, more), lambda c: c.start())
        for way, group in zip(ways, more):
            way += group
    for c in copies:
        c.wait()
    each((KIND, ways), lambda c: c.wait())


def mix(at_ref, limit_ref, runs, summed, carried, first_ref, second_ref, edge_ref, other_ref, rows_ref):
    a = lax.broadcasted_iota(jnp.int32, (COLS, COLS), 0)
    b = lax.broadcasted_iota(jnp.int32, (COLS, COLS), 1)
    turn = (a + b == COLS).astype(jnp.bfloat16)
    lane = lax.broadcasted_iota(jnp.int32, (C, LANES), 1)
    away = both_offsets(at_ref[FOLD])
    row0 = at_ref[ROW]
    rows = [first + i for first, count in runs for i in range(count)]
    swap = at_ref[CORE] == 0
    edges = [jnp.zeros((C, LANES), jnp.bfloat16)] * 2
    if carried:
        edge, other = carried[0][...], carried[1][...]
        edges = [jnp.where(swap, other, edge), jnp.where(swap, edge, other)]
    for group in range(len(rows) // STACK):
        at = group * STACK
        cells = summed[pl.ds(at, STACK)].reshape(STACK * C, WIDE)
        blocks = cells[:, :COLS], cells[:, COLS:]
        turned = [jnp.dot(x, turn, preferred_element_type=jnp.float32) for x in blocks]
        for i in range(2):
            mean = 0.5 * (blocks[i].astype(jnp.float32) + turned[1 - i])
            for j in range(STACK):
                m = at + j
                part = slice(C * j, C * (j + 1))
                seen = away[:, COLS * i : COLS * (i + 1)] <= threshold(limit_ref, row0 + rows[m])
                rows_ref[m, :, COLS * i : COLS * (i + 1)] = jnp.where(seen, mean[part], 0.0).astype(jnp.bfloat16)
                tile = blocks[i][part, :LANES]
                tile = pltpu.roll(tile, rows[m], axis=1) if rows[m] else tile
                edges[i] = jnp.where(lane == rows[m], tile, edges[i])
    edge_ref[...] = jnp.where(swap, edges[1], edges[0])
    other_ref[...] = jnp.where(swap, edges[0], edges[1])
    early = at_ref[ORDER] == 0

    @pl.when(early)
    def _():
        first_ref[...] = jnp.swapaxes(rows_ref[pl.ds(0, len(rows)), :, :COLS], 0, 1)
        second_ref[...] = jnp.swapaxes(rows_ref[pl.ds(0, len(rows)), :, COLS:], 0, 1)

    @pl.when(jnp.logical_not(early))
    def _():
        first_ref[...] = jnp.swapaxes(rows_ref[pl.ds(0, len(rows)), :, COLS:], 0, 1)
        second_ref[...] = jnp.swapaxes(rows_ref[pl.ds(0, len(rows)), :, :COLS], 0, 1)


def conv(at, d, row_limit, own, halos, corners, weight, bias, hidden=None, runs=((0, ROWS),), carried=()):
    final = hidden is not None
    count = sum(n for _, n in runs)
    low, high = reach(runs)
    args = [at, d, row_limit, *own, *halos, weight, bias]
    in_specs = [SMEM] * 3 + [ANY] * 7 + [VMEM] * 2
    if needs_corners(runs):
        args += corners
        in_specs += [ANY] * 2
    if final:
        args += [hidden, *carried]
        in_specs += [ANY] + [VMEM] * len(carried)
    out_shape = [shape(C, count, COLS)] * 2 + [shape(C, LANES)] * 2 if final else [shape(ROWS, C, WIDE)] + EDGES
    scratch = [pltpu.VMEM((count, C, n), jnp.bfloat16) for n in ((WIDE, WIDE) if final else (WIDE, LANES, LANES))]
    return pl.pallas_call(
        functools.partial(conv_kernel, int(final), runs, len(carried)),
        in_specs=in_specs,
        out_specs=[VMEM if final else HBM] * len(out_shape),
        out_shape=out_shape,
        scratch_shapes=scratch
        + [pltpu.VMEM((high - low, C, n), jnp.bfloat16) for n in (WIDE, LANES, LANES, WIDE, WIDE)]
        + [pltpu.SemaphoreType.DMA((96,))],
        compiler_params=PARAMS,
        name="second" if final else "first",
    )(*args)


def behind_kernel(*refs):
    del refs


def behind(cells):
    return pl.pallas_call(
        behind_kernel,
        in_specs=[ANY] * len(cells),
        out_specs=[ANY] * len(cells),
        out_shape=[shape(*x.shape) for x in cells],
        input_output_aliases={i: i for i in range(len(cells))},
        compiler_params=PARAMS,
        name="behind",
    )(*cells)


def flat(weight):
    return jnp.transpose(weight, (1, 0, 2)).reshape(C, 9 * C)


def local(band_map, dilations, row_limit, weight_one, bias_one, weight_two, bias_two):
    at = whereabouts()
    vector = jnp.stack(at)
    early, late = routes(0), routes(1)

    own = [lax.ppermute(enter(i, vector, row_limit, band_map), AXES, routes(i)) for i in range(2)]
    weights = [flat(weight_one), flat(weight_two)]
    biases = [bias_one[:, None], bias_two[:, None]]
    halos, corners = exchange(at, *pack(vector, *own, weights + biases))
    hidden, *edges = conv(vector, dilations, row_limit, own, halos, corners, weights[0], biases[0])
    halos, corners = exchange(at, *edges)

    pos, off = lax.axis_index("pos"), lax.axis_index("off")
    here = lambda pairs: functools.reduce(jnp.logical_or, [(pos % 2 == s) & (off == b) for s, b in pairs])
    stays, relayed = here(STAY), here(VIA)
    kept = [(to, at_work) for to, at_work in late if (to // 8 % 2, to % 8) in STAY]
    lends = functools.reduce(jnp.logical_or, [(pos == a // 8) & (off == a % 8) for _, a in kept])

    def relay(pairs, turn):
        leave, arrive = [], []
        for to, at_work in pairs:
            stored, block = to // 8, to % 8
            if (stored % 2, block) in VIA:
                via = device(stored // 2, *VIA[stored % 2, block])
                leave.append((at_work, via))
                arrive.append((via, to))
            elif (stored % 2, block) not in STAY:
                leave.append((at_work, to))
            elif turn:
                arrive.append((at_work, to))
        return leave, arrive

    leave, arrive = relay(early, 0)
    leave_late, arrive_late = relay(late, 1)

    def second(rows, carried):
        return conv(
            vector, dilations, row_limit, own, halos, corners, weights[1], biases[1], hidden, rows, carried
        )

    def sorted_out(first, passed, ended):
        return jnp.where(stays, first, jnp.where(relayed, ended, passed))

    first, late_first, *carried = second(PARTS[0], [])
    passed = lax.ppermute(first, AXES, leave)
    through = lax.ppermute(late_first, AXES, leave_late)
    more, late_more, *carried = second(PARTS[1], carried)
    passed, through, more, late_more, edge, other = behind((passed, through, more, late_more, *carried))
    passed_more = lax.ppermute(more, AXES, leave)
    direct = lax.ppermute(late_more, AXES, [(b, a) for a, b in late])
    ended = lax.ppermute(passed, AXES, arrive)
    ended_late = lax.ppermute(jnp.where(lends, late_first, through), AXES, arrive_late)
    ended_more = lax.ppermute(passed_more, AXES, arrive)
    gots = [sorted_out(first, passed, ended), sorted_out(more, passed_more, ended_more)]
    directs = [jnp.where(stays | relayed, ended_late, through), direct]

    to_first = lambda core: [(place(s, f), home(s // 2, f + 1)) for s, f in CELLS if s % 2 == core]
    to_second = lambda core: [(place(s, f), home(s // 2, 8 - f)) for s, f in CELLS if s % 2 == core and f]
    edge = lax.ppermute(edge, AXES, to_first(0) + to_second(1))
    other = lax.ppermute(other, AXES, to_second(0) + to_first(1))
    low = at[STORED_BLOCK] <= 4
    halves = jnp.where(low, edge, other), jnp.where(low, other, edge)
    top_first = at[EARLY] == 0
    column = lax.broadcasted_iota(jnp.int32, (1, 1, COLS), 2)
    out = []
    for half in range(2):
        pieces = []
        for runs, *pair in zip(PARTS, gots, directs):
            got = jnp.where(top_first, *(pair if half == 0 else pair[::-1]))
            at_row = 0
            for start, count in runs:
                cells = lax.slice_in_dim(got, at_row, at_row + count, axis=1)
                edge = lax.slice_in_dim(halves[half], start, start + count, axis=1)[:, :, None]
                more = (cells.astype(jnp.float32) + 0.5 * edge.astype(jnp.float32)).astype(jnp.bfloat16)
                pieces.append((start, jnp.where(column == 0, more, cells)))
                at_row += count
        out += [piece for _, piece in sorted(pieces, key=lambda x: x[0])]
    return jnp.concatenate(out, axis=1)


def solution(mesh):
    in_specs = (P(None, "pos", "off"), P(), P(), P(), P(), P(), P())
    out_specs = P(None, "pos", "off")
    return jax.shard_map(local, mesh=mesh, in_specs=in_specs, out_specs=out_specs, check_vma=False)
```

time: 247 us -> 241 us (0.976)
  starting transfers between devices: 67.1 us -> 58.8 us
  waiting for transfers between devices: 109 us -> 102 us
  Pallas kernels: 57.4 us -> 60.6 us
  other arithmetic: 5.02 us -> 7.68 us
    ppermute x16 -> x19, waiting for transfers between devices: 66.3 us -> 98.4 us  [the longest x2 31.8 us: exchange(): far = lax.ppermute(far, AXES, FAR)]
    ppermute x2 -> x1, waiting for transfers between devices: 26.7 us -> 0.01 us  [local(): passed = lax.ppermute(first, AXES, leave)]
    ppermute x2 -> x1, waiting for transfers between devices: 15 us -> 3.37 us  [local(): ended = lax.ppermute(passed, AXES, arrive)]
    ppermute x2 -> x1, starting transfers between devices: 12.5 us -> 5.59 us  [local(): passed = lax.ppermute(first, AXES, leave)]
    pallas_call x4, Pallas kernels: 44 us -> 47.7 us  [the longest x3 47.7 us: conv(): pl.pallas_call(functools.partial(conv_kernel, int(final), runs, len(carri...]
    select_n x6 -> x7, other arithmetic: 2.76 us -> 5.42 us  [the longest x2 2.8 us: exchange(): jnp.where(at[FOLD] == 3, *[lax.dynamic_slice_in_dim(x, first, CORNER) for...]
    ppermute x16 -> x19, starting transfers between devices: 47.7 us -> 47.6 us  [the longest x2 14.4 us: local(): lax.ppermute(enter(i, vector, row_limit, band_map), AXES, routes(i))]
  transfers between devices with their start and end apart: 22 -> 23, of which waited for: 14 -> 11; matrix products, arithmetic and copies ran while one was open for 2% -> 3% of each run, Pallas kernels for 8% -> 9%
where the time goes in v4:
time: 241 us; the launch traced here: 236 us
  waiting for transfers between devices  102 us (42%)
  Pallas kernels  60.6 us (25%)
  starting transfers between devices  58.8 us (24%)
  other arithmetic  7.68 us (3%)
  local copies, waits for them, and re-layouts  6.36 us (3%)
    pallas_call x3, Pallas kernels, conv(): pl.pallas_call(functools.partial(conv_kernel, int(final), runs, len(carri...  47.7 us
    ppermute x2, waiting for transfers between devices, exchange(): far = lax.ppermute(far, AXES, FAR)  31.8 us
    ppermute x2, waiting for transfers between devices, local(): lax.ppermute(enter(i, vector, row_limit, band_map), AXES, routes(i))  21.3 us
    ppermute x2, starting transfers between devices, local(): lax.ppermute(enter(i, vector, row_limit, band_map), AXES, routes(i))  14.4 us
    ppermute x1, waiting for transfers between devices, local(): direct = lax.ppermute(late_more, AXES, [(b, a) for a, b in late])  13.5 us
    ppermute x1, waiting for transfers between devices, local(): ended_more = lax.ppermute(passed_more, AXES, arrive)  11.2 us
    ppermute x2, waiting for transfers between devices, exchange(): lax.ppermute(ends(jnp.where(down, 0, ROWS - CORNER)), AXES, OTHERS)  10.7 us
    ppermute x1, waiting for transfers between devices, local(): passed_more = lax.ppermute(more, AXES, leave)  8.37 us
  transfers between devices with their start and end apart: 23, of which 11 were waited for; matrix products, arithmetic and copies ran while one was open for 3% of the time, Pallas kernels for 9%

profile of v4, /device:TPU:118, one launch (start us, length us, event | category | flops | bytes accessed | tf_op | source)
XLA Modules:
  0.0 235.9 jit_solution(13607486076335173604)
XLA Ops:
  0.0 0.6 stack.39.at_ref
  0.6 3.9 %enter.2 = bf16[72,48,256]{2,1,0:T(8,128)(2,1)} custom-call(s32[9]{0:T(128)} %stack.39.at_ref, s32[2304]{0:T(1024)} %limit_ref.9, bf16[48,144,256]{2,1,0:T(8,128)(2,1)} %x_ref.3), custom_call_target="tpu_custom_call" | custom-call | tf_op jit(solution)/shard_map/enter/pallas_call | solution.py:114
  4.5 2.1 collective-permute-start
  6.6 3.9 %enter.3 = bf16[72,48,256]{2,1,0:T(8,128)(2,1)} custom-call(s32[9]{0:T(128)} %stack.39.at_ref, s32[2304]{0:T(1024)} %limit_ref.9, bf16[48,144,256]{2,1,0:T(8,128)(2,1)} %x_ref.3), custom_call_target="tpu_custom_call" | custom-call | tf_op jit(solution)/shard_map/enter/pallas_call | solution.py:114
  10.5 12.4 %collective-permute-start.1 = (bf16[72,48,256]{2,1,0:T(8,128)(2,1)}, bf16[72,48,256]{2,1,0:T(8,128)(2,1)}, u32[]{:S(2)}, u32[]{:S(2)}) collective-permute-start(bf16[72,48,256]{2,1,0:T(8,128)(2,1)} %enter.3), channel_id=1, source_target_pairs={{7,0},{1,6},{5,4},{4,2},{0,8},{6,14},{2,12},{3,10},{15,1},{14,7},{... | collective-permute-start | bytes 5308424 | tf_op jit(solution)/shard_map/ppermute | solution.py:525
  22.9 0.1 copy.22
  23.0 0.7 copy.24.refs_1_.refs_5_
  23.7 0.7 copy.26.refs_3_.refs_6_
  24.4 0.1 copy.21
  24.5 0.7 copy.23.refs_0_.refs_5_
  25.3 0.7 copy.25.refs_2_.refs_6_
  25.9 4.1 %collective-permute-done.early_ref = bf16[72,48,256]{2,1,0:T(8,128)(2,1)} collective-permute-done((bf16[72,48,256]{2,1,0:T(8,128)(2,1)}, bf16[72,48,256]{2,1,0:T(8,128)(2,1)}, u32[]{:S(2)}, u32[]{:S(2)}) %collective-permute-start) | collective-permute-done | bytes 1769504 | tf_op jit(solution)/shard_map/ppermute | solution.py:525
  30.0 17.2 %collective-permute-done.1.late_ref = bf16[72,48,256]{2,1,0:T(8,128)(2,1)} collective-permute-done((bf16[72,48,256]{2,1,0:T(8,128)(2,1)}, bf16[72,48,256]{2,1,0:T(8,128)(2,1)}, u32[]{:S(2)}, u32[]{:S(2)}) %collective-permute-start.1) | collective-permute-done | bytes 1769504 | tf_op jit(solution)/shard_map/ppermute | solution.py:525
  47.2 5.1 %pack.1 = (bf16[72,48,128]{2,1,0:T(8,128)(2,1)}, bf16[72,48,128]{2,1,0:T(8,128)(2,1)}, bf16[32,48,512]{2,1,0:T(8,128)(2,1)}, bf16[32,48,512]{2,1,0:T(8,128)(2,1)}) custom-call(s32[9]{0:T(128)} %stack.39.at_ref, bf16[72,48,256]{2,1,0:T(8,128)(2,1)} %collective-permute-done.early_ref, bf16[72,48,256]{2,1,0:T(8,128)(2,1)} %collective-permute-done.1.late_ref, ...), custom_call_target="tpu_custom_call" | custom-call | tf_op jit(solution)/shard_map/pack/pallas_call | solution.py:193
  52.3 1.9 collective-permute-start.3
  54.3 0.5 collective-permute-start.2
  54.7 1.4 collective-permute-start.4
  56.1 3.9 %collective-permute-start.5 = (bf16[32,48,512]{2,1,0:T(8,128)(2,1)}, bf16[32,48,512]{2,1,0:T(8,128)(2,1)}, u32[]{:S(2)}, u32[]{:S(2)}) collective-permute-start(bf16[32,48,512]{2,1,0:T(8,128)(2,1)} %get-tuple-element.31), channel_id=1, source_target_pairs={{8,1},{14,7},{12,5},{10,3},{1,8},{7,14},{5,12},{3,10},{9,16},{15,2... | collective-permute-start | bytes 4718600 | tf_op jit(solution)/shard_map/ppermute | solution.py:220
  60.0 16.3 %collective-permute-done.3.refs_1_ = bf16[72,48,128]{2,1,0:T(8,128)(2,1)S(1)} collective-permute-done((bf16[72,48,128]{2,1,0:T(8,128)(2,1)}, bf16[72,48,128]{2,1,0:T(8,128)(2,1)S(1)}, u32[]{:S(2)}, u32[]{:S(2)}) %collective-permute-start.3) | collective-permute-done | bytes 884768 | tf_op jit(solution)/shard_map/ppermute | solution.py:218
  76.3 1.4 dynamic-slice_select_fusion.2
  77.7 0.0 collective-permute-done.2.refs_0_
  77.8 1.9 collective-permute-start.7
  79.8 2.1 collective-permute-start.6
  81.9 5.0 %collective-permute-done.7.refs_8_ = bf16[32,48,128]{2,1,0:T(8,128)(2,1)S(1)} collective-permute-done((bf16[32,48,128]{2,1,0:T(8,128)(2,1)S(1)}, bf16[32,48,128]{2,1,0:T(8,128)(2,1)S(1)}, u32[]{:S(2)}, u32[]{:S(2)}) %collective-permute-start.7) | collective-permute-done | bytes 393248 | tf_op jit(solution)/shard_map/ppermute | solution.py:230
  86.9 0.7 copy-done.10
  87.7 0.1 copy-done.11
  87.8 19.4 %first.1 = (bf16[72,48,512]{2,1,0:T(8,128)(2,1)}, bf16[72,48,128]{2,1,0:T(8,128)(2,1)}, bf16[72,48,128]{2,1,0:T(8,128)(2,1)}, bf16[32,48,512]{2,1,0:T(8,128)(2,1)}, bf16[32,48,512]{2,1,0:T(8,128)(2,1)}) custom-call(s32[9]{0:T(128)} %stack.39.at_ref, s32[2]{0:T(128)} %d_ref.5, s32[2304]{0:T(1024)} %limit_ref.9, ...), custom_call_target="tpu_custom_call" | custom-call | tf_op jit(solution)/shard_map/first/pallas_call | solution.py:487
  107.2 2.9 %collective-permute-start.9 = (bf16[72,48,128]{2,1,0:T(8,128)(2,1)}, bf16[72,48,128]{2,1,0:T(8,128)(2,1)S(1)}, u32[]{:S(2)}, u32[]{:S(2)}) collective-permute-start(bf16[72,48,128]{2,1,0:T(8,128)(2,1)} %get-tuple-element.33.refs_2_), channel_id=1, source_target_pairs={{6,4},{4,6},{14,12},{12,14},{7,5},{5,7},{15,13},{13,15},{22,20},{2... | collective-permute-start | bytes 2654216 | tf_op jit(solution)/shard_map/ppermute | solution.py:218
  110.1 0.1 collective-permute-start.8
  110.2 2.3 collective-permute-start.10
  112.5 1.9 collective-permute-start.11
  114.4 15.4 %collective-permute-done.9.refs_1_ = bf16[72,48,128]{2,1,0:T(8,128)(2,1)S(1)} collective-permute-done((bf16[72,48,128]{2,1,0:T(8,128)(2,1)}, bf16[72,48,128]{2,1,0:T(8,128)(2,1)S(1)}, u32[]{:S(2)}, u32[]{:S(2)}) %collective-permute-start.9) | collective-permute-done | bytes 884768 | tf_op jit(solution)/shard_map/ppermute | solution.py:218
  129.9 1.4 dynamic-slice_select_fusion
  131.3 1.5 collective-permute-done.8.refs_0_
  132.9 1.9 collective-permute-start.13
  134.9 1.5 collective-permute-start.12
  136.4 5.7 %collective-permute-done.13.refs_8_ = bf16[32,48,128]{2,1,0:T(8,128)(2,1)S(1)} collective-permute-done((bf16[32,48,128]{2,1,0:T(8,128)(2,1)S(1)}, bf16[32,48,128]{2,1,0:T(8,128)(2,1)S(1)}, u32[]{:S(2)}, u32[]{:S(2)}) %collective-permute-start.13) | collective-permute-done | bytes 393248 | tf_op jit(solution)/shard_map/ppermute | solution.py:230
  142.0 0.7 copy-done.7
  142.8 0.1 copy-done.8
  142.9 11.6 %second.2 = (bf16[48,24,256]{2,1,0:T(8,128)(2,1)}, bf16[48,24,256]{2,1,0:T(8,128)(2,1)}, bf16[48,128]{1,0:T(8,128)(2,1)}, bf16[48,128]{1,0:T(8,128)(2,1)}) custom-call(s32[9]{0:T(128)} %stack.39.at_ref, s32[2]{0:T(128)} %d_ref.5, s32[2304]{0:T(1024)} %limit_ref.9, bf16[72,48,256]{2,1,0:T(8,128)(2,1)} %collective-permute-done.early_ref, ...), custom_call_target="tpu_custom_call" | custom-call | tf_op jit(solution)/shard_map/second/pallas_call | solution.py:487
  154.5 5.6 %collective-permute-start.14 = (bf16[48,24,256]{2,1,0:T(8,128)(2,1)}, bf16[48,24,256]{2,1,0:T(8,128)(2,1)}, u32[]{:S(2)}, u32[]{:S(2)}) collective-permute-start(bf16[48,24,256]{2,1,0:T(8,128)(2,1)} %get-tuple-element.37), channel_id=1, source_target_pairs={{4,2},{2,3},{8,6},{14,0},{12,5},{10,4},{1,8},{7,9},{5,11},{3,13},{... | collective-permute-start | bytes 1769480 | tf_op jit(solution)/shard_map/ppermute | solution.py:564
  160.1 1.3 collective-permute-start.15
  161.4 16.8 %second.3 = (bf16[48,48,256]{2,1,0:T(8,128)(2,1)}, bf16[48,48,256]{2,1,0:T(8,128)(2,1)}, bf16[48,128]{1,0:T(8,128)(2,1)}, bf16[48,128]{1,0:T(8,128)(2,1)}) custom-call(s32[9]{0:T(128)} %stack.39.at_ref, s32[2]{0:T(128)} %d_ref.5, s32[2304]{0:T(1024)} %limit_ref.9, bf16[72,48,256]{2,1,0:T(8,128)(2,1)} %collective-permute-done.early_ref, ...), custom_call_target="tpu_custom_call" | custom-call | tf_op jit(solution)/shard_map/second/pallas_call | solution.py:487
  178.2 0.0 copy-start
  178.2 0.8 copy-done
  179.1 4.8 %collective-permute-start.20 = (bf16[48,48,256]{2,1,0:T(8,128)(2,1)}, bf16[48,48,256]{2,1,0:T(8,128)(2,1)S(1)}, u32[]{:S(2)}, u32[]{:S(2)}) collective-permute-start(bf16[48,48,256]{2,1,0:T(8,128)(2,1)} %get-tuple-element.49), channel_id=1, source_target_pairs={{4,2},{2,3},{8,6},{14,0},{12,5},{10,4},{1,8},{7,9},{5,11},{3,13},{... | collective-permute-start | bytes 3538952 | tf_op jit(solution)/shard_map/ppermute | solution.py:568
  184.2 2.4 %collective-permute-start.18 = (bf16[48,128]{1,0:T(8,128)(2,1)}, bf16[48,128]{1,0:T(8,128)(2,1)S(1)}, u32[]{:S(2)}, u32[]{:S(2)}) collective-permute-start(bf16[48,128]{1,0:T(8,128)(2,1)} %get-tuple-element.47), channel_id=1, source_target_pairs={{0,1},{6,2},{4,3},{2,4},{1,9},{7,10},{5,11},{3,12},{16,17},{22,18}... | collective-permute-start | bytes 36872 | tf_op jit(solution)/shard_map/ppermute | solution.py:578
  186.5 1.9 collective-permute-start.19
  188.5 1.1 broadcast_select_fusion
  189.6 1.3 collective-permute-start.17
  190.9 1.3 collective-permute-start.16
  192.2 2.3 collective-permute-start.22
  194.5 8.4 %collective-permute-done.20 = bf16[48,48,256]{2,1,0:T(8,128)(2,1)S(1)} collective-permute-done((bf16[48,48,256]{2,1,0:T(8,128)(2,1)}, bf16[48,48,256]{2,1,0:T(8,128)(2,1)S(1)}, u32[]{:S(2)}, u32[]{:S(2)}) %collective-permute-start.20) | collective-permute-done | bytes 1179680 | tf_op jit(solution)/shard_map/ppermute | solution.py:568
  202.9 1.3 collective-permute-start.21
  204.2 0.1 convert_multiply_fusion.2
  204.3 0.1 convert_multiply_fusion
  204.3 3.4 %collective-permute-done.16 = bf16[48,24,256]{2,1,0:T(8,128)(2,1)S(1)} collective-permute-done((bf16[48,24,256]{2,1,0:T(8,128)(2,1)}, bf16[48,24,256]{2,1,0:T(8,128)(2,1)S(1)}, u32[]{:S(2)}, u32[]{:S(2)}) %collective-permute-start.16) | collective-permute-done | bytes 589856 | tf_op jit(solution)/shard_map/ppermute | solution.py:570
  207.7 0.3 fusion.2
  208.0 0.2 fusion.3
  208.3 13.5 %collective-permute-done.22 = bf16[48,48,256]{2,1,0:T(8,128)(2,1)S(1)} collective-permute-done((bf16[48,48,256]{2,1,0:T(8,128)(2,1)S(1)}, bf16[48,48,256]{2,1,0:T(8,128)(2,1)S(1)}, u32[]{:S(2)}, u32[]{:S(2)}) %collective-permute-start.22) | collective-permute-done | bytes 1179680 | tf_op jit(solution)/shard_map/ppermute | solution.py:569
  221.8 11.2 %collective-permute-done.21 = bf16[48,48,256]{2,1,0:T(8,128)(2,1)S(1)} collective-permute-done((bf16[48,48,256]{2,1,0:T(8,128)(2,1)S(1)}, bf16[48,48,256]{2,1,0:T(8,128)(2,1)S(1)}, u32[]{:S(2)}, u32[]{:S(2)}) %collective-permute-start.21) | collective-permute-done | bytes 1179680 | tf_op jit(solution)/shard_map/ppermute | solution.py:572
  233.0 0.5 fusion
  233.5 0.4 fusion.1
  234.0 1.9 pad_maximum_fusion
  (48 shorter events, 0.3 us)
Async XLA Ops:
  4.5 18.4 %copy-start.12 = (bf16[9,48,48]{2,1,0:T(8,128)(2,1)S(1)}, bf16[9,48,48]{2,1,0:T(8,128)(2,1)}, u32[]{:S(2)}) copy-start(bf16[9,48,48]{2,1,0:T(8,128)(2,1)} %param.12) | copy-start | bytes 124420
  4.5 19.2 %copy-start.14 = (f32[48]{0:T(128)S(1)}, f32[48]{0:T(128)}, u32[]{:S(2)}) copy-start(f32[48]{0:T(128)} %param.13) | copy-start | bytes 580
  4.5 19.9 %copy-start.13 = (bf16[9,48,48]{2,1,0:T(8,128)(2,1)S(1)}, bf16[9,48,48]{2,1,0:T(8,128)(2,1)}, u32[]{:S(2)}) copy-start(bf16[9,48,48]{2,1,0:T(8,128)(2,1)} %param.10) | copy-start | bytes 124420
  4.5 20.7 %copy-start.15 = (f32[48]{0:T(128)S(1)}, f32[48]{0:T(128)}, u32[]{:S(2)}) copy-start(f32[48]{0:T(128)} %param.11) | copy-start | bytes 580
  4.5 25.5 %collective-permute-start = (bf16[72,48,256]{2,1,0:T(8,128)(2,1)}, bf16[72,48,256]{2,1,0:T(8,128)(2,1)}, u32[]{:S(2)}, u32[]{:S(2)}) collective-permute-start(bf16[72,48,256]{2,1,0:T(8,128)(2,1)} %enter.2), channel_id=1, source_target_pairs={{0,0},{6,6},{2,4},{3,2},{7,8},{1,14},{5,12},{4,10},{8,1},{9,7},{10... | collective-permute-start | bytes 5308424 | tf_op jit(solution)/shard_map/ppermute | solution.py:525
  10.5 36.7 %collective-permute-start.1 = (bf16[72,48,256]{2,1,0:T(8,128)(2,1)}, bf16[72,48,256]{2,1,0:T(8,128)(2,1)}, u32[]{:S(2)}, u32[]{:S(2)}) collective-permute-start(bf16[72,48,256]{2,1,0:T(8,128)(2,1)} %enter.3), channel_id=1, source_target_pairs={{7,0},{1,6},{5,4},{4,2},{0,8},{6,14},{2,12},{3,10},{15,1},{14,7},{... | collective-permute-start | bytes 5308424 | tf_op jit(solution)/shard_map/ppermute | solution.py:525
  52.3 24.0 %collective-permute-start.3 = (bf16[72,48,128]{2,1,0:T(8,128)(2,1)}, bf16[72,48,128]{2,1,0:T(8,128)(2,1)S(1)}, u32[]{:S(2)}, u32[]{:S(2)}) collective-permute-start(bf16[72,48,128]{2,1,0:T(8,128)(2,1)} %get-tuple-element.29.refs_2_), channel_id=1, source_target_pairs={{6,4},{4,6},{14,12},{12,14},{7,5},{5,7},{15,13},{13,15},{22,20},{2... | collective-permute-start | bytes 2654216 | tf_op jit(solution)/shard_map/ppermute | solution.py:218
  54.3 23.5 %collective-permute-start.2 = (bf16[72,48,128]{2,1,0:T(8,128)(2,1)}, bf16[72,48,128]{2,1,0:T(8,128)(2,1)S(1)}, u32[]{:S(2)}, u32[]{:S(2)}) collective-permute-start(bf16[72,48,128]{2,1,0:T(8,128)(2,1)} %get-tuple-element.28), channel_id=1, source_target_pairs={{0,6},{6,0},{4,2},{2,4},{8,14},{14,8},{12,10},{10,12},{1,7},{7,1},... | collective-permute-start | bytes 2654216 | tf_op jit(solution)/shard_map/ppermute | solution.py:217
  54.7 32.2 %collective-permute-start.4 = (bf16[32,48,512]{2,1,0:T(8,128)(2,1)}, bf16[32,48,512]{2,1,0:T(8,128)(2,1)}, u32[]{:S(2)}, u32[]{:S(2)}) collective-permute-start(bf16[32,48,512]{2,1,0:T(8,128)(2,1)} %get-tuple-element.30), channel_id=1, source_target_pairs={{0,8},{6,14},{4,12},{2,10},{8,0},{14,6},{12,4},{10,2},{1,9},{7,15}... | collective-permute-start | bytes 4718600 | tf_op jit(solution)/shard_map/ppermute | solution.py:219
  56.1 30.9 %collective-permute-start.5 = (bf16[32,48,512]{2,1,0:T(8,128)(2,1)}, bf16[32,48,512]{2,1,0:T(8,128)(2,1)}, u32[]{:S(2)}, u32[]{:S(2)}) collective-permute-start(bf16[32,48,512]{2,1,0:T(8,128)(2,1)} %get-tuple-element.31), channel_id=1, source_target_pairs={{8,1},{14,7},{12,5},{10,3},{1,8},{7,14},{5,12},{3,10},{9,16},{15,2... | collective-permute-start | bytes 4718600 | tf_op jit(solution)/shard_map/ppermute | solution.py:220
  76.3 3.5 %copy-start.5 = (bf16[72,48,128]{2,1,0:T(8,128)(2,1)}, bf16[72,48,128]{2,1,0:T(8,128)(2,1)S(1)}, u32[]{:S(2)}) copy-start(bf16[72,48,128]{2,1,0:T(8,128)(2,1)S(1)} %collective-permute-done.3.refs_1_) | copy-start | bytes 2654212
  77.7 4.2 %copy-start.6 = (bf16[72,48,128]{2,1,0:T(8,128)(2,1)}, bf16[72,48,128]{2,1,0:T(8,128)(2,1)S(1)}, u32[]{:S(2)}) copy-start(bf16[72,48,128]{2,1,0:T(8,128)(2,1)S(1)} %collective-permute-done.2.refs_0_) | copy-start | bytes 2654212
  77.8 9.1 %collective-permute-start.7 = (bf16[32,48,128]{2,1,0:T(8,128)(2,1)S(1)}, bf16[32,48,128]{2,1,0:T(8,128)(2,1)S(1)}, u32[]{:S(2)}, u32[]{:S(2)}) collective-permute-start(bf16[32,48,128]{2,1,0:T(8,128)(2,1)S(1)} %pad_maximum_fusion.2), channel_id=1, source_target_pairs={{8,1},{14,7},{12,5},{10,3},{1,8},{7,14},{5,12},{3,10},{9,16},{15,2... | collective-permute-start | bytes 1179656 | tf_op jit(solution)/shard_map/ppermute | solution.py:230
  79.8 7.1 %collective-permute-start.6 = (bf16[32,48,128]{2,1,0:T(8,128)(2,1)S(1)}, bf16[32,48,128]{2,1,0:T(8,128)(2,1)S(1)}, u32[]{:S(2)}, u32[]{:S(2)}) collective-permute-start(bf16[32,48,128]{2,1,0:T(8,128)(2,1)S(1)} %pad_maximum_fusion.1), channel_id=1, source_target_pairs={{0,8},{6,14},{4,12},{2,10},{8,0},{14,6},{12,4},{10,2},{1,9},{7,15}... | collective-permute-start | bytes 1179656 | tf_op jit(solution)/shard_map/ppermute | solution.py:229
  86.9 0.7 copy-start.10
  86.9 0.9 copy-start.11
  107.2 22.7 %collective-permute-start.9 = (bf16[72,48,128]{2,1,0:T(8,128)(2,1)}, bf16[72,48,128]{2,1,0:T(8,128)(2,1)S(1)}, u32[]{:S(2)}, u32[]{:S(2)}) collective-permute-start(bf16[72,48,128]{2,1,0:T(8,128)(2,1)} %get-tuple-element.33.refs_2_), channel_id=1, source_target_pairs={{6,4},{4,6},{14,12},{12,14},{7,5},{5,7},{15,13},{13,15},{22,20},{2... | collective-permute-start | bytes 2654216 | tf_op jit(solution)/shard_map/ppermute | solution.py:218
  110.1 22.7 %collective-permute-start.8 = (bf16[72,48,128]{2,1,0:T(8,128)(2,1)}, bf16[72,48,128]{2,1,0:T(8,128)(2,1)S(1)}, u32[]{:S(2)}, u32[]{:S(2)}) collective-permute-start(bf16[72,48,128]{2,1,0:T(8,128)(2,1)} %get-tuple-element.32), channel_id=1, source_target_pairs={{0,6},{6,0},{4,2},{2,4},{8,14},{14,8},{12,10},{10,12},{1,7},{7,1},... | collective-permute-start | bytes 2654216 | tf_op jit(solution)/shard_map/ppermute | solution.py:217
  110.2 31.8 %collective-permute-start.10 = (bf16[32,48,512]{2,1,0:T(8,128)(2,1)}, bf16[32,48,512]{2,1,0:T(8,128)(2,1)}, u32[]{:S(2)}, u32[]{:S(2)}) collective-permute-start(bf16[32,48,512]{2,1,0:T(8,128)(2,1)} %get-tuple-element.34), channel_id=1, source_target_pairs={{0,8},{6,14},{4,12},{2,10},{8,0},{14,6},{12,4},{10,2},{1,9},{7,15}... | collective-permute-start | bytes 4718600 | tf_op jit(solution)/shard_map/ppermute | solution.py:219
  112.5 29.5 %collective-permute-start.11 = (bf16[32,48,512]{2,1,0:T(8,128)(2,1)}, bf16[32,48,512]{2,1,0:T(8,128)(2,1)}, u32[]{:S(2)}, u32[]{:S(2)}) collective-permute-start(bf16[32,48,512]{2,1,0:T(8,128)(2,1)} %get-tuple-element.35), channel_id=1, source_target_pairs={{8,1},{14,7},{12,5},{10,3},{1,8},{7,14},{5,12},{3,10},{9,16},{15,2... | collective-permute-start | bytes 4718600 | tf_op jit(solution)/shard_map/ppermute | solution.py:220
  129.9 5.0 %copy-start.2 = (bf16[72,48,128]{2,1,0:T(8,128)(2,1)}, bf16[72,48,128]{2,1,0:T(8,128)(2,1)S(1)}, u32[]{:S(2)}) copy-start(bf16[72,48,128]{2,1,0:T(8,128)(2,1)S(1)} %collective-permute-done.9.refs_1_) | copy-start | bytes 2654212
  132.8 3.5 %copy-start.3 = (bf16[72,48,128]{2,1,0:T(8,128)(2,1)}, bf16[72,48,128]{2,1,0:T(8,128)(2,1)S(1)}, u32[]{:S(2)}) copy-start(bf16[72,48,128]{2,1,0:T(8,128)(2,1)S(1)} %collective-permute-done.8.refs_0_) | copy-start | bytes 2654212
  132.9 9.1 %collective-permute-start.13 = (bf16[32,48,128]{2,1,0:T(8,128)(2,1)S(1)}, bf16[32,48,128]{2,1,0:T(8,128)(2,1)S(1)}, u32[]{:S(2)}, u32[]{:S(2)}) collective-permute-start(bf16[32,48,128]{2,1,0:T(8,128)(2,1)S(1)} %pad_maximum_fusion.4), channel_id=1, source_target_pairs={{8,1},{14,7},{12,5},{10,3},{1,8},{7,14},{5,12},{3,10},{9,16},{15,2... | collective-permute-start | bytes 1179656 | tf_op jit(solution)/shard_map/ppermute | solution.py:230
  134.9 7.1 %collective-permute-start.12 = (bf16[32,48,128]{2,1,0:T(8,128)(2,1)S(1)}, bf16[32,48,128]{2,1,0:T(8,128)(2,1)S(1)}, u32[]{:S(2)}, u32[]{:S(2)}) collective-permute-start(bf16[32,48,128]{2,1,0:T(8,128)(2,1)S(1)} %pad_maximum_fusion.3), channel_id=1, source_target_pairs={{0,8},{6,14},{4,12},{2,10},{8,0},{14,6},{12,4},{10,2},{1,9},{7,15}... | collective-permute-start | bytes 1179656 | tf_op jit(solution)/shard_map/ppermute | solution.py:229
  142.0 0.8 copy-start.7
  142.0 0.9 copy-start.8
  154.5 23.7 %collective-permute-start.14 = (bf16[48,24,256]{2,1,0:T(8,128)(2,1)}, bf16[48,24,256]{2,1,0:T(8,128)(2,1)}, u32[]{:S(2)}, u32[]{:S(2)}) collective-permute-start(bf16[48,24,256]{2,1,0:T(8,128)(2,1)} %get-tuple-element.37), channel_id=1, source_target_pairs={{4,2},{2,3},{8,6},{14,0},{12,5},{10,4},{1,8},{7,9},{5,11},{3,13},{... | collective-permute-start | bytes 1769480 | tf_op jit(solution)/shard_map/ppermute | solution.py:564
  160.1 18.1 %collective-permute-start.15 = (bf16[48,24,256]{2,1,0:T(8,128)(2,1)}, bf16[48,24,256]{2,1,0:T(8,128)(2,1)S(1)}, u32[]{:S(2)}, u32[]{:S(2)}) collective-permute-start(bf16[48,24,256]{2,1,0:T(8,128)(2,1)} %get-tuple-element.38), channel_id=1, source_target_pairs={{0,6},{6,0},{4,5},{2,4},{12,2},{10,3},{1,15},{7,14},{9,8},{15,9},{... | collective-permute-start | bytes 1769480 | tf_op jit(solution)/shard_map/ppermute | solution.py:565
  178.2 0.8 copy-start
  179.0 13.2 %copy-start.9 = (bf16[48,48,256]{2,1,0:T(8,128)(2,1)S(1)}, bf16[48,48,256]{2,1,0:T(8,128)(2,1)}, u32[]{:S(2)}) copy-start(bf16[48,48,256]{2,1,0:T(8,128)(2,1)} %get-tuple-element.50) | copy-start | bytes 3538948
  179.0 28.7 %copy-start.1 = (bf16[48,24,256]{2,1,0:T(8,128)(2,1)S(1)}, bf16[48,24,256]{2,1,0:T(8,128)(2,1)}, u32[]{:S(2)}) copy-start(bf16[48,24,256]{2,1,0:T(8,128)(2,1)} %get-tuple-element.46) | copy-start | bytes 1769476
  179.1 23.8 %collective-permute-start.20 = (bf16[48,48,256]{2,1,0:T(8,128)(2,1)}, bf16[48,48,256]{2,1,0:T(8,128)(2,1)S(1)}, u32[]{:S(2)}, u32[]{:S(2)}) collective-permute-start(bf16[48,48,256]{2,1,0:T(8,128)(2,1)} %get-tuple-element.49), channel_id=1, source_target_pairs={{4,2},{2,3},{8,6},{14,0},{12,5},{10,4},{1,8},{7,9},{5,11},{3,13},{... | collective-permute-start | bytes 3538952 | tf_op jit(solution)/shard_map/ppermute | solution.py:568
  184.2 8.1 %collective-permute-start.18 = (bf16[48,128]{1,0:T(8,128)(2,1)}, bf16[48,128]{1,0:T(8,128)(2,1)S(1)}, u32[]{:S(2)}, u32[]{:S(2)}) collective-permute-start(bf16[48,128]{1,0:T(8,128)(2,1)} %get-tuple-element.47), channel_id=1, source_target_pairs={{0,1},{6,2},{4,3},{2,4},{1,9},{7,10},{5,11},{3,12},{16,17},{22,18}... | collective-permute-start | bytes 36872 | tf_op jit(solution)/shard_map/ppermute | solution.py:578
  186.5 8.0 %collective-permute-start.19 = (bf16[48,128]{1,0:T(8,128)(2,1)}, bf16[48,128]{1,0:T(8,128)(2,1)S(1)}, u32[]{:S(2)}, u32[]{:S(2)}) collective-permute-start(bf16[48,128]{1,0:T(8,128)(2,1)} %get-tuple-element.48), channel_id=1, source_target_pairs={{6,7},{4,6},{2,5},{7,15},{5,14},{3,13},{22,23},{20,22},{18,21},{23... | collective-permute-start | bytes 36872 | tf_op jit(solution)/shard_map/ppermute | solution.py:579
  189.6 14.7 %collective-permute-start.17 = (bf16[48,24,256]{2,1,0:T(8,128)(2,1)S(1)}, bf16[48,24,256]{2,1,0:T(8,128)(2,1)S(1)}, u32[]{:S(2)}, u32[]{:S(2)}) collective-permute-start(bf16[48,24,256]{2,1,0:T(8,128)(2,1)S(1)} %broadcast_select_fusion), channel_id=1, source_target_pairs={{6,7},{0,1},{8,0},{14,6},{5,13},{3,11},{11,10},{13,12},{22,23},{16... | collective-permute-start | bytes 1769480 | tf_op jit(solution)/shard_map/ppermute | solution.py:571
  190.9 16.8 %collective-permute-start.16 = (bf16[48,24,256]{2,1,0:T(8,128)(2,1)}, bf16[48,24,256]{2,1,0:T(8,128)(2,1)S(1)}, u32[]{:S(2)}, u32[]{:S(2)}) collective-permute-start(bf16[48,24,256]{2,1,0:T(8,128)(2,1)} %get-tuple-element.45), channel_id=1, source_target_pairs={{6,7},{0,1},{11,10},{13,12},{22,23},{16,17},{27,26},{29,28},{38,39... | collective-permute-start | bytes 1769480 | tf_op jit(solution)/shard_map/ppermute | solution.py:570
  192.2 29.6 %collective-permute-start.22 = (bf16[48,48,256]{2,1,0:T(8,128)(2,1)S(1)}, bf16[48,48,256]{2,1,0:T(8,128)(2,1)S(1)}, u32[]{:S(2)}, u32[]{:S(2)}) collective-permute-start(bf16[48,48,256]{2,1,0:T(8,128)(2,1)S(1)} %copy-done.9), channel_id=1, source_target_pairs={{0,7},{6,1},{4,5},{2,4},{8,0},{14,6},{12,2},{10,3},{1,15},{7,14},{... | collective-permute-start | bytes 3538952 | tf_op jit(solution)/shard_map/ppermute | solution.py:569
  202.9 30.1 %collective-permute-start.21 = (bf16[48,48,256]{2,1,0:T(8,128)(2,1)S(1)}, bf16[48,48,256]{2,1,0:T(8,128)(2,1)S(1)}, u32[]{:S(2)}, u32[]{:S(2)}) collective-permute-start(bf16[48,48,256]{2,1,0:T(8,128)(2,1)S(1)} %collective-permute-done.20), channel_id=1, source_target_pairs={{6,7},{0,1},{11,10},{13,12},{22,23},{16,17},{27,26},{29,28},{38,39... | collective-permute-start | bytes 3538952 | tf_op jit(solution)/shard_map/ppermute | solution.py:572
  208.0 25.0 %copy-start.4 = (bf16[48,48,256]{2,1,0:T(8,128)(2,1)S(1)}, bf16[48,48,256]{2,1,0:T(8,128)(2,1)}, u32[]{:S(2)}) copy-start(bf16[48,48,256]{2,1,0:T(8,128)(2,1)} %get-tuple-element.49) | copy-start | bytes 3538948

commit v5 on v4

--- a/solution.py
+++ b/solution.py
@@ -19,7 +19,7 @@
 CHUNK = 24
 PARTS = (((0, 24),), ((24, 48),))
 PREP = 8
-UNROLL = 8
+UNROLL = 24
 STACK = 8
 AXES = ("pos", "off")
 
@@ -218,13 +218,16 @@
     far = lax.ppermute(far, AXES, FAR)
     mate = lax.ppermute(mate, AXES, MATES)
     other = lax.ppermute(other, AXES, OTHERS)
-    ends = lambda first: jnp.concatenate(
-        [
-            lax.dynamic_slice_in_dim(near, first, CORNER),
-            jnp.where(at[FOLD] == 3, *[lax.dynamic_slice_in_dim(x, first, CORNER) for x in (beside, far)]),
-        ],
-        axis=0,
-    )
+    lane = lax.broadcasted_iota(jnp.int32, (1, 1, LANES), 2)
+
+    def ends(first):
+        rows = lambda x: lax.dynamic_slice_in_dim(x, first, CORNER)
+        packed = []
+        for x in (rows(near), jnp.where(at[FOLD] == 3, rows(beside), rows(far))):
+            turned = jnp.concatenate([x[CORNER // 2 :, :, 64:], x[CORNER // 2 :, :, :64]], axis=2)
+            packed.append(jnp.where((lane < 32) | (lane >= 96), x[: CORNER // 2], turned))
+        return jnp.concatenate(packed, axis=0)
+
     down = at[CORE] == 0
     corner_mate = lax.ppermute(ends(jnp.where(down, ROWS - CORNER, 0)), AXES, MATES)
     corner_other = lax.ppermute(ends(jnp.where(down, 0, ROWS - CORNER)), AXES, OTHERS)
@@ -249,10 +252,10 @@
     if final:
         hidden_ref, carried, refs = refs[0], refs[1 : 1 + extra], refs[1 + extra :]
         outs, scratch = refs[:4], refs[4:]
-        out_ref, own, mid, before, behind, plus_ref, minus_ref, sems = scratch
+        out_ref, own, mid, before, behind, plus_ref, minus_ref, packed_ref, sems = scratch
     else:
         outs, scratch = refs[:5], refs[5:]
-        out_ref, in_ref, back_ref, mid, before, behind, plus_ref, minus_ref, sems = scratch
+        out_ref, in_ref, back_ref, mid, before, behind, plus_ref, minus_ref, packed_ref, sems = scratch
 
     base, end = reach(runs)
     made = []
@@ -292,22 +295,12 @@
         for a, b, x in ((behind, before, far), (before, behind, far), (before, behind, beside))
     ]
     choices = [(CORE, rows), (SIDE, sides)]
-    if needs_corners(runs):
-        ends = []
-        for kind in range(4):
-            above, below = (corner_mate, corner_other) if kind % 2 else (corner_other, corner_mate)
-            a, b = (before, behind) if kind // 2 else (behind, before)
-            ends.append(
-                fetch(above, -CORNER, 0, a, -CORNER)
-                + fetch(above, -CORNER, 0, b, -2 * CORNER)
-                + fetch(below, ROWS, ROWS + CORNER, a, ROWS)
-                + fetch(below, ROWS, ROWS + CORNER, b, ROWS - CORNER)
-            )
-        choices.append((KIND, ends))
     always = []
     later = []
+    if needs_corners(runs):
+        always += [copy(corner_mate, packed_ref.at[0]), copy(corner_other, packed_ref.at[1])]
     if final:
-        always = fetch(hidden_ref, 0, ROWS, mid, 0)
+        always += fetch(hidden_ref, 0, ROWS, mid, 0)
         at = 0
         for first, count in runs:
             later.append((ORDER, own_cells(first, count, own, at)))
@@ -323,6 +316,25 @@
         c.wait()
     for choice in choices:
         each(choice, lambda c: c.wait())
+
+    def corners(kind):
+        above, below = (0, 1) if kind % 2 else (1, 0)
+        sides = (before, behind) if kind // 2 else (behind, before)
+
+        def case():
+            for which, low in ((above, -CORNER), (below, ROWS)):
+                if low < base or low + CORNER > end:
+                    continue
+                for i, side in enumerate(sides):
+                    for j in range(CORNER // 2):
+                        cells = packed_ref[which, i * CORNER // 2 + j]
+                        side[low - base + j] = cells
+                        side[low - base + CORNER // 2 + j] = pltpu.roll(cells, 64, axis=1)
+
+        return case
+
+    if needs_corners(runs):
+        choose(at_ref, KIND, [corners(kind) for kind in range(4)])
 
     d = d_ref[which]
     lo = d // 2
@@ -478,7 +490,7 @@
     in_specs = [SMEM] * 3 + [ANY] * 7 + [VMEM] * 2
     if needs_corners(runs):
         args += corners
-        in_specs += [ANY] * 2
+        in_specs += [HBM] * 2
     if final:
         args += [hidden, *carried]
         in_specs += [ANY] + [VMEM] * len(carried)
@@ -491,6 +503,7 @@
         out_shape=out_shape,
         scratch_shapes=scratch
         + [pltpu.VMEM((high - low, C, n), jnp.bfloat16) for n in (WIDE, LANES, LANES, WIDE, WIDE)]
+        + [pltpu.VMEM((2, CORNER, C, LANES), jnp.bfloat16)]
         + [pltpu.SemaphoreType.DMA((96,))],
         compiler_params=PARAMS,
         name="second" if final else "first",
@@ -504,8 +517,8 @@
 def behind(cells):
     return pl.pallas_call(
         behind_kernel,
-        in_specs=[ANY] * len(cells),
-        out_specs=[ANY] * len(cells),
+        in_specs=[HBM] * len(cells),
+        out_specs=[HBM] * len(cells),
         out_shape=[shape(*x.shape) for x in cells],
         input_output_aliases={i: i for i in range(len(cells))},
         compiler_params=PARAMS,
@@ -532,25 +545,15 @@
     pos, off = lax.axis_index("pos"), lax.axis_index("off")
     here = lambda pairs: functools.reduce(jnp.logical_or, [(pos % 2 == s) & (off == b) for s, b in pairs])
     stays, relayed = here(STAY), here(VIA)
-    kept = [(to, at_work) for to, at_work in late if (to // 8 % 2, to % 8) in STAY]
-    lends = functools.reduce(jnp.logical_or, [(pos == a // 8) & (off == a % 8) for _, a in kept])
-
-    def relay(pairs, turn):
-        leave, arrive = [], []
-        for to, at_work in pairs:
-            stored, block = to // 8, to % 8
-            if (stored % 2, block) in VIA:
-                via = device(stored // 2, *VIA[stored % 2, block])
-                leave.append((at_work, via))
-                arrive.append((via, to))
-            elif (stored % 2, block) not in STAY:
-                leave.append((at_work, to))
-            elif turn:
-                arrive.append((at_work, to))
-        return leave, arrive
-
-    leave, arrive = relay(early, 0)
-    leave_late, arrive_late = relay(late, 1)
+    leave, arrive = [], []
+    for to, at_work in early:
+        stored, block = to // 8, to % 8
+        if (stored % 2, block) in VIA:
+            via = device(stored // 2, *VIA[stored % 2, block])
+            leave.append((at_work, via))
+            arrive.append((via, to))
+        elif at_work != to:
+            leave.append((at_work, to))
 
     def second(rows, carried):
         return conv(
@@ -560,18 +563,18 @@
     def sorted_out(first, passed, ended):
         return jnp.where(stays, first, jnp.where(relayed, ended, passed))
 
+    straight = [(b, a) for a, b in late]
     first, late_first, *carried = second(PARTS[0], [])
     passed = lax.ppermute(first, AXES, leave)
-    through = lax.ppermute(late_first, AXES, leave_late)
+    direct = lax.ppermute(late_first, AXES, straight)
     more, late_more, *carried = second(PARTS[1], carried)
-    passed, through, more, late_more, edge, other = behind((passed, through, more, late_more, *carried))
+    passed, direct, more, late_more, edge, other = behind((passed, direct, more, late_more, *carried))
     passed_more = lax.ppermute(more, AXES, leave)
-    direct = lax.ppermute(late_more, AXES, [(b, a) for a, b in late])
+    direct_more = lax.ppermute(late_more, AXES, straight)
     ended = lax.ppermute(passed, AXES, arrive)
-    ended_late = lax.ppermute(jnp.where(lends, late_first, through), AXES, arrive_late)
     ended_more = lax.ppermute(passed_more, AXES, arrive)
     gots = [sorted_out(first, passed, ended), sorted_out(more, passed_more, ended_more)]
-    directs = [jnp.where(stays | relayed, ended_late, through), direct]
+    directs = [direct, direct_more]
 
     to_first = lambda core: [(place(s, f), home(s // 2, f + 1)) for s, f in CELLS if s % 2 == core]
     to_second = lambda core: [(place(s, f), home(s // 2, 8 - f)) for s, f in CELLS if s % 2 == core and f]

time: 241 us -> 236 us (0.979); the launches traced: 236 us -> 235 us
  starting transfers between devices: 58.8 us -> 55 us
    ppermute x1, waiting for transfers between devices: 8.37 us -> 25.1 us  [local(): passed_more = lax.ppermute(more, AXES, leave)]
    ppermute x3 -> x2, waiting for transfers between devices: 13.5 us -> 0.01 us  [the longest x1 0.01 us: local(): direct = lax.ppermute(late_first, AXES, straight)]
    ppermute x2, waiting for transfers between devices: 10.7 us -> 6.47 us  [exchange(): lax.ppermute(ends(jnp.where(down, 0, ROWS - CORNER)), AXES, OTHERS)]
    ppermute x3 -> x2, starting transfers between devices: 4.87 us -> 0.96 us  [the longest x1 0.96 us: local(): direct_more = lax.ppermute(late_more, AXES, straight)]
    ppermute x1, waiting for transfers between devices: 11.2 us -> 15 us  [local(): ended_more = lax.ppermute(passed_more, AXES, arrive)]
    ppermute x1, waiting for transfers between devices: 3.37 us -> 0.01 us  [local(): ended = lax.ppermute(passed, AXES, arrive)]
  transfers between devices with their start and end apart: 23 -> 22, of which waited for: 11 -> 11; matrix products, arithmetic and copies ran while one was open for 3% -> 4% of each run, Pallas kernels for 9% -> 9%
where the time goes in v5:
time: 236 us; the launch traced here: 235 us
  waiting for transfers between devices  104 us (44%)
  Pallas kernels  59.9 us (25%)
  starting transfers between devices  55 us (23%)
  other arithmetic  8.09 us (3%)
  local copies, waits for them, and re-layouts  7.24 us (3%)
    pallas_call x3, Pallas kernels, conv(): pl.pallas_call(functools.partial(conv_kernel, int(final), runs, len(carri...  47 us
    ppermute x2, waiting for transfers between devices, exchange(): far = lax.ppermute(far, AXES, FAR)  31.7 us
    ppermute x1, waiting for transfers between devices, local(): passed_more = lax.ppermute(more, AXES, leave)  25.1 us
    ppermute x2, waiting for transfers between devices, local(): lax.ppermute(enter(i, vector, row_limit, band_map), AXES, routes(i))  21.3 us
    ppermute x1, waiting for transfers between devices, local(): ended_more = lax.ppermute(passed_more, AXES, arrive)  15 us
    ppermute x2, starting transfers between devices, local(): lax.ppermute(enter(i, vector, row_limit, band_map), AXES, routes(i))  14.4 us
    pallas_call x2, Pallas kernels, enter(): pl.pallas_call(functools.partial(enter_kernel, turn), grid_spec=pltpu.Pre...  7.75 us
    ppermute x2, waiting for transfers between devices, exchange(): lax.ppermute(ends(jnp.where(down, 0, ROWS - CORNER)), AXES, OTHERS)  6.47 us
  transfers between devices with their start and end apart: 22, of which 11 were waited for; matrix products, arithmetic and copies ran while one was open for 4% of the time, Pallas kernels for 9%

profile of v5, /device:TPU:118, one launch (start us, length us, event | category | flops | bytes accessed | tf_op | source)
XLA Modules:
  0.0 235.0 jit_solution(2377820657882946270)
XLA Ops:
  0.0 0.6 stack.39.at_ref
  0.6 3.9 %enter.2 = bf16[72,48,256]{2,1,0:T(8,128)(2,1)} custom-call(s32[9]{0:T(128)} %stack.39.at_ref, s32[2304]{0:T(1024)} %limit_ref.9, bf16[48,144,256]{2,1,0:T(8,128)(2,1)} %x_ref.3), custom_call_target="tpu_custom_call" | custom-call | tf_op jit(solution)/shard_map/enter/pallas_call | solution.py:114
  4.5 2.1 collective-permute-start
  6.6 3.9 %enter.3 = bf16[72,48,256]{2,1,0:T(8,128)(2,1)} custom-call(s32[9]{0:T(128)} %stack.39.at_ref, s32[2304]{0:T(1024)} %limit_ref.9, bf16[48,144,256]{2,1,0:T(8,128)(2,1)} %x_ref.3), custom_call_target="tpu_custom_call" | custom-call | tf_op jit(solution)/shard_map/enter/pallas_call | solution.py:114
  10.5 12.3 %collective-permute-start.1 = (bf16[72,48,256]{2,1,0:T(8,128)(2,1)}, bf16[72,48,256]{2,1,0:T(8,128)(2,1)}, u32[]{:S(2)}, u32[]{:S(2)}) collective-permute-start(bf16[72,48,256]{2,1,0:T(8,128)(2,1)} %enter.3), channel_id=1, source_target_pairs={{7,0},{1,6},{5,4},{4,2},{0,8},{6,14},{2,12},{3,10},{15,1},{14,7},{... | collective-permute-start | bytes 5308424 | tf_op jit(solution)/shard_map/ppermute | solution.py:538
  22.8 0.1 copy.22
  22.9 0.7 copy.24.refs_1_.refs_5_
  23.6 0.7 copy.26.refs_3_.refs_6_
  24.3 0.1 copy.21
  24.4 0.7 copy.23.refs_0_.refs_5_
  25.2 0.7 copy.25.refs_2_.refs_6_
  25.9 4.1 %collective-permute-done.early_ref = bf16[72,48,256]{2,1,0:T(8,128)(2,1)} collective-permute-done((bf16[72,48,256]{2,1,0:T(8,128)(2,1)}, bf16[72,48,256]{2,1,0:T(8,128)(2,1)}, u32[]{:S(2)}, u32[]{:S(2)}) %collective-permute-start) | collective-permute-done | bytes 1769504 | tf_op jit(solution)/shard_map/ppermute | solution.py:538
  30.0 17.2 %collective-permute-done.1.late_ref = bf16[72,48,256]{2,1,0:T(8,128)(2,1)} collective-permute-done((bf16[72,48,256]{2,1,0:T(8,128)(2,1)}, bf16[72,48,256]{2,1,0:T(8,128)(2,1)}, u32[]{:S(2)}, u32[]{:S(2)}) %collective-permute-start.1) | collective-permute-done | bytes 1769504 | tf_op jit(solution)/shard_map/ppermute | solution.py:538
  47.2 5.1 %pack.1 = (bf16[72,48,128]{2,1,0:T(8,128)(2,1)}, bf16[72,48,128]{2,1,0:T(8,128)(2,1)}, bf16[32,48,512]{2,1,0:T(8,128)(2,1)}, bf16[32,48,512]{2,1,0:T(8,128)(2,1)}) custom-call(s32[9]{0:T(128)} %stack.39.at_ref, bf16[72,48,256]{2,1,0:T(8,128)(2,1)} %collective-permute-done.early_ref, bf16[72,48,256]{2,1,0:T(8,128)(2,1)} %collective-permute-done.1.late_ref, ...), custom_call_target="tpu_custom_call" | custom-call | tf_op jit(solution)/shard_map/pack/pallas_call | solution.py:193
  52.3 1.9 collective-permute-start.3
  54.2 0.5 collective-permute-start.2
  54.7 1.4 collective-permute-start.4
  56.1 3.9 %collective-permute-start.5 = (bf16[32,48,512]{2,1,0:T(8,128)(2,1)}, bf16[32,48,512]{2,1,0:T(8,128)(2,1)}, u32[]{:S(2)}, u32[]{:S(2)}) collective-permute-start(bf16[32,48,512]{2,1,0:T(8,128)(2,1)} %get-tuple-element.31), channel_id=1, source_target_pairs={{8,1},{14,7},{12,5},{10,3},{1,8},{7,14},{5,12},{3,10},{9,16},{15,2... | collective-permute-start | bytes 4718600 | tf_op jit(solution)/shard_map/ppermute | solution.py:220
  60.0 16.3 %collective-permute-done.3.refs_1_ = bf16[72,48,128]{2,1,0:T(8,128)(2,1)S(1)} collective-permute-done((bf16[72,48,128]{2,1,0:T(8,128)(2,1)}, bf16[72,48,128]{2,1,0:T(8,128)(2,1)S(1)}, u32[]{:S(2)}, u32[]{:S(2)}) %collective-permute-start.3) | collective-permute-done | bytes 884768 | tf_op jit(solution)/shard_map/ppermute | solution.py:218
  76.3 1.4 dynamic-slice_select_fusion.2
  77.7 0.1 constant_dynamic-slice_fusion.6
  77.9 0.1 fusion.6
  78.0 0.3 dynamic-slice_select_fusion.6
  78.3 0.4 copy-done.5
  78.7 1.9 collective-permute-start.7
  80.6 2.1 collective-permute-start.6
  82.7 2.9 %collective-permute-done.7.refs_8_ = bf16[16,48,128]{2,1,0:T(8,128)(2,1)S(1)} collective-permute-done((bf16[16,48,128]{2,1,0:T(8,128)(2,1)S(1)}, bf16[16,48,128]{2,1,0:T(8,128)(2,1)S(1)}, u32[]{:S(2)}, u32[]{:S(2)}) %collective-permute-start.7) | collective-permute-done | bytes 196640 | tf_op jit(solution)/shard_map/ppermute | solution.py:233
  85.7 0.6 copy-done.9
  86.4 19.2 %first.1 = (bf16[72,48,512]{2,1,0:T(8,128)(2,1)}, bf16[72,48,128]{2,1,0:T(8,128)(2,1)}, bf16[72,48,128]{2,1,0:T(8,128)(2,1)}, bf16[32,48,512]{2,1,0:T(8,128)(2,1)}, bf16[32,48,512]{2,1,0:T(8,128)(2,1)}) custom-call(s32[9]{0:T(128)} %stack.39.at_ref, s32[2]{0:T(128)} %d_ref.5, s32[2304]{0:T(1024)} %limit_ref.9, ...), custom_call_target="tpu_custom_call" | custom-call | tf_op jit(solution)/shard_map/first/pallas_call | solution.py:499
  105.6 3.0 %collective-permute-start.9 = (bf16[72,48,128]{2,1,0:T(8,128)(2,1)}, bf16[72,48,128]{2,1,0:T(8,128)(2,1)S(1)}, u32[]{:S(2)}, u32[]{:S(2)}) collective-permute-start(bf16[72,48,128]{2,1,0:T(8,128)(2,1)} %get-tuple-element.33.refs_2_), channel_id=1, source_target_pairs={{6,4},{4,6},{14,12},{12,14},{7,5},{5,7},{15,13},{13,15},{22,20},{2... | collective-permute-start | bytes 2654216 | tf_op jit(solution)/shard_map/ppermute | solution.py:218
  108.6 0.1 collective-permute-start.8
  108.7 2.3 collective-permute-start.10
  111.0 1.9 collective-permute-start.11
  112.9 15.4 %collective-permute-done.9.refs_1_ = bf16[72,48,128]{2,1,0:T(8,128)(2,1)S(1)} collective-permute-done((bf16[72,48,128]{2,1,0:T(8,128)(2,1)}, bf16[72,48,128]{2,1,0:T(8,128)(2,1)S(1)}, u32[]{:S(2)}, u32[]{:S(2)}) %collective-permute-start.9) | collective-permute-done | bytes 884768 | tf_op jit(solution)/shard_map/ppermute | solution.py:218
  128.3 1.4 dynamic-slice_select_fusion
  129.7 1.6 collective-permute-done.8.refs_0_
  131.3 0.1 constant_dynamic-slice_fusion
  131.4 0.1 fusion.4
  131.5 0.1 fusion.5
  131.6 0.3 dynamic-slice_select_fusion.4
  131.9 0.3 copy-done
  132.3 1.9 collective-permute-start.13
  134.2 1.5 collective-permute-start.12
  135.7 3.5 %collective-permute-done.13.refs_8_ = bf16[16,48,128]{2,1,0:T(8,128)(2,1)S(1)} collective-permute-done((bf16[16,48,128]{2,1,0:T(8,128)(2,1)S(1)}, bf16[16,48,128]{2,1,0:T(8,128)(2,1)S(1)}, u32[]{:S(2)}, u32[]{:S(2)}) %collective-permute-start.13) | collective-permute-done | bytes 196640 | tf_op jit(solution)/shard_map/ppermute | solution.py:233
  139.3 0.7 copy-done.7
  140.0 11.4 %second.2 = (bf16[48,24,256]{2,1,0:T(8,128)(2,1)}, bf16[48,24,256]{2,1,0:T(8,128)(2,1)}, bf16[48,128]{1,0:T(8,128)(2,1)}, bf16[48,128]{1,0:T(8,128)(2,1)}) custom-call(s32[9]{0:T(128)} %stack.39.at_ref, s32[2]{0:T(128)} %d_ref.5, s32[2304]{0:T(1024)} %limit_ref.9, bf16[72,48,256]{2,1,0:T(8,128)(2,1)} %collective-permute-done.early_ref, ...), custom_call_target="tpu_custom_call" | custom-call | tf_op jit(solution)/shard_map/second/pallas_call | solution.py:499
  151.4 5.6 %collective-permute-start.14 = (bf16[48,24,256]{2,1,0:T(8,128)(2,1)}, bf16[48,24,256]{2,1,0:T(8,128)(2,1)}, u32[]{:S(2)}, u32[]{:S(2)}) collective-permute-start(bf16[48,24,256]{2,1,0:T(8,128)(2,1)} %get-tuple-element.37), channel_id=1, source_target_pairs={{4,2},{2,3},{8,6},{14,0},{12,5},{10,4},{1,8},{7,9},{5,11},{3,13},{... | collective-permute-start | bytes 1769480 | tf_op jit(solution)/shard_map/ppermute | solution.py:568
  157.1 16.4 %second.3 = (bf16[48,48,256]{2,1,0:T(8,128)(2,1)}, bf16[48,48,256]{2,1,0:T(8,128)(2,1)}, bf16[48,128]{1,0:T(8,128)(2,1)}, bf16[48,128]{1,0:T(8,128)(2,1)}) custom-call(s32[9]{0:T(128)} %stack.39.at_ref, s32[2]{0:T(128)} %d_ref.5, s32[2304]{0:T(1024)} %limit_ref.9, bf16[72,48,256]{2,1,0:T(8,128)(2,1)} %collective-permute-done.early_ref, ...), custom_call_target="tpu_custom_call" | custom-call | tf_op jit(solution)/shard_map/second/pallas_call | solution.py:499
  173.4 1.9 collective-permute-done.14.refs_0_
  175.4 0.8 copy-done.1
  176.2 5.1 %collective-permute-start.19 = (bf16[48,48,256]{2,1,0:T(8,128)(2,1)}, bf16[48,48,256]{2,1,0:T(8,128)(2,1)S(1)}, u32[]{:S(2)}, u32[]{:S(2)}) collective-permute-start(bf16[48,48,256]{2,1,0:T(8,128)(2,1)} %get-tuple-element.49), channel_id=1, source_target_pairs={{4,2},{2,3},{8,6},{14,0},{12,5},{10,4},{1,8},{7,9},{5,11},{3,13},{... | collective-permute-start | bytes 3538952 | tf_op jit(solution)/shard_map/ppermute | solution.py:572
  181.3 1.9 collective-permute-start.17
  183.2 2.2 collective-permute-start.18
  185.4 1.3 collective-permute-start.16
  186.7 1.0 collective-permute-start.21
  187.7 1.3 collective-permute-done.18
  189.0 25.1 %collective-permute-done.19 = bf16[48,48,256]{2,1,0:T(8,128)(2,1)S(1)} collective-permute-done((bf16[48,48,256]{2,1,0:T(8,128)(2,1)}, bf16[48,48,256]{2,1,0:T(8,128)(2,1)S(1)}, u32[]{:S(2)}, u32[]{:S(2)}) %collective-permute-start.19) | collective-permute-done | bytes 1179680 | tf_op jit(solution)/shard_map/ppermute | solution.py:572
  214.1 1.3 collective-permute-start.20
  215.5 1.4 fusion.2
  216.9 0.2 fusion.3
  217.2 15.0 %collective-permute-done.20 = bf16[48,48,256]{2,1,0:T(8,128)(2,1)S(1)} collective-permute-done((bf16[48,48,256]{2,1,0:T(8,128)(2,1)S(1)}, bf16[48,48,256]{2,1,0:T(8,128)(2,1)S(1)}, u32[]{:S(2)}, u32[]{:S(2)}) %collective-permute-start.20) | collective-permute-done | bytes 1179680 | tf_op jit(solution)/shard_map/ppermute | solution.py:575
  232.1 0.5 fusion
  232.7 0.4 fusion.1
  233.1 1.9 pad_maximum_fusion
  (49 shorter events, 0.5 us)
Async XLA Ops:
  4.5 18.3 %copy-start.11 = (bf16[9,48,48]{2,1,0:T(8,128)(2,1)S(1)}, bf16[9,48,48]{2,1,0:T(8,128)(2,1)}, u32[]{:S(2)}) copy-start(bf16[9,48,48]{2,1,0:T(8,128)(2,1)} %param.12) | copy-start | bytes 124420
  4.5 19.1 %copy-start.13 = (f32[48]{0:T(128)S(1)}, f32[48]{0:T(128)}, u32[]{:S(2)}) copy-start(f32[48]{0:T(128)} %param.13) | copy-start | bytes 580
  4.5 19.8 %copy-start.12 = (bf16[9,48,48]{2,1,0:T(8,128)(2,1)S(1)}, bf16[9,48,48]{2,1,0:T(8,128)(2,1)}, u32[]{:S(2)}) copy-start(bf16[9,48,48]{2,1,0:T(8,128)(2,1)} %param.10) | copy-start | bytes 124420
  4.5 20.7 %copy-start.14 = (f32[48]{0:T(128)S(1)}, f32[48]{0:T(128)}, u32[]{:S(2)}) copy-start(f32[48]{0:T(128)} %param.11) | copy-start | bytes 580
  4.5 25.5 %collective-permute-start = (bf16[72,48,256]{2,1,0:T(8,128)(2,1)}, bf16[72,48,256]{2,1,0:T(8,128)(2,1)}, u32[]{:S(2)}, u32[]{:S(2)}) collective-permute-start(bf16[72,48,256]{2,1,0:T(8,128)(2,1)} %enter.2), channel_id=1, source_target_pairs={{0,0},{6,6},{2,4},{3,2},{7,8},{1,14},{5,12},{4,10},{8,1},{9,7},{10... | collective-permute-start | bytes 5308424 | tf_op jit(solution)/shard_map/ppermute | solution.py:538
  10.5 36.7 %collective-permute-start.1 = (bf16[72,48,256]{2,1,0:T(8,128)(2,1)}, bf16[72,48,256]{2,1,0:T(8,128)(2,1)}, u32[]{:S(2)}, u32[]{:S(2)}) collective-permute-start(bf16[72,48,256]{2,1,0:T(8,128)(2,1)} %enter.3), channel_id=1, source_target_pairs={{7,0},{1,6},{5,4},{4,2},{0,8},{6,14},{2,12},{3,10},{15,1},{14,7},{... | collective-permute-start | bytes 5308424 | tf_op jit(solution)/shard_map/ppermute | solution.py:538
  52.3 24.0 %collective-permute-start.3 = (bf16[72,48,128]{2,1,0:T(8,128)(2,1)}, bf16[72,48,128]{2,1,0:T(8,128)(2,1)S(1)}, u32[]{:S(2)}, u32[]{:S(2)}) collective-permute-start(bf16[72,48,128]{2,1,0:T(8,128)(2,1)} %get-tuple-element.29.refs_2_), channel_id=1, source_target_pairs={{6,4},{4,6},{14,12},{12,14},{7,5},{5,7},{15,13},{13,15},{22,20},{2... | collective-permute-start | bytes 2654216 | tf_op jit(solution)/shard_map/ppermute | solution.py:218
  54.2 23.5 %collective-permute-start.2 = (bf16[72,48,128]{2,1,0:T(8,128)(2,1)}, bf16[72,48,128]{2,1,0:T(8,128)(2,1)S(1)}, u32[]{:S(2)}, u32[]{:S(2)}) collective-permute-start(bf16[72,48,128]{2,1,0:T(8,128)(2,1)} %get-tuple-element.28), channel_id=1, source_target_pairs={{0,6},{6,0},{4,2},{2,4},{8,14},{14,8},{12,10},{10,12},{1,7},{7,1},... | collective-permute-start | bytes 2654216 | tf_op jit(solution)/shard_map/ppermute | solution.py:217
  54.7 31.0 %collective-permute-start.4 = (bf16[32,48,512]{2,1,0:T(8,128)(2,1)}, bf16[32,48,512]{2,1,0:T(8,128)(2,1)}, u32[]{:S(2)}, u32[]{:S(2)}) collective-permute-start(bf16[32,48,512]{2,1,0:T(8,128)(2,1)} %get-tuple-element.30), channel_id=1, source_target_pairs={{0,8},{6,14},{4,12},{2,10},{8,0},{14,6},{12,4},{10,2},{1,9},{7,15}... | collective-permute-start | bytes 4718600 | tf_op jit(solution)/shard_map/ppermute | solution.py:219
  56.1 29.6 %collective-permute-start.5 = (bf16[32,48,512]{2,1,0:T(8,128)(2,1)}, bf16[32,48,512]{2,1,0:T(8,128)(2,1)}, u32[]{:S(2)}, u32[]{:S(2)}) collective-permute-start(bf16[32,48,512]{2,1,0:T(8,128)(2,1)} %get-tuple-element.31), channel_id=1, source_target_pairs={{8,1},{14,7},{12,5},{10,3},{1,8},{7,14},{5,12},{3,10},{9,16},{15,2... | collective-permute-start | bytes 4718600 | tf_op jit(solution)/shard_map/ppermute | solution.py:220
  76.3 2.0 copy-start.6
  77.7 0.9 copy-start.5
  78.7 7.0 %collective-permute-start.7 = (bf16[16,48,128]{2,1,0:T(8,128)(2,1)S(1)}, bf16[16,48,128]{2,1,0:T(8,128)(2,1)S(1)}, u32[]{:S(2)}, u32[]{:S(2)}) collective-permute-start(bf16[16,48,128]{2,1,0:T(8,128)(2,1)S(1)} %pad_maximum_fusion.2), channel_id=1, source_target_pairs={{8,1},{14,7},{12,5},{10,3},{1,8},{7,14},{5,12},{3,10},{9,16},{15,2... | collective-permute-start | bytes 589832 | tf_op jit(solution)/shard_map/ppermute | solution.py:233
  80.6 5.0 %collective-permute-start.6 = (bf16[16,48,128]{2,1,0:T(8,128)(2,1)S(1)}, bf16[16,48,128]{2,1,0:T(8,128)(2,1)S(1)}, u32[]{:S(2)}, u32[]{:S(2)}) collective-permute-start(bf16[16,48,128]{2,1,0:T(8,128)(2,1)S(1)} %pad_maximum_fusion.1), channel_id=1, source_target_pairs={{0,8},{6,14},{4,12},{2,10},{8,0},{14,6},{12,4},{10,2},{1,9},{7,15}... | collective-permute-start | bytes 589832 | tf_op jit(solution)/shard_map/ppermute | solution.py:232
  85.7 0.7 copy-start.9
  85.7 0.7 copy-start.10
  105.6 22.7 %collective-permute-start.9 = (bf16[72,48,128]{2,1,0:T(8,128)(2,1)}, bf16[72,48,128]{2,1,0:T(8,128)(2,1)S(1)}, u32[]{:S(2)}, u32[]{:S(2)}) collective-permute-start(bf16[72,48,128]{2,1,0:T(8,128)(2,1)} %get-tuple-element.33.refs_2_), channel_id=1, source_target_pairs={{6,4},{4,6},{14,12},{12,14},{7,5},{5,7},{15,13},{13,15},{22,20},{2... | collective-permute-start | bytes 2654216 | tf_op jit(solution)/shard_map/ppermute | solution.py:218
  108.6 22.7 %collective-permute-start.8 = (bf16[72,48,128]{2,1,0:T(8,128)(2,1)}, bf16[72,48,128]{2,1,0:T(8,128)(2,1)S(1)}, u32[]{:S(2)}, u32[]{:S(2)}) collective-permute-start(bf16[72,48,128]{2,1,0:T(8,128)(2,1)} %get-tuple-element.32), channel_id=1, source_target_pairs={{0,6},{6,0},{4,2},{2,4},{8,14},{14,8},{12,10},{10,12},{1,7},{7,1},... | collective-permute-start | bytes 2654216 | tf_op jit(solution)/shard_map/ppermute | solution.py:217
  108.7 30.6 %collective-permute-start.10 = (bf16[32,48,512]{2,1,0:T(8,128)(2,1)}, bf16[32,48,512]{2,1,0:T(8,128)(2,1)}, u32[]{:S(2)}, u32[]{:S(2)}) collective-permute-start(bf16[32,48,512]{2,1,0:T(8,128)(2,1)} %get-tuple-element.34), channel_id=1, source_target_pairs={{0,8},{6,14},{4,12},{2,10},{8,0},{14,6},{12,4},{10,2},{1,9},{7,15}... | collective-permute-start | bytes 4718600 | tf_op jit(solution)/shard_map/ppermute | solution.py:219
  111.0 28.3 %collective-permute-start.11 = (bf16[32,48,512]{2,1,0:T(8,128)(2,1)}, bf16[32,48,512]{2,1,0:T(8,128)(2,1)}, u32[]{:S(2)}, u32[]{:S(2)}) collective-permute-start(bf16[32,48,512]{2,1,0:T(8,128)(2,1)} %get-tuple-element.35), channel_id=1, source_target_pairs={{8,1},{14,7},{12,5},{10,3},{1,8},{7,14},{5,12},{3,10},{9,16},{15,2... | collective-permute-start | bytes 4718600 | tf_op jit(solution)/shard_map/ppermute | solution.py:220
  128.3 3.6 %copy-start.3 = (bf16[72,48,128]{2,1,0:T(8,128)(2,1)}, bf16[72,48,128]{2,1,0:T(8,128)(2,1)S(1)}, u32[]{:S(2)}) copy-start(bf16[72,48,128]{2,1,0:T(8,128)(2,1)S(1)} %collective-permute-done.9.refs_1_) | copy-start | bytes 2654212
  131.3 1.0 copy-start
  132.3 7.0 %collective-permute-start.13 = (bf16[16,48,128]{2,1,0:T(8,128)(2,1)S(1)}, bf16[16,48,128]{2,1,0:T(8,128)(2,1)S(1)}, u32[]{:S(2)}, u32[]{:S(2)}) collective-permute-start(bf16[16,48,128]{2,1,0:T(8,128)(2,1)S(1)} %pad_maximum_fusion.4), channel_id=1, source_target_pairs={{8,1},{14,7},{12,5},{10,3},{1,8},{7,14},{5,12},{3,10},{9,16},{15,2... | collective-permute-start | bytes 589832 | tf_op jit(solution)/shard_map/ppermute | solution.py:233
  134.2 5.0 %collective-permute-start.12 = (bf16[16,48,128]{2,1,0:T(8,128)(2,1)S(1)}, bf16[16,48,128]{2,1,0:T(8,128)(2,1)S(1)}, u32[]{:S(2)}, u32[]{:S(2)}) collective-permute-start(bf16[16,48,128]{2,1,0:T(8,128)(2,1)S(1)} %pad_maximum_fusion.3), channel_id=1, source_target_pairs={{0,8},{6,14},{4,12},{2,10},{8,0},{14,6},{12,4},{10,2},{1,9},{7,15}... | collective-permute-start | bytes 589832 | tf_op jit(solution)/shard_map/ppermute | solution.py:232
  139.3 0.7 copy-start.7
  139.3 0.7 copy-start.8
  151.4 23.9 %collective-permute-start.14 = (bf16[48,24,256]{2,1,0:T(8,128)(2,1)}, bf16[48,24,256]{2,1,0:T(8,128)(2,1)}, u32[]{:S(2)}, u32[]{:S(2)}) collective-permute-start(bf16[48,24,256]{2,1,0:T(8,128)(2,1)} %get-tuple-element.37), channel_id=1, source_target_pairs={{4,2},{2,3},{8,6},{14,0},{12,5},{10,4},{1,8},{7,9},{5,11},{3,13},{... | collective-permute-start | bytes 1769480 | tf_op jit(solution)/shard_map/ppermute | solution.py:568
  157.0 18.3 %collective-permute-start.15 = (bf16[48,24,256]{2,1,0:T(8,128)(2,1)}, bf16[48,24,256]{2,1,0:T(8,128)(2,1)S(1)}, u32[]{:S(2)}, u32[]{:S(2)}) collective-permute-start(bf16[48,24,256]{2,1,0:T(8,128)(2,1)} %get-tuple-element.38), channel_id=1, source_target_pairs={{0,7},{6,1},{4,5},{2,4},{8,0},{14,6},{12,2},{10,3},{1,15},{7,14},{... | collective-permute-start | bytes 1769480 | tf_op jit(solution)/shard_map/ppermute | solution.py:569
  175.4 0.8 copy-start.1
  176.2 37.9 %collective-permute-start.19 = (bf16[48,48,256]{2,1,0:T(8,128)(2,1)}, bf16[48,48,256]{2,1,0:T(8,128)(2,1)S(1)}, u32[]{:S(2)}, u32[]{:S(2)}) collective-permute-start(bf16[48,48,256]{2,1,0:T(8,128)(2,1)} %get-tuple-element.49), channel_id=1, source_target_pairs={{4,2},{2,3},{8,6},{14,0},{12,5},{10,4},{1,8},{7,9},{5,11},{3,13},{... | collective-permute-start | bytes 3538952 | tf_op jit(solution)/shard_map/ppermute | solution.py:572
  181.3 6.4 %collective-permute-start.17 = (bf16[48,128]{1,0:T(8,128)(2,1)}, bf16[48,128]{1,0:T(8,128)(2,1)S(1)}, u32[]{:S(2)}, u32[]{:S(2)}) collective-permute-start(bf16[48,128]{1,0:T(8,128)(2,1)} %get-tuple-element.47), channel_id=1, source_target_pairs={{0,1},{6,2},{4,3},{2,4},{1,9},{7,10},{5,11},{3,12},{16,17},{22,18}... | collective-permute-start | bytes 36872 | tf_op jit(solution)/shard_map/ppermute | solution.py:581
  183.2 5.8 %collective-permute-start.18 = (bf16[48,128]{1,0:T(8,128)(2,1)}, bf16[48,128]{1,0:T(8,128)(2,1)S(1)}, u32[]{:S(2)}, u32[]{:S(2)}) collective-permute-start(bf16[48,128]{1,0:T(8,128)(2,1)} %get-tuple-element.48), channel_id=1, source_target_pairs={{6,7},{4,6},{2,5},{7,15},{5,14},{3,13},{22,23},{20,22},{18,21},{23... | collective-permute-start | bytes 36872 | tf_op jit(solution)/shard_map/ppermute | solution.py:582
  185.4 30.1 %collective-permute-start.16 = (bf16[48,24,256]{2,1,0:T(8,128)(2,1)}, bf16[48,24,256]{2,1,0:T(8,128)(2,1)S(1)}, u32[]{:S(2)}, u32[]{:S(2)}) collective-permute-start(bf16[48,24,256]{2,1,0:T(8,128)(2,1)} %get-tuple-element.45), channel_id=1, source_target_pairs={{6,7},{0,1},{11,10},{13,12},{22,23},{16,17},{27,26},{29,28},{38,39... | collective-permute-start | bytes 1769480 | tf_op jit(solution)/shard_map/ppermute | solution.py:574
  186.7 30.4 %collective-permute-start.21 = (bf16[48,48,256]{2,1,0:T(8,128)(2,1)}, bf16[48,48,256]{2,1,0:T(8,128)(2,1)S(1)}, u32[]{:S(2)}, u32[]{:S(2)}) collective-permute-start(bf16[48,48,256]{2,1,0:T(8,128)(2,1)} %get-tuple-element.50), channel_id=1, source_target_pairs={{0,7},{6,1},{4,5},{2,4},{8,0},{14,6},{12,2},{10,3},{1,15},{7,14},{... | collective-permute-start | bytes 3538952 | tf_op jit(solution)/shard_map/ppermute | solution.py:573
  214.1 18.1 %collective-permute-start.20 = (bf16[48,48,256]{2,1,0:T(8,128)(2,1)S(1)}, bf16[48,48,256]{2,1,0:T(8,128)(2,1)S(1)}, u32[]{:S(2)}, u32[]{:S(2)}) collective-permute-start(bf16[48,48,256]{2,1,0:T(8,128)(2,1)S(1)} %collective-permute-done.19), channel_id=1, source_target_pairs={{6,7},{0,1},{11,10},{13,12},{22,23},{16,17},{27,26},{29,28},{38,39... | collective-permute-start | bytes 3538952 | tf_op jit(solution)/shard_map/ppermute | solution.py:575
  215.5 1.4 copy-start.2
  216.9 15.2 %copy-start.4 = (bf16[48,48,256]{2,1,0:T(8,128)(2,1)S(1)}, bf16[48,48,256]{2,1,0:T(8,128)(2,1)}, u32[]{:S(2)}) copy-start(bf16[48,48,256]{2,1,0:T(8,128)(2,1)} %get-tuple-element.49) | copy-start | bytes 3538948

commit v6 on v5

--- a/solution.py
+++ b/solution.py
@@ -20,7 +20,7 @@
 PARTS = (((0, 24),), ((24, 48),))
 PREP = 8
 UNROLL = 24
-STACK = 8
+STACK = 12
 AXES = ("pos", "off")
 
 SMEM = pl.BlockSpec(memory_space=pltpu.SMEM)

time: 236 us -> 236 us (level)
  transfers between devices with their start and end apart: 22 -> 22, of which waited for: 11 -> 11; matrix products, arithmetic and copies ran while one was open for 4% -> 4% of each run, Pallas kernels for 9% -> 8%
where the time goes in v6:
time: 236 us; the launch traced here: 234 us
  waiting for transfers between devices  105 us (44%)
  Pallas kernels  58.6 us (25%)
  starting transfers between devices  55 us (23%)
  other arithmetic  8.09 us (3%)
  local copies, waits for them, and re-layouts  7.24 us (3%)
    pallas_call x3, Pallas kernels, conv(): pl.pallas_call(functools.partial(conv_kernel, int(final), runs, len(carri...  45.7 us
    ppermute x2, waiting for transfers between devices, exchange(): far = lax.ppermute(far, AXES, FAR)  31.7 us
    ppermute x1, waiting for transfers between devices, local(): passed_more = lax.ppermute(more, AXES, leave)  25.1 us
    ppermute x2, waiting for transfers between devices, local(): lax.ppermute(enter(i, vector, row_limit, band_map), AXES, routes(i))  21.3 us
    ppermute x1, waiting for transfers between devices, local(): ended_more = lax.ppermute(passed_more, AXES, arrive)  15 us
    ppermute x2, starting transfers between devices, local(): lax.ppermute(enter(i, vector, row_limit, band_map), AXES, routes(i))  14.4 us
    pallas_call x2, Pallas kernels, enter(): pl.pallas_call(functools.partial(enter_kernel, turn), grid_spec=pltpu.Pre...  7.75 us
    ppermute x2, waiting for transfers between devices, exchange(): lax.ppermute(ends(jnp.where(down, 0, ROWS - CORNER)), AXES, OTHERS)  6.47 us
  transfers between devices with their start and end apart: 22, of which 11 were waited for; matrix products, arithmetic and copies ran while one was open for 4% of the time, Pallas kernels for 8%

profile of v6, /device:TPU:118, one launch (start us, length us, event | category | flops | bytes accessed | tf_op | source)
XLA Modules:
  0.0 234.3 jit_solution(6140772843269572000)
XLA Ops:
  0.0 0.6 stack.39.at_ref
  0.6 3.9 %enter.2 = bf16[72,48,256]{2,1,0:T(8,128)(2,1)} custom-call(s32[9]{0:T(128)} %stack.39.at_ref, s32[2304]{0:T(1024)} %limit_ref.9, bf16[48,144,256]{2,1,0:T(8,128)(2,1)} %x_ref.3), custom_call_target="tpu_custom_call" | custom-call | tf_op jit(solution)/shard_map/enter/pallas_call | solution.py:114
  4.5 2.1 collective-permute-start
  6.6 3.9 %enter.3 = bf16[72,48,256]{2,1,0:T(8,128)(2,1)} custom-call(s32[9]{0:T(128)} %stack.39.at_ref, s32[2304]{0:T(1024)} %limit_ref.9, bf16[48,144,256]{2,1,0:T(8,128)(2,1)} %x_ref.3), custom_call_target="tpu_custom_call" | custom-call | tf_op jit(solution)/shard_map/enter/pallas_call | solution.py:114
  10.5 12.3 %collective-permute-start.1 = (bf16[72,48,256]{2,1,0:T(8,128)(2,1)}, bf16[72,48,256]{2,1,0:T(8,128)(2,1)}, u32[]{:S(2)}, u32[]{:S(2)}) collective-permute-start(bf16[72,48,256]{2,1,0:T(8,128)(2,1)} %enter.3), channel_id=1, source_target_pairs={{7,0},{1,6},{5,4},{4,2},{0,8},{6,14},{2,12},{3,10},{15,1},{14,7},{... | collective-permute-start | bytes 5308424 | tf_op jit(solution)/shard_map/ppermute | solution.py:538
  22.8 0.1 copy.22
  22.9 0.7 copy.24.refs_1_.refs_5_
  23.6 0.7 copy.26.refs_3_.refs_6_
  24.3 0.1 copy.21
  24.4 0.7 copy.23.refs_0_.refs_5_
  25.2 0.7 copy.25.refs_2_.refs_6_
  25.9 4.1 %collective-permute-done.early_ref = bf16[72,48,256]{2,1,0:T(8,128)(2,1)} collective-permute-done((bf16[72,48,256]{2,1,0:T(8,128)(2,1)}, bf16[72,48,256]{2,1,0:T(8,128)(2,1)}, u32[]{:S(2)}, u32[]{:S(2)}) %collective-permute-start) | collective-permute-done | bytes 1769504 | tf_op jit(solution)/shard_map/ppermute | solution.py:538
  30.0 17.2 %collective-permute-done.1.late_ref = bf16[72,48,256]{2,1,0:T(8,128)(2,1)} collective-permute-done((bf16[72,48,256]{2,1,0:T(8,128)(2,1)}, bf16[72,48,256]{2,1,0:T(8,128)(2,1)}, u32[]{:S(2)}, u32[]{:S(2)}) %collective-permute-start.1) | collective-permute-done | bytes 1769504 | tf_op jit(solution)/shard_map/ppermute | solution.py:538
  47.2 5.1 %pack.1 = (bf16[72,48,128]{2,1,0:T(8,128)(2,1)}, bf16[72,48,128]{2,1,0:T(8,128)(2,1)}, bf16[32,48,512]{2,1,0:T(8,128)(2,1)}, bf16[32,48,512]{2,1,0:T(8,128)(2,1)}) custom-call(s32[9]{0:T(128)} %stack.39.at_ref, bf16[72,48,256]{2,1,0:T(8,128)(2,1)} %collective-permute-done.early_ref, bf16[72,48,256]{2,1,0:T(8,128)(2,1)} %collective-permute-done.1.late_ref, ...), custom_call_target="tpu_custom_call" | custom-call | tf_op jit(solution)/shard_map/pack/pallas_call | solution.py:193
  52.3 1.9 collective-permute-start.3
  54.2 0.5 collective-permute-start.2
  54.7 1.4 collective-permute-start.4
  56.1 3.9 %collective-permute-start.5 = (bf16[32,48,512]{2,1,0:T(8,128)(2,1)}, bf16[32,48,512]{2,1,0:T(8,128)(2,1)}, u32[]{:S(2)}, u32[]{:S(2)}) collective-permute-start(bf16[32,48,512]{2,1,0:T(8,128)(2,1)} %get-tuple-element.31), channel_id=1, source_target_pairs={{8,1},{14,7},{12,5},{10,3},{1,8},{7,14},{5,12},{3,10},{9,16},{15,2... | collective-permute-start | bytes 4718600 | tf_op jit(solution)/shard_map/ppermute | solution.py:220
  60.0 16.3 %collective-permute-done.3.refs_1_ = bf16[72,48,128]{2,1,0:T(8,128)(2,1)S(1)} collective-permute-done((bf16[72,48,128]{2,1,0:T(8,128)(2,1)}, bf16[72,48,128]{2,1,0:T(8,128)(2,1)S(1)}, u32[]{:S(2)}, u32[]{:S(2)}) %collective-permute-start.3) | collective-permute-done | bytes 884768 | tf_op jit(solution)/shard_map/ppermute | solution.py:218
  76.3 1.4 dynamic-slice_select_fusion.2
  77.7 0.1 constant_dynamic-slice_fusion.6
  77.9 0.1 fusion.6
  78.0 0.3 dynamic-slice_select_fusion.6
  78.3 0.4 copy-done.5
  78.7 1.9 collective-permute-start.7
  80.6 2.1 collective-permute-start.6
  82.7 2.9 %collective-permute-done.7.refs_8_ = bf16[16,48,128]{2,1,0:T(8,128)(2,1)S(1)} collective-permute-done((bf16[16,48,128]{2,1,0:T(8,128)(2,1)S(1)}, bf16[16,48,128]{2,1,0:T(8,128)(2,1)S(1)}, u32[]{:S(2)}, u32[]{:S(2)}) %collective-permute-start.7) | collective-permute-done | bytes 196640 | tf_op jit(solution)/shard_map/ppermute | solution.py:233
  85.7 0.6 copy-done.9
  86.4 19.2 %first.1 = (bf16[72,48,512]{2,1,0:T(8,128)(2,1)}, bf16[72,48,128]{2,1,0:T(8,128)(2,1)}, bf16[72,48,128]{2,1,0:T(8,128)(2,1)}, bf16[32,48,512]{2,1,0:T(8,128)(2,1)}, bf16[32,48,512]{2,1,0:T(8,128)(2,1)}) custom-call(s32[9]{0:T(128)} %stack.39.at_ref, s32[2]{0:T(128)} %d_ref.5, s32[2304]{0:T(1024)} %limit_ref.9, ...), custom_call_target="tpu_custom_call" | custom-call | tf_op jit(solution)/shard_map/first/pallas_call | solution.py:499
  105.6 3.0 %collective-permute-start.9 = (bf16[72,48,128]{2,1,0:T(8,128)(2,1)}, bf16[72,48,128]{2,1,0:T(8,128)(2,1)S(1)}, u32[]{:S(2)}, u32[]{:S(2)}) collective-permute-start(bf16[72,48,128]{2,1,0:T(8,128)(2,1)} %get-tuple-element.33.refs_2_), channel_id=1, source_target_pairs={{6,4},{4,6},{14,12},{12,14},{7,5},{5,7},{15,13},{13,15},{22,20},{2... | collective-permute-start | bytes 2654216 | tf_op jit(solution)/shard_map/ppermute | solution.py:218
  108.6 0.1 collective-permute-start.8
  108.7 2.3 collective-permute-start.10
  111.0 1.9 collective-permute-start.11
  112.9 15.4 %collective-permute-done.9.refs_1_ = bf16[72,48,128]{2,1,0:T(8,128)(2,1)S(1)} collective-permute-done((bf16[72,48,128]{2,1,0:T(8,128)(2,1)}, bf16[72,48,128]{2,1,0:T(8,128)(2,1)S(1)}, u32[]{:S(2)}, u32[]{:S(2)}) %collective-permute-start.9) | collective-permute-done | bytes 884768 | tf_op jit(solution)/shard_map/ppermute | solution.py:218
  128.3 1.4 dynamic-slice_select_fusion
  129.7 1.6 collective-permute-done.8.refs_0_
  131.3 0.1 constant_dynamic-slice_fusion
  131.4 0.1 fusion.4
  131.5 0.1 fusion.5
  131.6 0.3 dynamic-slice_select_fusion.4
  131.9 0.3 copy-done
  132.3 1.9 collective-permute-start.13
  134.2 1.5 collective-permute-start.12
  135.7 3.5 %collective-permute-done.13.refs_8_ = bf16[16,48,128]{2,1,0:T(8,128)(2,1)S(1)} collective-permute-done((bf16[16,48,128]{2,1,0:T(8,128)(2,1)S(1)}, bf16[16,48,128]{2,1,0:T(8,128)(2,1)S(1)}, u32[]{:S(2)}, u32[]{:S(2)}) %collective-permute-start.13) | collective-permute-done | bytes 196640 | tf_op jit(solution)/shard_map/ppermute | solution.py:233
  139.3 0.7 copy-done.7
  140.0 10.7 %second.2 = (bf16[48,24,256]{2,1,0:T(8,128)(2,1)}, bf16[48,24,256]{2,1,0:T(8,128)(2,1)}, bf16[48,128]{1,0:T(8,128)(2,1)}, bf16[48,128]{1,0:T(8,128)(2,1)}) custom-call(s32[9]{0:T(128)} %stack.39.at_ref, s32[2]{0:T(128)} %d_ref.5, s32[2304]{0:T(1024)} %limit_ref.9, bf16[72,48,256]{2,1,0:T(8,128)(2,1)} %collective-permute-done.early_ref, ...), custom_call_target="tpu_custom_call" | custom-call | tf_op jit(solution)/shard_map/second/pallas_call | solution.py:499
  150.7 5.6 %collective-permute-start.14 = (bf16[48,24,256]{2,1,0:T(8,128)(2,1)}, bf16[48,24,256]{2,1,0:T(8,128)(2,1)}, u32[]{:S(2)}, u32[]{:S(2)}) collective-permute-start(bf16[48,24,256]{2,1,0:T(8,128)(2,1)} %get-tuple-element.37), channel_id=1, source_target_pairs={{4,2},{2,3},{8,6},{14,0},{12,5},{10,4},{1,8},{7,9},{5,11},{3,13},{... | collective-permute-start | bytes 1769480 | tf_op jit(solution)/shard_map/ppermute | solution.py:568
  156.3 15.8 %second.3 = (bf16[48,48,256]{2,1,0:T(8,128)(2,1)}, bf16[48,48,256]{2,1,0:T(8,128)(2,1)}, bf16[48,128]{1,0:T(8,128)(2,1)}, bf16[48,128]{1,0:T(8,128)(2,1)}) custom-call(s32[9]{0:T(128)} %stack.39.at_ref, s32[2]{0:T(128)} %d_ref.5, s32[2304]{0:T(1024)} %limit_ref.9, bf16[72,48,256]{2,1,0:T(8,128)(2,1)} %collective-permute-done.early_ref, ...), custom_call_target="tpu_custom_call" | custom-call | tf_op jit(solution)/shard_map/second/pallas_call | solution.py:499
  172.1 2.5 %collective-permute-done.14.refs_0_ = bf16[48,24,256]{2,1,0:T(8,128)(2,1)} collective-permute-done((bf16[48,24,256]{2,1,0:T(8,128)(2,1)}, bf16[48,24,256]{2,1,0:T(8,128)(2,1)}, u32[]{:S(2)}, u32[]{:S(2)}) %collective-permute-start.14) | collective-permute-done | bytes 589856 | tf_op jit(solution)/shard_map/ppermute | solution.py:568
  174.6 0.8 copy-done.1
  175.4 5.1 %collective-permute-start.19 = (bf16[48,48,256]{2,1,0:T(8,128)(2,1)}, bf16[48,48,256]{2,1,0:T(8,128)(2,1)S(1)}, u32[]{:S(2)}, u32[]{:S(2)}) collective-permute-start(bf16[48,48,256]{2,1,0:T(8,128)(2,1)} %get-tuple-element.49), channel_id=1, source_target_pairs={{4,2},{2,3},{8,6},{14,0},{12,5},{10,4},{1,8},{7,9},{5,11},{3,13},{... | collective-permute-start | bytes 3538952 | tf_op jit(solution)/shard_map/ppermute | solution.py:572
  180.5 1.9 collective-permute-start.17
  182.4 2.2 collective-permute-start.18
  184.7 1.3 collective-permute-start.16
  186.0 1.0 collective-permute-start.21
  186.9 1.3 collective-permute-done.18
  188.2 25.1 %collective-permute-done.19 = bf16[48,48,256]{2,1,0:T(8,128)(2,1)S(1)} collective-permute-done((bf16[48,48,256]{2,1,0:T(8,128)(2,1)}, bf16[48,48,256]{2,1,0:T(8,128)(2,1)S(1)}, u32[]{:S(2)}, u32[]{:S(2)}) %collective-permute-start.19) | collective-permute-done | bytes 1179680 | tf_op jit(solution)/shard_map/ppermute | solution.py:572
  213.3 1.3 collective-permute-start.20
  214.8 1.4 fusion.2
  216.2 0.2 fusion.3
  216.4 15.0 %collective-permute-done.20 = bf16[48,48,256]{2,1,0:T(8,128)(2,1)S(1)} collective-permute-done((bf16[48,48,256]{2,1,0:T(8,128)(2,1)S(1)}, bf16[48,48,256]{2,1,0:T(8,128)(2,1)S(1)}, u32[]{:S(2)}, u32[]{:S(2)}) %collective-permute-start.20) | collective-permute-done | bytes 1179680 | tf_op jit(solution)/shard_map/ppermute | solution.py:575
  231.4 0.5 fusion
  231.9 0.4 fusion.1
  232.3 1.9 pad_maximum_fusion
  (49 shorter events, 0.5 us)
Async XLA Ops:
  4.5 18.3 %copy-start.11 = (bf16[9,48,48]{2,1,0:T(8,128)(2,1)S(1)}, bf16[9,48,48]{2,1,0:T(8,128)(2,1)}, u32[]{:S(2)}) copy-start(bf16[9,48,48]{2,1,0:T(8,128)(2,1)} %param.12) | copy-start | bytes 124420
  4.5 19.1 %copy-start.13 = (f32[48]{0:T(128)S(1)}, f32[48]{0:T(128)}, u32[]{:S(2)}) copy-start(f32[48]{0:T(128)} %param.13) | copy-start | bytes 580
  4.5 19.8 %copy-start.12 = (bf16[9,48,48]{2,1,0:T(8,128)(2,1)S(1)}, bf16[9,48,48]{2,1,0:T(8,128)(2,1)}, u32[]{:S(2)}) copy-start(bf16[9,48,48]{2,1,0:T(8,128)(2,1)} %param.10) | copy-start | bytes 124420
  4.5 20.7 %copy-start.14 = (f32[48]{0:T(128)S(1)}, f32[48]{0:T(128)}, u32[]{:S(2)}) copy-start(f32[48]{0:T(128)} %param.11) | copy-start | bytes 580
  4.5 25.5 %collective-permute-start = (bf16[72,48,256]{2,1,0:T(8,128)(2,1)}, bf16[72,48,256]{2,1,0:T(8,128)(2,1)}, u32[]{:S(2)}, u32[]{:S(2)}) collective-permute-start(bf16[72,48,256]{2,1,0:T(8,128)(2,1)} %enter.2), channel_id=1, source_target_pairs={{0,0},{6,6},{2,4},{3,2},{7,8},{1,14},{5,12},{4,10},{8,1},{9,7},{10... | collective-permute-start | bytes 5308424 | tf_op jit(solution)/shard_map/ppermute | solution.py:538
  10.5 36.7 %collective-permute-start.1 = (bf16[72,48,256]{2,1,0:T(8,128)(2,1)}, bf16[72,48,256]{2,1,0:T(8,128)(2,1)}, u32[]{:S(2)}, u32[]{:S(2)}) collective-permute-start(bf16[72,48,256]{2,1,0:T(8,128)(2,1)} %enter.3), channel_id=1, source_target_pairs={{7,0},{1,6},{5,4},{4,2},{0,8},{6,14},{2,12},{3,10},{15,1},{14,7},{... | collective-permute-start | bytes 5308424 | tf_op jit(solution)/shard_map/ppermute | solution.py:538
  52.3 24.0 %collective-permute-start.3 = (bf16[72,48,128]{2,1,0:T(8,128)(2,1)}, bf16[72,48,128]{2,1,0:T(8,128)(2,1)S(1)}, u32[]{:S(2)}, u32[]{:S(2)}) collective-permute-start(bf16[72,48,128]{2,1,0:T(8,128)(2,1)} %get-tuple-element.29.refs_2_), channel_id=1, source_target_pairs={{6,4},{4,6},{14,12},{12,14},{7,5},{5,7},{15,13},{13,15},{22,20},{2... | collective-permute-start | bytes 2654216 | tf_op jit(solution)/shard_map/ppermute | solution.py:218
  54.2 23.5 %collective-permute-start.2 = (bf16[72,48,128]{2,1,0:T(8,128)(2,1)}, bf16[72,48,128]{2,1,0:T(8,128)(2,1)S(1)}, u32[]{:S(2)}, u32[]{:S(2)}) collective-permute-start(bf16[72,48,128]{2,1,0:T(8,128)(2,1)} %get-tuple-element.28), channel_id=1, source_target_pairs={{0,6},{6,0},{4,2},{2,4},{8,14},{14,8},{12,10},{10,12},{1,7},{7,1},... | collective-permute-start | bytes 2654216 | tf_op jit(solution)/shard_map/ppermute | solution.py:217
  54.7 31.0 %collective-permute-start.4 = (bf16[32,48,512]{2,1,0:T(8,128)(2,1)}, bf16[32,48,512]{2,1,0:T(8,128)(2,1)}, u32[]{:S(2)}, u32[]{:S(2)}) collective-permute-start(bf16[32,48,512]{2,1,0:T(8,128)(2,1)} %get-tuple-element.30), channel_id=1, source_target_pairs={{0,8},{6,14},{4,12},{2,10},{8,0},{14,6},{12,4},{10,2},{1,9},{7,15}... | collective-permute-start | bytes 4718600 | tf_op jit(solution)/shard_map/ppermute | solution.py:219
  56.1 29.6 %collective-permute-start.5 = (bf16[32,48,512]{2,1,0:T(8,128)(2,1)}, bf16[32,48,512]{2,1,0:T(8,128)(2,1)}, u32[]{:S(2)}, u32[]{:S(2)}) collective-permute-start(bf16[32,48,512]{2,1,0:T(8,128)(2,1)} %get-tuple-element.31), channel_id=1, source_target_pairs={{8,1},{14,7},{12,5},{10,3},{1,8},{7,14},{5,12},{3,10},{9,16},{15,2... | collective-permute-start | bytes 4718600 | tf_op jit(solution)/shard_map/ppermute | solution.py:220
  76.3 2.0 copy-start.6
  77.7 0.9 copy-start.5
  78.7 7.0 %collective-permute-start.7 = (bf16[16,48,128]{2,1,0:T(8,128)(2,1)S(1)}, bf16[16,48,128]{2,1,0:T(8,128)(2,1)S(1)}, u32[]{:S(2)}, u32[]{:S(2)}) collective-permute-start(bf16[16,48,128]{2,1,0:T(8,128)(2,1)S(1)} %pad_maximum_fusion.2), channel_id=1, source_target_pairs={{8,1},{14,7},{12,5},{10,3},{1,8},{7,14},{5,12},{3,10},{9,16},{15,2... | collective-permute-start | bytes 589832 | tf_op jit(solution)/shard_map/ppermute | solution.py:233
  80.6 5.0 %collective-permute-start.6 = (bf16[16,48,128]{2,1,0:T(8,128)(2,1)S(1)}, bf16[16,48,128]{2,1,0:T(8,128)(2,1)S(1)}, u32[]{:S(2)}, u32[]{:S(2)}) collective-permute-start(bf16[16,48,128]{2,1,0:T(8,128)(2,1)S(1)} %pad_maximum_fusion.1), channel_id=1, source_target_pairs={{0,8},{6,14},{4,12},{2,10},{8,0},{14,6},{12,4},{10,2},{1,9},{7,15}... | collective-permute-start | bytes 589832 | tf_op jit(solution)/shard_map/ppermute | solution.py:232
  85.7 0.7 copy-start.9
  85.7 0.7 copy-start.10
  105.6 22.7 %collective-permute-start.9 = (bf16[72,48,128]{2,1,0:T(8,128)(2,1)}, bf16[72,48,128]{2,1,0:T(8,128)(2,1)S(1)}, u32[]{:S(2)}, u32[]{:S(2)}) collective-permute-start(bf16[72,48,128]{2,1,0:T(8,128)(2,1)} %get-tuple-element.33.refs_2_), channel_id=1, source_target_pairs={{6,4},{4,6},{14,12},{12,14},{7,5},{5,7},{15,13},{13,15},{22,20},{2... | collective-permute-start | bytes 2654216 | tf_op jit(solution)/shard_map/ppermute | solution.py:218
  108.6 22.7 %collective-permute-start.8 = (bf16[72,48,128]{2,1,0:T(8,128)(2,1)}, bf16[72,48,128]{2,1,0:T(8,128)(2,1)S(1)}, u32[]{:S(2)}, u32[]{:S(2)}) collective-permute-start(bf16[72,48,128]{2,1,0:T(8,128)(2,1)} %get-tuple-element.32), channel_id=1, source_target_pairs={{0,6},{6,0},{4,2},{2,4},{8,14},{14,8},{12,10},{10,12},{1,7},{7,1},... | collective-permute-start | bytes 2654216 | tf_op jit(solution)/shard_map/ppermute | solution.py:217
  108.7 30.6 %collective-permute-start.10 = (bf16[32,48,512]{2,1,0:T(8,128)(2,1)}, bf16[32,48,512]{2,1,0:T(8,128)(2,1)}, u32[]{:S(2)}, u32[]{:S(2)}) collective-permute-start(bf16[32,48,512]{2,1,0:T(8,128)(2,1)} %get-tuple-element.34), channel_id=1, source_target_pairs={{0,8},{6,14},{4,12},{2,10},{8,0},{14,6},{12,4},{10,2},{1,9},{7,15}... | collective-permute-start | bytes 4718600 | tf_op jit(solution)/shard_map/ppermute | solution.py:219
  111.0 28.3 %collective-permute-start.11 = (bf16[32,48,512]{2,1,0:T(8,128)(2,1)}, bf16[32,48,512]{2,1,0:T(8,128)(2,1)}, u32[]{:S(2)}, u32[]{:S(2)}) collective-permute-start(bf16[32,48,512]{2,1,0:T(8,128)(2,1)} %get-tuple-element.35), channel_id=1, source_target_pairs={{8,1},{14,7},{12,5},{10,3},{1,8},{7,14},{5,12},{3,10},{9,16},{15,2... | collective-permute-start | bytes 4718600 | tf_op jit(solution)/shard_map/ppermute | solution.py:220
  128.3 3.6 %copy-start.3 = (bf16[72,48,128]{2,1,0:T(8,128)(2,1)}, bf16[72,48,128]{2,1,0:T(8,128)(2,1)S(1)}, u32[]{:S(2)}) copy-start(bf16[72,48,128]{2,1,0:T(8,128)(2,1)S(1)} %collective-permute-done.9.refs_1_) | copy-start | bytes 2654212
  131.3 1.0 copy-start
  132.3 7.0 %collective-permute-start.13 = (bf16[16,48,128]{2,1,0:T(8,128)(2,1)S(1)}, bf16[16,48,128]{2,1,0:T(8,128)(2,1)S(1)}, u32[]{:S(2)}, u32[]{:S(2)}) collective-permute-start(bf16[16,48,128]{2,1,0:T(8,128)(2,1)S(1)} %pad_maximum_fusion.4), channel_id=1, source_target_pairs={{8,1},{14,7},{12,5},{10,3},{1,8},{7,14},{5,12},{3,10},{9,16},{15,2... | collective-permute-start | bytes 589832 | tf_op jit(solution)/shard_map/ppermute | solution.py:233
  134.2 5.0 %collective-permute-start.12 = (bf16[16,48,128]{2,1,0:T(8,128)(2,1)S(1)}, bf16[16,48,128]{2,1,0:T(8,128)(2,1)S(1)}, u32[]{:S(2)}, u32[]{:S(2)}) collective-permute-start(bf16[16,48,128]{2,1,0:T(8,128)(2,1)S(1)} %pad_maximum_fusion.3), channel_id=1, source_target_pairs={{0,8},{6,14},{4,12},{2,10},{8,0},{14,6},{12,4},{10,2},{1,9},{7,15}... | collective-permute-start | bytes 589832 | tf_op jit(solution)/shard_map/ppermute | solution.py:232
  139.3 0.7 copy-start.7
  139.3 0.7 copy-start.8
  150.7 23.9 %collective-permute-start.14 = (bf16[48,24,256]{2,1,0:T(8,128)(2,1)}, bf16[48,24,256]{2,1,0:T(8,128)(2,1)}, u32[]{:S(2)}, u32[]{:S(2)}) collective-permute-start(bf16[48,24,256]{2,1,0:T(8,128)(2,1)} %get-tuple-element.37), channel_id=1, source_target_pairs={{4,2},{2,3},{8,6},{14,0},{12,5},{10,4},{1,8},{7,9},{5,11},{3,13},{... | collective-permute-start | bytes 1769480 | tf_op jit(solution)/shard_map/ppermute | solution.py:568
  156.3 18.3 %collective-permute-start.15 = (bf16[48,24,256]{2,1,0:T(8,128)(2,1)}, bf16[48,24,256]{2,1,0:T(8,128)(2,1)S(1)}, u32[]{:S(2)}, u32[]{:S(2)}) collective-permute-start(bf16[48,24,256]{2,1,0:T(8,128)(2,1)} %get-tuple-element.38), channel_id=1, source_target_pairs={{0,7},{6,1},{4,5},{2,4},{8,0},{14,6},{12,2},{10,3},{1,15},{7,14},{... | collective-permute-start | bytes 1769480 | tf_op jit(solution)/shard_map/ppermute | solution.py:569
  174.6 0.8 copy-start.1
  175.4 37.9 %collective-permute-start.19 = (bf16[48,48,256]{2,1,0:T(8,128)(2,1)}, bf16[48,48,256]{2,1,0:T(8,128)(2,1)S(1)}, u32[]{:S(2)}, u32[]{:S(2)}) collective-permute-start(bf16[48,48,256]{2,1,0:T(8,128)(2,1)} %get-tuple-element.49), channel_id=1, source_target_pairs={{4,2},{2,3},{8,6},{14,0},{12,5},{10,4},{1,8},{7,9},{5,11},{3,13},{... | collective-permute-start | bytes 3538952 | tf_op jit(solution)/shard_map/ppermute | solution.py:572
  180.5 6.4 %collective-permute-start.17 = (bf16[48,128]{1,0:T(8,128)(2,1)}, bf16[48,128]{1,0:T(8,128)(2,1)S(1)}, u32[]{:S(2)}, u32[]{:S(2)}) collective-permute-start(bf16[48,128]{1,0:T(8,128)(2,1)} %get-tuple-element.47), channel_id=1, source_target_pairs={{0,1},{6,2},{4,3},{2,4},{1,9},{7,10},{5,11},{3,12},{16,17},{22,18}... | collective-permute-start | bytes 36872 | tf_op jit(solution)/shard_map/ppermute | solution.py:581
  182.4 5.8 %collective-permute-start.18 = (bf16[48,128]{1,0:T(8,128)(2,1)}, bf16[48,128]{1,0:T(8,128)(2,1)S(1)}, u32[]{:S(2)}, u32[]{:S(2)}) collective-permute-start(bf16[48,128]{1,0:T(8,128)(2,1)} %get-tuple-element.48), channel_id=1, source_target_pairs={{6,7},{4,6},{2,5},{7,15},{5,14},{3,13},{22,23},{20,22},{18,21},{23... | collective-permute-start | bytes 36872 | tf_op jit(solution)/shard_map/ppermute | solution.py:582
  184.7 30.1 %collective-permute-start.16 = (bf16[48,24,256]{2,1,0:T(8,128)(2,1)}, bf16[48,24,256]{2,1,0:T(8,128)(2,1)S(1)}, u32[]{:S(2)}, u32[]{:S(2)}) collective-permute-start(bf16[48,24,256]{2,1,0:T(8,128)(2,1)} %get-tuple-element.45), channel_id=1, source_target_pairs={{6,7},{0,1},{11,10},{13,12},{22,23},{16,17},{27,26},{29,28},{38,39... | collective-permute-start | bytes 1769480 | tf_op jit(solution)/shard_map/ppermute | solution.py:574
  186.0 30.4 %collective-permute-start.21 = (bf16[48,48,256]{2,1,0:T(8,128)(2,1)}, bf16[48,48,256]{2,1,0:T(8,128)(2,1)S(1)}, u32[]{:S(2)}, u32[]{:S(2)}) collective-permute-start(bf16[48,48,256]{2,1,0:T(8,128)(2,1)} %get-tuple-element.50), channel_id=1, source_target_pairs={{0,7},{6,1},{4,5},{2,4},{8,0},{14,6},{12,2},{10,3},{1,15},{7,14},{... | collective-permute-start | bytes 3538952 | tf_op jit(solution)/shard_map/ppermute | solution.py:573
  213.3 18.1 %collective-permute-start.20 = (bf16[48,48,256]{2,1,0:T(8,128)(2,1)S(1)}, bf16[48,48,256]{2,1,0:T(8,128)(2,1)S(1)}, u32[]{:S(2)}, u32[]{:S(2)}) collective-permute-start(bf16[48,48,256]{2,1,0:T(8,128)(2,1)S(1)} %collective-permute-done.19), channel_id=1, source_target_pairs={{6,7},{0,1},{11,10},{13,12},{22,23},{16,17},{27,26},{29,28},{38,39... | collective-permute-start | bytes 3538952 | tf_op jit(solution)/shard_map/ppermute | solution.py:575
  214.8 1.4 copy-start.2
  216.2 15.2 %copy-start.4 = (bf16[48,48,256]{2,1,0:T(8,128)(2,1)S(1)}, bf16[48,48,256]{2,1,0:T(8,128)(2,1)}, u32[]{:S(2)}) copy-start(bf16[48,48,256]{2,1,0:T(8,128)(2,1)} %get-tuple-element.49) | copy-start | bytes 3538948
